TPU v7x, 512 devices: a whole 4x4x16 slice. The times are simulated.
512 devices in a mesh: grp: 16 (over z), brick: 32 (over y, x, core).
Axes of the slice: x: 4, y: 4, z: 16, core: 2. Of those that a mesh axis runs over, the one named last changes fastest.
Arguments:
- probes: bfloat16 [65536, 256], P('brick'), may hold values from -6 to 6
- weights: bfloat16 [16, 256, 3, 256, 256], P('grp', 'brick'), may hold values from -0.21875 to 0.21875
- columns: int32 [16, 256, 3], P('grp', 'brick'), may hold values from 0 to 23, as said below
Outputs:
- basis: float32 [65536, 256], P('brick')
- triangle: float32 [256, 256], replicated
Inputs may be any that keep to these rules, and one draw needn't show every extreme that they name: `columns`: for data block r the three ids are: 8 + r % 8, one id below 8, and one id of at least 16.
All inputs are finite; a program needn't handle non-finite values.
Results may differ from a plain program's by a relative error of at most 0.0029.
Values may be sent and summed in bfloat16 or wider, within the bound.
No kernel may reach another device: no remote copies, remote signals or barrier semaphores. Data moves between devices by JAX's collectives and lax.ppermute only.
A program may use at most 64 MiB of HBM per device.

v0:
```python
import math

import jax
import jax.numpy as jnp
from jax import lax
from jax.sharding import PartitionSpec as P


def padded(block, sides, width):
    for axis, dim in sides:
        count = lax.axis_size(axis)
        forward = [(i, i + 1) for i in range(count - 1)]
        backward = [(target, source) for source, target in forward]
        low = lax.ppermute(
            lax.slice_in_dim(block, block.shape[dim] - width, None, axis=dim), axis, forward
        )
        high = lax.ppermute(lax.slice_in_dim(block, 0, width, axis=dim), axis, backward)
        block = jnp.concatenate([low, block, high], axis=dim)
    return block


def shifted(value, axis, steps):
    count = lax.axis_size(axis)
    leading, last = (max(0, -steps), min(count, count - steps))
    return lax.ppermute(value, axis, [(source, source + steps) for source in range(leading, last)])


def factorize(image, gram):
    lower = jnp.linalg.cholesky(gram)
    basis = jax.scipy.linalg.solve_triangular(lower, image.T, lower=True).T
    return (basis, lower)


def body(probes, weights, columns):
    rows_dev, width = probes.shape
    w_local = weights[0]
    c_local = columns[0]
    nblocks = w_local.shape[0]
    slots = w_local.shape[1]
    bsize = w_local.shape[2]
    extended = padded(probes, (("brick", 0),), rows_dev)
    extended = extended.reshape(3 * nblocks, bsize, width)
    picked = extended[c_local]
    data = jnp.einsum("rjac,rjck->rak", w_local, picked, preferred_element_type=jnp.float32).astype(
        jnp.bfloat16
    )
    contrib = jnp.einsum("rjac,rak->rjck", w_local, data, preferred_element_type=jnp.float32)
    onehot = (
        c_local.reshape(-1)[None, :] == jnp.arange(3 * nblocks, dtype=jnp.int32)[:, None]
    ).astype(jnp.float32)
    spread = jnp.einsum(
        "sx,xck->sck",
        onehot,
        contrib.reshape(nblocks * slots, bsize, width),
        precision=lax.Precision.HIGHEST,
    )
    from_above = shifted(spread[:nblocks].astype(jnp.bfloat16), "brick", -1).astype(jnp.float32)
    from_below = shifted(spread[2 * nblocks :].astype(jnp.bfloat16), "brick", 1).astype(jnp.float32)
    own_term = (spread[nblocks : 2 * nblocks] + from_above + from_below).reshape(rows_dev, width)
    factor = math.sqrt(rows_dev * lax.axis_size("brick"))
    total = lax.psum(own_term, "grp")
    image = probes.astype(jnp.float32) + total
    gram = lax.psum(jnp.dot(image.T, image, precision=lax.Precision.HIGHEST), "brick")
    basis, lower = factorize(image, gram)
    return (basis * factor, lower.T / factor)


def solution(mesh):
    in_specs = (P("brick", None), P("grp", "brick", None, None, None), P("grp", "brick", None))
    out_specs = (P("brick", None), P())
    return jax.shard_map(body, mesh=mesh, in_specs=in_specs, out_specs=out_specs, check_vma=False)
```

profile of v0, /device:TPU:1, one launch (start us, length us, event | category | flops | bytes accessed | tf_op | source)
XLA Modules:
  0.0 449.6 jit_solution(16962969252317994072)
XLA Ops:
  7.2 4.8 %collective-permute-start = (bf16[2048,256]{1,0:T(8,128)(2,1)}, bf16[2048,256]{1,0:T(8,128)(2,1)}, u32[]{:S(2)}, u32[]{:S(2)}) collective-permute-start(bf16[2048,256]{1,0:T(8,128)(2,1)} %param.3), channel_id=1, source_target_pairs={{0,1},{1,2},{2,3},{3,4},{4,5},{5,6},{6,7},{7,8},{8,9},{9,10},{10,1... | collective-permute-start | bytes 3145736 | tf_op jit(solution)/shard_map/ppermute | solution.py:14
  12.0 6.5 %collective-permute-start.1 = (bf16[2048,256]{1,0:T(8,128)(2,1)}, bf16[2048,256]{1,0:T(8,128)(2,1)}, u32[]{:S(2)}, u32[]{:S(2)}) collective-permute-start(bf16[2048,256]{1,0:T(8,128)(2,1)} %param.3), channel_id=1, source_target_pairs={{1,0},{2,1},{3,2},{4,3},{5,4},{6,5},{7,6},{8,7},{9,8},{10,9},{11,1... | collective-permute-start | bytes 3145736 | tf_op jit(solution)/shard_map/ppermute | solution.py:17
  18.6 0.8 copy.12
  19.3 0.7 compare_select_fusion
  20.0 0.1 copy.13
  20.1 0.1 reshape.85
  20.2 0.1 eq.15
  20.2 3.8 collective-permute-done
  24.0 4.4 collective-permute-done.1
  28.4 3.2 pad_maximum_fusion
  31.6 4.4 gather_fusion
  36.0 6.4 %fusion = f32[8,256,3,256]{3,1,2,0:T(8,128)} fusion(bf16[1,8,3,256,256]{4,3,2,1,0:T(8,128)(2,1)S(1)} %copy-done, bf16[8,3,256,256]{3,2,1,0:T(8,128)(2,1)} %bitcast.80), kind=kOutput, calls=%fused_computation.4 | convolution fusion | flops 1611137024 | bytes 12582912 | tf_op jit(solution)/shard_map/rjac,rak->rjck/dot_general | solution.py:47
  42.4 6.7 %copy.14 = f32[24,256,256]{2,0,1:T(8,128)} copy(f32[24,256,256]{1,2,0:T(8,128)} %bitcast.78) | data formatting | bytes 12582912 | tf_op jit(solution)/shard_map/reshape | solution.py:54
  49.1 5.4 %fusion.30 = (bf16[24,256,256]{2,0,1:T(8,128)(2,1)S(1)}, f32[24,256,256]{2,0,1:T(8,128)S(1)}) fusion(f32[24,256,256]{2,0,1:T(8,128)} %copy.14, s32[24]{0:T(128)S(1)} %eq.15), kind=kOutput, calls=%fused_computation.52 | convolution fusion | flops 454558272 | bytes 15728736 | tf_op jit(solution)/shard_map/sx,xck->sck/dot_general | solution.py:51
  54.5 0.1 fusion.29
  54.6 1.9 collective-permute-start.2
  56.5 3.6 collective-permute-start.3
  60.2 10.5 %collective-permute-done.2 = bf16[8,256,256]{2,0,1:T(8,128)(2,1)S(1)} collective-permute-done((bf16[8,256,256]{2,0,1:T(8,128)(2,1)S(1)}, bf16[8,256,256]{2,0,1:T(8,128)(2,1)S(1)}, u32[]{:S(2)}, u32[]{:S(2)}) %collective-permute-start.2) | collective-permute-done | bytes 1048608 | tf_op jit(solution)/shard_map/ppermute | solution.py:25
  70.7 1.2 collective-permute-done.3
  71.9 0.3 fusion.4
  72.3 2.0 copy.15
  74.2 0.2 all-reduce.6.cloned.1.call-start
  74.5 144.4 %all-reduce.4.cloned.1.call-done = f32[2048,256]{1,0:T(8,128)} async-done(((f32[2048,256]{1,0:T(8,128)}), f32[2048,256]{1,0:T(8,128)}) %all-reduce.4.cloned.1.call-update) | async-done | bytes 2097168 | tf_op jit(solution)/shard_map/psum | solution.py:61
  218.9 7.1 %fusion.9 = f32[256,256]{0,1:T(8,128)} fusion(f32[2048,256]{1,0:T(8,128)} %all-reduce.4.cloned.1.call-done, bf16[2048,256]{1,0:T(8,128)(2,1)} %param.3), kind=kOutput, calls=%fused_computation.16 | convolution fusion | flops 1611661312 | bytes 3407872 | tf_op jit(solution)/shard_map/dot_general | solution.py:63
  226.1 3.4 fusion.8
  229.5 133.7 %all-reduce.6.cloned.1.call-done = f32[256,256]{0,1:T(8,128)} async-done(((f32[256,256]{0,1:T(8,128)}), f32[256,256]{0,1:T(8,128)}) %all-reduce.6.cloned.1.call-update) | async-done | bytes 262160 | tf_op jit(solution)/shard_map/psum | solution.py:63
  363.2 1.1 copy.17
  364.3 1.0 fusion.17
  365.3 0.7 copy-done.3
  366.0 11.7 %cholesky.50 = f32[128,128]{1,0:T(8,128)S(1)} custom-call(f32[128,128]{1,0:T(8,128)S(1)} %cholesky.118), custom_call_target="Cholesky" | custom-call | tf_op jit(solution)/shard_map/jit(cholesky)/cholesky | solution.py:29
  377.7 9.8 %custom-call.15 = f32[1,128,128]{1,2,0:T(8,128)S(1)} custom-call(f32[1,128,128]{2,1,0:T(8,128)S(1)} %get-tuple-element.31), custom_call_target="InvertDiagBlocksLowerTriangular" | custom-call | tf_op jit(solution)/shard_map/jit(cholesky)/cholesky | solution.py:29
  387.5 1.0 constant_dynamic-update-slice_fusion.1
  388.6 1.1 convolution_subtract_fusion.1
  389.7 11.9 %cholesky.105 = f32[128,128]{1,0:T(8,128)S(1)} custom-call(f32[128,128]{1,0:T(8,128)S(1)} %convolution_subtract_fusion.1), custom_call_target="Cholesky" | custom-call | tf_op jit(solution)/shard_map/jit(cholesky)/cholesky | solution.py:29
  401.7 0.7 compare_reduce_fusion
  403.7 1.7 multiply_bitcast_fusion
  405.4 5.1 %while.1 = (s32[]{:T(128)}, f32[256,256]{1,0:T(8,128)S(1)}, s32[2,2]{1,0:T(2,128)S(1)}, f32[2,128,128]{2,1,0:T(8,128)}, s32[]{:T(128)}) while((s32[]{:T(128)}, f32[256,256]{1,0:T(8,128)S(1)}, s32[2,2]{1,0:T(2,128)S(1)}, f32[2,128,128]{2,1,0:T(8,128)}, s32[]{:T(128)}) %tuple.32), condition=%wide.while_cond, body=%wide.while_body.sunk | while | flops 2 | bytes 132705 | solution.py:30
  405.4 0.6 fusion.38
  406.0 2.0 bitcast_dynamic-update-slice_fusion.2
  408.0 0.6 fusion.38
  408.6 2.0 bitcast_dynamic-update-slice_fusion.2
  410.6 20.5 %custom-call.16 = f32[2,128,128]{1,2,0:T(8,128)S(1)} custom-call(f32[2,128,128]{2,1,0:T(8,128)} %get-tuple-element.9), custom_call_target="InvertDiagBlocksLowerTriangular" | custom-call | tf_op jit(solution)/shard_map/jit(_solve_triangular)/triangular_solve | solution.py:30
  431.0 2.3 fusion.15
  433.3 3.0 convolution_subtract_fusion
  436.4 1.1 fusion.20
  437.5 1.5 fusion.5
  439.0 2.9 copy.18
  441.9 0.8 copy.19
  (20 shorter events, 0.3 us)
Async XLA Ops:
  7.2 28.9 %copy-start = (bf16[1,8,3,256,256]{4,3,2,1,0:T(8,128)(2,1)S(1)}, bf16[1,8,3,256,256]{4,3,2,1,0:T(8,128)(2,1)}, u32[]{:S(2)}) copy-start(bf16[1,8,3,256,256]{4,3,2,1,0:T(8,128)(2,1)} %param.4) | copy-start | bytes 9437188
  7.2 211.8 %all-reduce.4.cloned.1.call-start = ((), (), s32[]{:S(2)}) async-start(), calls=%async_computation | async-start | bytes 4194304 | tf_op jit(solution)/shard_map/psum | solution.py:61
  7.2 16.8 %collective-permute-start = (bf16[2048,256]{1,0:T(8,128)(2,1)}, bf16[2048,256]{1,0:T(8,128)(2,1)}, u32[]{:S(2)}, u32[]{:S(2)}) collective-permute-start(bf16[2048,256]{1,0:T(8,128)(2,1)} %param.3), channel_id=1, source_target_pairs={{0,1},{1,2},{2,3},{3,4},{4,5},{5,6},{6,7},{7,8},{8,9},{9,10},{10,1... | collective-permute-start | bytes 3145736 | tf_op jit(solution)/shard_map/ppermute | solution.py:14
  12.0 16.4 %collective-permute-start.1 = (bf16[2048,256]{1,0:T(8,128)(2,1)}, bf16[2048,256]{1,0:T(8,128)(2,1)}, u32[]{:S(2)}, u32[]{:S(2)}) collective-permute-start(bf16[2048,256]{1,0:T(8,128)(2,1)} %param.3), channel_id=1, source_target_pairs={{1,0},{2,1},{3,2},{4,3},{5,4},{6,5},{7,6},{8,7},{9,8},{10,9},{11,1... | collective-permute-start | bytes 3145736 | tf_op jit(solution)/shard_map/ppermute | solution.py:17
  54.6 16.1 %collective-permute-start.2 = (bf16[8,256,256]{2,0,1:T(8,128)(2,1)S(1)}, bf16[8,256,256]{2,0,1:T(8,128)(2,1)S(1)}, u32[]{:S(2)}, u32[]{:S(2)}) collective-permute-start(bf16[8,256,256]{2,0,1:T(8,128)(2,1)S(1)} %get-tuple-element.24), channel_id=1, source_target_pairs={{1,0},{2,1},{3,2},{4,3},{5,4},{6,5},{7,6},{8,7},{9,8},{10,9},{11,1... | collective-permute-start | bytes 3145736 | tf_op jit(solution)/shard_map/ppermute | solution.py:25
  56.5 15.4 %collective-permute-start.3 = (bf16[8,256,256]{2,0,1:T(8,128)(2,1)S(1)}, bf16[8,256,256]{2,0,1:T(8,128)(2,1)S(1)}, u32[]{:S(2)}, u32[]{:S(2)}) collective-permute-start(bf16[8,256,256]{2,0,1:T(8,128)(2,1)S(1)} %get-tuple-element.25), channel_id=1, source_target_pairs={{0,1},{1,2},{2,3},{3,4},{4,5},{5,6},{6,7},{7,8},{8,9},{9,10},{10,1... | collective-permute-start | bytes 3145736 | tf_op jit(solution)/shard_map/ppermute | solution.py:25
  74.2 288.9 %all-reduce.6.cloned.1.call-start = ((), (), s32[]{:S(2)}) async-start(), calls=%async_computation.1 | async-start | bytes 524288 | tf_op jit(solution)/shard_map/psum | solution.py:63
  365.2 0.7 copy-start.3
  401.7 2.0 copy-start.1
  439.0 2.9 copy-start.2
Sparse Core Ops, SparseCore 0:
  74.4 144.5 all-reduce.3
  226.2 136.9 all-reduce.5
where the time goes:
time: 450 us
  waiting for transfers between devices  298 us (66%)
  other arithmetic  66.5 us (15%)
  matrix products  27.5 us (6%)
  local copies, waits for them, and re-layouts  25 us (6%)
  starting transfers between devices  17.1 us (4%)
  between operations  15.5 us (3%)
    psum x1, waiting for transfers between devices, body(): total = lax.psum(own_term, 'grp')  144 us
    psum x1, waiting for transfers between devices, body(): lax.psum(jnp.dot(image.T, image, precision=lax.Precision.HIGHEST), 'brick')  134 us
    another operation x6, other arithmetic, factorize(): lower = jnp.linalg.cholesky(gram)  34.2 us
    another operation x2, other arithmetic, factorize(): basis = jax.scipy.linalg.solve_triangular(lower, image.T, lower=True).T  20.5 us
    ppermute x2, waiting for transfers between devices, shifted(): lax.ppermute(value, axis, [(source, source + steps) for source in range(l...  11.7 us
  transfers between devices with their start and end apart: 6, of which 6 were waited for; matrix products, arithmetic and copies ran while one was open for 1% of the time, Pallas kernels for 0%

commit v1 on v0

v1 whole, which is shorter than its diff:
```python
import functools
import math

import jax
import jax.numpy as jnp
from jax import lax
from jax.experimental import pallas as pl
from jax.experimental.pallas import tpu as pltpu
from jax.sharding import Mesh
from jax.sharding import PartitionSpec as P

F32 = jnp.float32
BF16 = jnp.bfloat16
PANEL = 64
MIB = 1024 * 1024
DEPTH = ("zh", "zp")


def exact_dot(a, b, dims):
    return lax.dot_general(
        a, b, (dims, ((), ())), precision=lax.Precision.HIGHEST, preferred_element_type=F32
    )


def split_dot(a, b, dims):
    a_high, b_high = a.astype(BF16), b.astype(BF16)
    a_low = (a - a_high.astype(F32)).astype(BF16)
    b_low = (b - b_high.astype(F32)).astype(BF16)
    dot = functools.partial(
        lax.dot_general, dimension_numbers=(dims, ((), ())), preferred_element_type=F32
    )
    return dot(a_high, b_high) + (dot(a_high, b_low) + dot(a_low, b_high))


def operator_kernel(cols, w_ref, low_ref, own_ref, high_ref, o_own, o_below, o_above, s_below, s_above):
    r = pl.program_id(0)
    half = own_ref.shape[0]

    @pl.when(r == 0)
    def _():
        s_below[...] = jnp.zeros_like(s_below)
        s_above[...] = jnp.zeros_like(s_above)

    ids = [cols[3 * r + j] for j in range(3)]
    at_low = jnp.where(ids[0] < half, 0, jnp.where(ids[1] < half, 1, 2))
    at_high = jnp.where(ids[0] >= 2 * half, 0, jnp.where(ids[1] >= 2 * half, 1, 2))
    at_own = 3 - at_low - at_high
    c_low = cols[3 * r + at_low]
    c_high = cols[3 * r + at_high] - 2 * half
    w_low, w_own, w_high = w_ref[0, at_low], w_ref[0, at_own], w_ref[0, at_high]
    data = (
        jnp.dot(w_low, low_ref[c_low], preferred_element_type=F32)
        + jnp.dot(w_own, own_ref[r], preferred_element_type=F32)
        + jnp.dot(w_high, high_ref[c_high], preferred_element_type=F32)
    ).astype(BF16)
    back = functools.partial(
        lax.dot_general, dimension_numbers=(((0,), (0,)), ((), ())), preferred_element_type=F32
    )
    o_own[0] = back(w_own, data)
    s_below[c_low] += back(w_low, data)
    s_above[c_high] += back(w_high, data)

    @pl.when(r == pl.num_programs(0) - 1)
    def _():
        o_below[...] = s_below[...].astype(BF16)
        o_above[...] = s_above[...].astype(BF16)


def apply_operator(cols, weights, low, own, high):
    blocks, slots, bs, _ = weights.shape
    width = own.shape[-1]
    whole = pl.BlockSpec((blocks, bs, width), lambda r, c: (0, 0, 0))
    shape = (blocks, bs, width)
    return pl.pallas_call(
        operator_kernel,
        grid_spec=pltpu.PrefetchScalarGridSpec(
            num_scalar_prefetch=1,
            grid=(blocks,),
            in_specs=[
                pl.BlockSpec((1, slots, bs, bs), lambda r, c: (r, 0, 0, 0)),
                whole,
                whole,
                whole,
            ],
            out_specs=[pl.BlockSpec((1, bs, width), lambda r, c: (r, 0, 0)), whole, whole],
            scratch_shapes=[pltpu.VMEM(shape, F32), pltpu.VMEM(shape, F32)],
        ),
        out_shape=(
            jax.ShapeDtypeStruct(shape, F32),
            jax.ShapeDtypeStruct(shape, BF16),
            jax.ShapeDtypeStruct(shape, BF16),
        ),
        compiler_params=pltpu.CompilerParams(vmem_limit_bytes=40 * MIB),
        name="normal_operator",
    )(cols, weights, low, own, high)


def halves_kernel(odd, *refs):
    ins, outs = refs[:12], refs[12:]
    for k in range(4):
        own, above, below = ins[3 * k : 3 * k + 3]
        total = own[0] + above[0].astype(F32) + below[0].astype(F32)
        outs[k][...] = total.astype(outs[k].dtype)


def split_halves(odd, own, above, below):
    rows, width = own.shape
    part, step = rows // 4, rows // 16
    arrays = [x.reshape(4, part, width) for x in (own, above, below)]
    places = (
        lambda s, o: (o[0], s, 0),
        lambda s, o: (1 - o[0], s, 0),
        lambda s, o: (2 + o[0], s, 0),
        lambda s, o: (3 - o[0], s, 0),
    )
    in_specs = [pl.BlockSpec((1, step, width), place) for place in places for _ in range(3)]
    out = pl.BlockSpec((step, width), lambda s, o: (s, 0))
    kept, sent = (jax.ShapeDtypeStruct((part, width), t) for t in (F32, BF16))
    return pl.pallas_call(
        halves_kernel,
        grid_spec=pltpu.PrefetchScalarGridSpec(
            num_scalar_prefetch=1, grid=(part // step,), in_specs=in_specs, out_specs=[out] * 4
        ),
        out_shape=(kept, sent, kept, sent),
        name="split_halves",
    )(odd, *(arrays * 4))


def pairs_kernel(ka, ra, kb, rb, out):
    n = ka.shape[0]
    out[:n] = (ka[...] + ra[...].astype(F32)).astype(BF16)
    out[n:] = (kb[...] + rb[...].astype(F32)).astype(BF16)


def add_pairs(ka, ra, kb, rb):
    rows, width = ka.shape
    return pl.pallas_call(
        pairs_kernel, out_shape=jax.ShapeDtypeStruct((2 * rows, width), BF16), name="add_pairs"
    )(ka, ra, kb, rb)


def image_kernel(block, pieces, probes, image, gram):
    total = probes[...].astype(F32)
    for k in range(pieces.shape[0]):
        total = total + pieces[k].astype(F32)
    image[...] = total
    gram[...] = exact_dot(total, total, ((0,), (0,)))


def image_and_gram(block, pieces, probes):
    count, rows, width = pieces.shape
    return pl.pallas_call(
        image_kernel,
        grid_spec=pltpu.PrefetchScalarGridSpec(
            num_scalar_prefetch=1,
            grid=(1,),
            in_specs=[
                pl.BlockSpec((count, rows, width), lambda i, b: (0, 0, 0)),
                pl.BlockSpec((rows, width), lambda i, b: (b[0], 0)),
            ],
            out_specs=[
                pl.BlockSpec((rows, width), lambda i, b: (0, 0)),
                pl.BlockSpec((width, width), lambda i, b: (0, 0)),
            ],
        ),
        out_shape=(
            jax.ShapeDtypeStruct((rows, width), F32),
            jax.ShapeDtypeStruct((width, width), F32),
        ),
        name="image_and_gram",
    )(block, pieces, probes)


def spread_sum_kernel(pieces, out):
    total = pieces[0]
    for k in range(1, pieces.shape[0]):
        total = total + pieces[k]
    for k in range(out.shape[0]):
        out[k] = total


def spread_sum(pieces, copies):
    return pl.pallas_call(
        spread_sum_kernel,
        out_shape=jax.ShapeDtypeStruct((copies,) + pieces.shape[1:], F32),
        name="spread_sum",
    )(pieces)


def eliminate(tiles, lane0):
    count, wide = len(tiles), len(tiles[0])
    sub = lax.broadcasted_iota(jnp.int32, (8, 128), 0)
    out = []
    for j in range(count):
        head = tiles[j]

        def columns(tile):
            first = lane0 + 8 * j
            return [
                jnp.broadcast_to(tile[0][:, first + k : first + k + 1], (8, 128)) for k in range(8)
            ]

        cols = columns(head)
        s = [[jnp.broadcast_to(cols[k][i : i + 1, :], (8, 128)) for k in range(i + 1)] for i in range(8)]
        low = [[None] * 8 for _ in range(8)]
        inv = [None] * 8
        for k in range(8):
            inv[k] = lax.rsqrt(s[k][k])
            for i in range(k + 1, 8):
                low[i][k] = s[i][k] * inv[k]
            for i in range(k + 1, 8):
                for m in range(k + 1, i + 1):
                    s[i][m] = s[i][m] - low[i][k] * low[m][k]
        u = []
        for i in range(8):
            parts = []
            for v in range(wide):
                a = jnp.broadcast_to(head[v][i : i + 1, :], (8, 128))
                for k in range(i):
                    a = a - low[i][k] * u[k][v]
                parts.append(a * inv[i])
            u.append(parts)
        rows = []
        for v in range(wide):
            t = u[0][v]
            for i in range(1, 8):
                t = jnp.where(sub == i, u[i][v], t)
            rows.append(t)
        out.append(rows)
        for r in range(j + 1, count):
            c = columns(tiles[r])
            l = []
            for i in range(8):
                a = c[i]
                for k in range(i):
                    a = a - low[i][k] * l[k]
                l.append(a * inv[i])
            new = []
            for v in range(wide):
                t = tiles[r][v]
                for i in range(8):
                    t = t - l[i] * u[i][v]
                new.append(t)
            tiles[r] = new
    return out


def factor_kernel(scale, gram, upper, inverse, work):
    n = gram.shape[0]
    panels = n // PANEL
    lane = lax.broadcasted_iota(jnp.int32, (8, 128), 1)
    sub = lax.broadcasted_iota(jnp.int32, (8, 128), 0)
    src = gram
    for p in range(panels):
        r0 = p * PANEL
        first, lane0 = r0 // 128, r0 % 128
        used = range(first, n // 128)
        tiles = []
        for t in range(PANEL // 8):
            row = src[r0 + 8 * t : r0 + 8 * t + 8, :]
            unit = jnp.where(lane == sub + 8 * t, 1.0, 0.0).astype(F32)
            tiles.append([row[:, 128 * v : 128 * v + 128] for v in used] + [unit])
        out = eliminate(tiles, lane0)
        rows = [jnp.concatenate([o[v] for o in out], axis=0) for v in range(len(used))]
        corner = jnp.concatenate([o[-1] for o in out], axis=0)[:, :PANEL]
        rows = [jnp.zeros((PANEL, 128), F32)] * first + rows
        u = jnp.concatenate(rows, axis=1)
        row_id = lax.broadcasted_iota(jnp.int32, (PANEL, n), 0) + r0
        col_id = lax.broadcasted_iota(jnp.int32, (PANEL, n), 1)
        u = jnp.where(col_id >= row_id, u, 0.0)
        work[r0 : r0 + PANEL, :] = u
        upper[r0 : r0 + PANEL, :] = u * (1.0 / scale)
        for q0 in range(r0 + PANEL, n, PANEL):
            update = exact_dot(u[:, q0 : q0 + PANEL], u, ((0,), (0,)))
            work[q0 : q0 + PANEL, :] = src[q0 : q0 + PANEL, :] - update
        src = work
        right = jnp.where(col_id == row_id, 1.0, 0.0).astype(F32)
        if p:
            right = right - exact_dot(work[0:r0, r0 : r0 + PANEL], inverse[0:r0, :], ((0,), (0,)))
        inverse[r0 : r0 + PANEL, :] = exact_dot(corner, right, ((1,), (0,)))


def cholesky_and_inverse(gram, scale):
    n = gram.shape[0]
    shape = jax.ShapeDtypeStruct((n, n), F32)
    return pl.pallas_call(
        functools.partial(factor_kernel, scale),
        out_shape=(shape, shape),
        scratch_shapes=[pltpu.VMEM((n, n), F32)],
        compiler_params=pltpu.CompilerParams(vmem_limit_bytes=16 * MIB),
        name="cholesky_and_inverse",
    )(gram)


def basis_kernel(scale, image, inverse, out):
    x = image[0, :, 0].reshape(out.shape)
    out[...] = split_dot(x, inverse[...] * scale, ((1,), (1,)))


def make_basis(image, inverse, scale):
    rows, width = image.shape[-2:]
    view = image.reshape(2, 4, 2, rows, width)
    return pl.pallas_call(
        functools.partial(basis_kernel, scale),
        grid=(2, 2),
        in_specs=[
            pl.BlockSpec((1, 4, 1, rows, width), lambda h, o: (h, 0, o, 0, 0)),
            pl.BlockSpec((width, width), lambda h, o: (0, 0)),
        ],
        out_specs=pl.BlockSpec((4 * rows, width), lambda h, o: (2 * h + o, 0)),
        out_shape=jax.ShapeDtypeStruct((16 * rows, width), F32),
        name="make_basis",
    )(view, inverse)


def shifted(value, axis, steps):
    count = lax.axis_size(axis)
    leading, last = (max(0, -steps), min(count, count - steps))
    return lax.ppermute(value, axis, [(source, source + steps) for source in range(leading, last)])


def body(probes, weights, columns):
    rows, width = probes.shape
    w_local = weights[0]
    blocks, _, bs, _ = w_local.shape
    low = shifted(probes, "brick", 1)
    high = shifted(probes, "brick", -1)
    shape = (blocks, bs, width)
    own, below, above = apply_operator(
        columns.reshape(-1), w_local, low.reshape(shape), probes.reshape(shape), high.reshape(shape)
    )
    from_above = shifted(below.reshape(rows, width), "brick", -1)
    from_below = shifted(above.reshape(rows, width), "brick", 1)

    zh, zp = lax.axis_index("zh"), lax.axis_index("zp")
    odd = jnp.full((1,), zp, jnp.int32)
    keep_a, send_a, keep_b, send_b = split_halves(odd, own.reshape(rows, width), from_above, from_below)
    n = lax.axis_size("zh") * lax.axis_size("zp")
    got_a = lax.ppermute(send_a, DEPTH, [(i, i ^ 1) for i in range(n)])
    got_b = lax.ppermute(send_b, DEPTH, [(i, (((i + 1) ^ 1) - 1) % n) for i in range(n)])
    held = add_pairs(keep_a, got_a, keep_b, got_b)
    pieces = lax.all_to_all(held.reshape(n // 2, rows // n, width), "zh", 0, 0)
    block = (zh // 4) * 8 + zp * 4 + zh % 4
    image, gram = image_and_gram(jnp.full((1,), block, jnp.int32), pieces, probes)
    whole_image = lax.all_gather(image, DEPTH)

    bricks = lax.axis_size("brick")
    share = lax.all_to_all(gram.reshape(bricks, width // bricks, width), "brick", 0, 0)
    share = lax.all_to_all(spread_sum(share, n), DEPTH, 0, 0)
    gram = lax.all_to_all(spread_sum(share, bricks), "brick", 0, 0).reshape(width, width)

    scale = math.sqrt(rows * bricks)
    upper, inverse = cholesky_and_inverse(gram, scale)
    return make_basis(whole_image, inverse, scale), upper


def solution(mesh):
    deep = mesh.devices.reshape(mesh.devices.shape[0] // 2, 2, mesh.devices.shape[1])
    mesh = Mesh(deep, DEPTH + ("brick",))
    in_specs = (P("brick", None), P(DEPTH, "brick", None, None, None), P(DEPTH, "brick", None))
    out_specs = (P("brick", None), P())
    return jax.shard_map(body, mesh=mesh, in_specs=in_specs, out_specs=out_specs, check_vma=False)
```

time: 450 us -> 212 us (0.47)
  the two profiles are of different devices: /device:TPU:1 before, /device:TPU:28 now
where the time goes in v1:
time: 212 us
  waiting for transfers between devices  73 us (34%)
  blocking collectives  49 us (23%)
  starting transfers between devices  34.1 us (16%)
  Pallas kernels  32.9 us (16%)
  between operations  14.1 us (7%)
  local copies, waits for them, and re-layouts  8.43 us (4%)
    all_to_all x1, waiting for transfers between devices, body(): pieces = lax.all_to_all(held.reshape(n // 2, rows // n, width), 'zh', 0, 0)  29 us
    ppermute x4, waiting for transfers between devices, shifted(): lax.ppermute(value, axis, [(source, source + steps) for source in range(l...  26 us
    all_to_all x1, blocking collectives, body(): share = lax.all_to_all(spread_sum(share, n), DEPTH, 0, 0)  20.1 us
    all_to_all x1, blocking collectives, body(): lax.all_to_all(gram.reshape(bricks, width // bricks, width), 'brick', 0, 0)  15.9 us
    all_to_all x1, blocking collectives, body(): lax.all_to_all(spread_sum(share, bricks), 'brick', 0, 0)  13 us
    all_gather x1, waiting for transfers between devices, body(): whole_image = lax.all_gather(image, DEPTH)  12.9 us
    ppermute x4, starting transfers between devices, shifted(): lax.ppermute(value, axis, [(source, source + steps) for source in range(l...  11.2 us
    ppermute x1, starting transfers between devices, body(): lax.ppermute(send_b, DEPTH, [(i, ((i + 1 ^ 1) - 1) % n) for i in range(n)])  10.5 us
  transfers between devices with their start and end apart: 8, of which 7 were waited for; matrix products, arithmetic and copies ran while one was open for 0% of the time, Pallas kernels for 6%

profile of v1, /device:TPU:28, one launch (start us, length us, event | category | flops | bytes accessed | tf_op | source)
XLA Modules:
  0.0 211.5 jit_solution(2741999540627300426)
XLA Ops:
  7.2 1.9 collective-permute-start
  9.1 3.6 %collective-permute-start.1 = (bf16[2048,256]{1,0:T(8,128)(2,1)}, bf16[2048,256]{1,0:T(8,128)(2,1)S(1)}, u32[]{:S(2)}, u32[]{:S(2)}) collective-permute-start(bf16[2048,256]{1,0:T(8,128)(2,1)} %probes.1), channel_id=1, source_target_pairs={{1,0},{2,1},{3,2},{4,3},{5,4},{6,5},{7,6},{8,7},{9,8},{10,9},{11,1... | collective-permute-start | bytes 3145736 | tf_op jit(solution)/shard_map/ppermute | solution.py:319
  12.7 0.8 copy.6
  13.5 0.1 reshape.40.cols
  13.6 9.9 %collective-permute-done = bf16[2048,256]{1,0:T(8,128)(2,1)S(1)} collective-permute-done((bf16[2048,256]{1,0:T(8,128)(2,1)}, bf16[2048,256]{1,0:T(8,128)(2,1)S(1)}, u32[]{:S(2)}, u32[]{:S(2)}) %collective-permute-start) | collective-permute-done | bytes 1048608 | tf_op jit(solution)/shard_map/ppermute | solution.py:319
  23.5 1.9 collective-permute-done.1
  25.4 0.0 copy-start.1
  25.4 1.2 copy-done.1
  26.6 0.0 copy-start.2
  26.6 1.9 copy-done.2
  28.5 7.5 %normal_operator.1 = (f32[8,256,256]{2,1,0:T(8,128)S(1)}, bf16[8,256,256]{2,1,0:T(8,128)(2,1)}, bf16[8,256,256]{2,1,0:T(8,128)(2,1)S(1)}) custom-call(s32[24]{0:T(128)S(1)} %reshape.40.cols, bf16[8,3,256,256]{3,2,1,0:T(8,128)(2,1)S(1)} %bitcast.20, bf16[8,256,256]{2,1,0:T(8,128)(2,1)S(1)} %bitcast.21, bf16[8,256,256]{2,1,0:T(8,128)(2,1)S(1)} %bitcast.19, ...), custom_call_target="tpu_custom_call" | custom-call | tf_op jit(solution)/shard_map/normal_operator/pallas_call | solution.py:74
  35.9 0.0 copy-start
  35.9 1.3 copy-done
  37.3 3.7 %collective-permute-start.2 = (bf16[2048,256]{1,0:T(8,128)(2,1)}, bf16[2048,256]{1,0:T(8,128)(2,1)S(1)}, u32[]{:S(2)}, u32[]{:S(2)}) collective-permute-start(bf16[2048,256]{1,0:T(8,128)(2,1)} %bitcast.7), channel_id=1, source_target_pairs={{1,0},{2,1},{3,2},{4,3},{5,4},{6,5},{7,6},{8,7},{9,8},{10,9},{11,1... | collective-permute-start | bytes 3145736 | tf_op jit(solution)/shard_map/ppermute | solution.py:319
  41.0 1.9 collective-permute-start.3
  42.9 10.7 %collective-permute-done.2 = bf16[2048,256]{1,0:T(8,128)(2,1)S(1)} collective-permute-done((bf16[2048,256]{1,0:T(8,128)(2,1)}, bf16[2048,256]{1,0:T(8,128)(2,1)S(1)}, u32[]{:S(2)}, u32[]{:S(2)}) %collective-permute-start.2) | collective-permute-done | bytes 1048608 | tf_op jit(solution)/shard_map/ppermute | solution.py:319
  53.6 0.0 copy-start.4
  53.6 3.5 %collective-permute-done.3 = bf16[2048,256]{1,0:T(8,128)(2,1)S(1)} collective-permute-done((bf16[2048,256]{1,0:T(8,128)(2,1)S(1)}, bf16[2048,256]{1,0:T(8,128)(2,1)S(1)}, u32[]{:S(2)}, u32[]{:S(2)}) %collective-permute-start.3) | collective-permute-done | bytes 1048608 | tf_op jit(solution)/shard_map/ppermute | solution.py:319
  57.1 0.0 copy-start.5
  57.1 0.0 copy-done.4
  57.1 1.0 copy-done.5
  58.1 4.1 %split_halves.1 = (f32[512,256]{1,0:T(8,128)}, bf16[512,256]{1,0:T(8,128)(2,1)}, f32[512,256]{1,0:T(8,128)}, bf16[512,256]{1,0:T(8,128)(2,1)}) custom-call(s32[1]{0:T(128)} %bitcast.1.odd, f32[4,512,256]{2,1,0:T(8,128)} %bitcast.15, bf16[4,512,256]{2,1,0:T(8,128)(2,1)} %bitcast.25, bf16[4,512,256]{2,1,0:T(8,128)(2,1)} %bitcast.29, f32[4,512,256]{2,1,0:T(8,128)} %bitcast.16, ...), custom_call_target="tpu_custom_call" | custom-call | tf_op jit(solution)/shard_map/split_halves/pallas_call | solution.py:119
  62.1 3.8 %collective-permute-start.4 = (bf16[512,256]{1,0:T(8,128)(2,1)}, bf16[512,256]{1,0:T(8,128)(2,1)S(1)}, u32[]{:S(2)}, u32[]{:S(2)}) collective-permute-start(bf16[512,256]{1,0:T(8,128)(2,1)} %get-tuple-element.17), channel_id=1, source_target_pairs={{0,32},{32,0},{64,96},{96,64},{128,160},{160,128},{192,224},{224,1... | collective-permute-start | bytes 786440 | tf_op jit(solution)/shard_map/ppermute | solution.py:339
  66.0 10.5 %collective-permute-start.5 = (bf16[512,256]{1,0:T(8,128)(2,1)}, bf16[512,256]{1,0:T(8,128)(2,1)S(1)}, u32[]{:S(2)}, u32[]{:S(2)}) collective-permute-start(bf16[512,256]{1,0:T(8,128)(2,1)} %get-tuple-element.19), channel_id=1, source_target_pairs={{0,480},{32,64},{64,32},{96,128},{128,96},{160,192},{192,160},{224... | collective-permute-start | bytes 786440 | tf_op jit(solution)/shard_map/ppermute | solution.py:340
  76.5 0.0 collective-permute-done.4.ra
  76.5 0.0 copy-start.7
  76.5 5.2 %collective-permute-done.5.rb = bf16[512,256]{1,0:T(8,128)(2,1)S(1)} collective-permute-done((bf16[512,256]{1,0:T(8,128)(2,1)}, bf16[512,256]{1,0:T(8,128)(2,1)S(1)}, u32[]{:S(2)}, u32[]{:S(2)}) %collective-permute-start.5) | collective-permute-done | bytes 262176 | tf_op jit(solution)/shard_map/ppermute | solution.py:340
  81.7 0.0 copy-start.8
  81.7 0.0 copy-done.7
  81.7 0.7 copy-done.8
  82.4 2.2 %add_pairs.1 = bf16[1024,256]{1,0:T(8,128)(2,1)} custom-call(f32[512,256]{1,0:T(8,128)} %get-tuple-element.16.ka, bf16[512,256]{1,0:T(8,128)(2,1)} %copy-done.7, f32[512,256]{1,0:T(8,128)} %get-tuple-element.18.kb, bf16[512,256]{1,0:T(8,128)(2,1)} %copy-done.8), custom_call_target="tpu_custom_call" | custom-call | tf_op jit(solution)/shard_map/add_pairs/pallas_call | solution.py:137
  84.6 8.6 %all-to-all-start = ((bf16[8,128,256]{2,1,0:T(8,128)(2,1)}), bf16[8,128,256]{2,1,0:T(8,128)(2,1)S(1)}, u32[]{:S(2)}, u32[]{:S(2)}) async-start(bf16[8,128,256]{2,1,0:T(8,128)(2,1)} %bitcast.34), calls=%async_computation | async-start | bytes 1048576 | tf_op jit(solution)/shard_map/all_to_all | solution.py:342
  93.2 0.0 all-gather.3.cloned.1.call-start
  93.2 29.0 %all-to-all-done.pieces = bf16[8,128,256]{2,1,0:T(8,128)(2,1)S(1)} async-done(((bf16[8,128,256]{2,1,0:T(8,128)(2,1)}), bf16[8,128,256]{2,1,0:T(8,128)(2,1)S(1)}, u32[]{:S(2)}, u32[]{:S(2)}) %all-to-all-start) | async-done | bytes 524320 | tf_op jit(solution)/shard_map/all_to_all | solution.py:342
  122.2 0.0 copy-start.6
  122.2 0.8 copy-done.6
  123.0 2.2 %image_and_gram.1 = (f32[128,256]{1,0:T(8,128)}, f32[256,256]{1,0:T(8,128)}) custom-call(s32[1]{0:T(128)} %bitcast.block, bf16[8,128,256]{2,1,0:T(8,128)(2,1)} %copy-done.6, bf16[2048,256]{1,0:T(8,128)(2,1)} %probes.1), custom_call_target="tpu_custom_call" | custom-call | tf_op jit(solution)/shard_map/image_and_gram/pallas_call | solution.py:152
  125.2 0.0 all-gather.3.cloned.1.call-update
  125.2 15.9 %all_to_all.20.pieces = f32[32,8,256]{2,1,0:T(8,128)} all-to-all(f32[32,8,256]{2,1,0:T(8,128)} %bitcast.35), channel_id=1, replica_groups=mesh['zh'=8,'zp'=2,'brick'=32] {'brick'}, dimensions={0} | all-to-all | bytes 524288 | tf_op jit(solution)/shard_map/all_to_all | solution.py:348
  141.2 1.6 spread_sum.2
  142.8 20.1 %all_to_all.21.pieces = f32[16,8,256]{2,1,0:T(8,128)} all-to-all(f32[16,8,256]{2,1,0:T(8,128)} %spread_sum.2), channel_id=1, replica_groups=mesh['zh'=8,'zp'=2,'brick'=32] {'zh','zp'}, dimensions={0} | all-to-all | bytes 262144 | tf_op jit(solution)/shard_map/all_to_all | solution.py:349
  162.9 1.6 spread_sum.3
  164.5 13.0 %all_to_all.22 = f32[32,8,256]{2,1,0:T(8,128)S(1)} all-to-all(f32[32,8,256]{2,1,0:T(8,128)} %spread_sum.3), channel_id=1, replica_groups=mesh['zh'=8,'zp'=2,'brick'=32] {'brick'}, dimensions={0} | all-to-all | bytes 524288 | tf_op jit(solution)/shard_map/all_to_all | solution.py:350
  177.5 9.0 %cholesky_and_inverse.1 = (f32[256,256]{1,0:T(8,128)}, f32[256,256]{1,0:T(8,128)S(1)}) custom-call(f32[256,256]{1,0:T(8,128)S(1)} %bitcast.23), custom_call_target="tpu_custom_call" | custom-call | tf_op jit(solution)/shard_map/cholesky_and_inverse/pallas_call | solution.py:286
  186.5 0.0 copy-start.3
  186.5 0.7 copy-done.3
  187.2 12.9 %all-gather.3.cloned.1.call-done = f32[2048,256]{1,0:T(8,128)} async-done(((f32[128,256]{1,0:T(8,128)}), f32[2048,256]{1,0:T(8,128)}) %all-gather.3.cloned.1.call-update) | async-done | bytes 2097168 | tf_op jit(solution)/shard_map/all_gather | solution.py:345
  200.1 4.6 %make_basis.1 = f32[2048,256]{1,0:T(8,128)} custom-call(f32[2,4,2,128,256]{4,3,2,1,0:T(8,128)} %bitcast.33, f32[256,256]{1,0:T(8,128)} %copy-done.3), custom_call_target="tpu_custom_call" | custom-call | tf_op jit(solution)/shard_map/make_basis/pallas_call | solution.py:303
Async XLA Ops:
  7.2 16.3 %collective-permute-start = (bf16[2048,256]{1,0:T(8,128)(2,1)}, bf16[2048,256]{1,0:T(8,128)(2,1)S(1)}, u32[]{:S(2)}, u32[]{:S(2)}) collective-permute-start(bf16[2048,256]{1,0:T(8,128)(2,1)} %probes.1), channel_id=1, source_target_pairs={{0,1},{1,2},{2,3},{3,4},{4,5},{5,6},{6,7},{7,8},{8,9},{9,10},{10,1... | collective-permute-start | bytes 3145736 | tf_op jit(solution)/shard_map/ppermute | solution.py:319
  9.1 16.3 %collective-permute-start.1 = (bf16[2048,256]{1,0:T(8,128)(2,1)}, bf16[2048,256]{1,0:T(8,128)(2,1)S(1)}, u32[]{:S(2)}, u32[]{:S(2)}) collective-permute-start(bf16[2048,256]{1,0:T(8,128)(2,1)} %probes.1), channel_id=1, source_target_pairs={{1,0},{2,1},{3,2},{4,3},{5,4},{6,5},{7,6},{8,7},{9,8},{10,9},{11,1... | collective-permute-start | bytes 3145736 | tf_op jit(solution)/shard_map/ppermute | solution.py:319
  25.4 1.2 copy-start.1
  26.6 1.9 copy-start.2
  35.9 1.3 copy-start
  37.3 16.3 %collective-permute-start.2 = (bf16[2048,256]{1,0:T(8,128)(2,1)}, bf16[2048,256]{1,0:T(8,128)(2,1)S(1)}, u32[]{:S(2)}, u32[]{:S(2)}) collective-permute-start(bf16[2048,256]{1,0:T(8,128)(2,1)} %bitcast.7), channel_id=1, source_target_pairs={{1,0},{2,1},{3,2},{4,3},{5,4},{6,5},{7,6},{8,7},{9,8},{10,9},{11,1... | collective-permute-start | bytes 3145736 | tf_op jit(solution)/shard_map/ppermute | solution.py:319
  41.0 16.1 %collective-permute-start.3 = (bf16[2048,256]{1,0:T(8,128)(2,1)S(1)}, bf16[2048,256]{1,0:T(8,128)(2,1)S(1)}, u32[]{:S(2)}, u32[]{:S(2)}) collective-permute-start(bf16[2048,256]{1,0:T(8,128)(2,1)S(1)} %bitcast.24), channel_id=1, source_target_pairs={{0,1},{1,2},{2,3},{3,4},{4,5},{5,6},{6,7},{7,8},{8,9},{9,10},{10,1... | collective-permute-start | bytes 3145736 | tf_op jit(solution)/shard_map/ppermute | solution.py:319
  53.6 3.5 %copy-start.4 = (bf16[2048,256]{1,0:T(8,128)(2,1)}, bf16[2048,256]{1,0:T(8,128)(2,1)S(1)}, u32[]{:S(2)}) copy-start(bf16[2048,256]{1,0:T(8,128)(2,1)S(1)} %collective-permute-done.2) | copy-start | bytes 3145732
  57.1 1.0 copy-start.5
  62.1 14.3 %collective-permute-start.4 = (bf16[512,256]{1,0:T(8,128)(2,1)}, bf16[512,256]{1,0:T(8,128)(2,1)S(1)}, u32[]{:S(2)}, u32[]{:S(2)}) collective-permute-start(bf16[512,256]{1,0:T(8,128)(2,1)} %get-tuple-element.17), channel_id=1, source_target_pairs={{0,32},{32,0},{64,96},{96,64},{128,160},{160,128},{192,224},{224,1... | collective-permute-start | bytes 786440 | tf_op jit(solution)/shard_map/ppermute | solution.py:339
  66.0 15.7 %collective-permute-start.5 = (bf16[512,256]{1,0:T(8,128)(2,1)}, bf16[512,256]{1,0:T(8,128)(2,1)S(1)}, u32[]{:S(2)}, u32[]{:S(2)}) collective-permute-start(bf16[512,256]{1,0:T(8,128)(2,1)} %get-tuple-element.19), channel_id=1, source_target_pairs={{0,480},{32,64},{64,32},{96,128},{128,96},{160,192},{192,160},{224... | collective-permute-start | bytes 786440 | tf_op jit(solution)/shard_map/ppermute | solution.py:340
  76.5 5.2 %copy-start.7 = (bf16[512,256]{1,0:T(8,128)(2,1)}, bf16[512,256]{1,0:T(8,128)(2,1)S(1)}, u32[]{:S(2)}) copy-start(bf16[512,256]{1,0:T(8,128)(2,1)S(1)} %collective-permute-done.4.ra) | copy-start | bytes 786436
  81.7 0.7 copy-start.8
  84.6 37.6 %all-to-all-start = ((bf16[8,128,256]{2,1,0:T(8,128)(2,1)}), bf16[8,128,256]{2,1,0:T(8,128)(2,1)S(1)}, u32[]{:S(2)}, u32[]{:S(2)}) async-start(bf16[8,128,256]{2,1,0:T(8,128)(2,1)} %bitcast.34), calls=%async_computation | async-start | bytes 1048576 | tf_op jit(solution)/shard_map/all_to_all | solution.py:342
  93.2 106.9 %all-gather.3.cloned.1.call-start = ((), (), s32[]{:S(2)}) async-start(), calls=%async_computation.4 | async-start | bytes 2228224 | tf_op jit(solution)/shard_map/all_gather | solution.py:345
  122.2 0.8 copy-start.6
  186.5 0.7 copy-start.3
Sparse Core Ops, SparseCore 0:
  125.4 74.6 all-gather.2

commit v2 on v1

v2 whole, which is shorter than its diff:
```python
import functools
import math

import jax
import jax.numpy as jnp
from jax import lax
from jax.experimental import pallas as pl
from jax.experimental.pallas import tpu as pltpu
from jax.sharding import Mesh
from jax.sharding import PartitionSpec as P

F32 = jnp.float32
BF16 = jnp.bfloat16
PANEL = 64
MIB = 1024 * 1024
DEPTH = ("zh", "zp")


def exact_dot(a, b, dims):
    return lax.dot_general(
        a, b, (dims, ((), ())), precision=lax.Precision.HIGHEST, preferred_element_type=F32
    )


def in_vmem():
    return pl.BlockSpec(memory_space=pltpu.VMEM)


def params(mib):
    return pltpu.CompilerParams(vmem_limit_bytes=mib * MIB)


def operator_kernel(cols, w_hbm, low_ref, own_ref, high_ref, o_own, o_below, o_above, w_ref, s_below, s_above, sems):
    blocks = own_ref.shape[0]

    def fetch(r):
        return pltpu.make_async_copy(w_hbm.at[r], w_ref.at[r], sems.at[r])

    for r in range(blocks):
        fetch(r).start()
    s_below[...] = jnp.zeros_like(s_below)
    s_above[...] = jnp.zeros_like(s_above)

    def step(r, carry):
        ids = [cols[3 * r + j] for j in range(3)]
        at_low = jnp.where(ids[0] < blocks, 0, jnp.where(ids[1] < blocks, 1, 2))
        at_high = jnp.where(ids[0] >= 2 * blocks, 0, jnp.where(ids[1] >= 2 * blocks, 1, 2))
        at_own = 3 - at_low - at_high
        c_low = cols[3 * r + at_low]
        c_high = cols[3 * r + at_high] - 2 * blocks
        fetch(r).wait()
        w_low, w_own, w_high = w_ref[r, at_low], w_ref[r, at_own], w_ref[r, at_high]
        dot = functools.partial(jnp.dot, preferred_element_type=F32)
        data = dot(w_low, low_ref[c_low]) + dot(w_own, own_ref[r]) + dot(w_high, high_ref[c_high])
        data = data.T.astype(BF16)
        term = dot(data, w_own)
        o_own[2 * r] = term[:, :128]
        o_own[2 * r + 1] = term[:, 128:]
        s_below[c_low] += dot(data, w_low)
        s_above[c_high] += dot(data, w_high)
        return carry

    lax.fori_loop(0, blocks, step, 0)
    for q in range(blocks):
        for field, out in ((s_below, o_below), (s_above, o_above)):
            out[2 * q] = field[q, :, :128].astype(BF16)
            out[2 * q + 1] = field[q, :, 128:].astype(BF16)


def apply_operator(cols, weights, low, own, high):
    blocks, slots, bs, _ = weights.shape
    width = own.shape[-1]
    shape = (2 * blocks, width, bs // 2)
    field = pltpu.VMEM((blocks, width, bs), F32)
    return pl.pallas_call(
        operator_kernel,
        in_specs=[
            pl.BlockSpec(memory_space=pltpu.SMEM),
            pl.BlockSpec(memory_space=pltpu.HBM),
            in_vmem(),
            in_vmem(),
            in_vmem(),
        ],
        out_specs=[in_vmem()] * 3,
        out_shape=(
            jax.ShapeDtypeStruct(shape, F32),
            jax.ShapeDtypeStruct(shape, BF16),
            jax.ShapeDtypeStruct(shape, BF16),
        ),
        scratch_shapes=[
            pltpu.VMEM(weights.shape, BF16),
            field,
            field,
            pltpu.SemaphoreType.DMA((blocks,)),
        ],
        compiler_params=params(24),
        name="normal_operator",
    )(cols, weights, low, own, high)


def halves_kernel(odd, own, above, below, keep_a, send_a, keep_b, send_b):
    part = keep_a.shape[0]
    o = odd[0]
    for out, first in ((keep_a, o), (send_a, 1 - o), (keep_b, 2 + o), (send_b, 3 - o)):
        for i in range(part):
            p = part * first + i
            out[i] = (own[p] + (above[p].astype(F32) + below[p].astype(F32))).astype(out.dtype)


def split_halves(odd, own, above, below):
    pieces, width, cells = own.shape
    kept, sent = (jax.ShapeDtypeStruct((pieces // 4, width, cells), t) for t in (F32, BF16))
    return pl.pallas_call(
        halves_kernel,
        in_specs=[pl.BlockSpec(memory_space=pltpu.SMEM)] + [in_vmem()] * 3,
        out_specs=[in_vmem()] * 4,
        out_shape=(kept, sent, kept, sent),
        compiler_params=params(12),
        name="split_halves",
    )(odd, own, above, below)


def pairs_kernel(ka, ra, kb, rb, out):
    n = ka.shape[0]
    for i in range(n):
        out[i] = (ka[i] + ra[i].astype(F32)).astype(BF16)
        out[n + i] = (kb[i] + rb[i].astype(F32)).astype(BF16)


def add_pairs(ka, ra, kb, rb):
    n, width, cells = ka.shape
    return pl.pallas_call(
        pairs_kernel,
        in_specs=[in_vmem()] * 4,
        out_specs=in_vmem(),
        out_shape=jax.ShapeDtypeStruct((2 * n, width, cells), BF16),
        compiler_params=params(8),
        name="add_pairs",
    )(ka, ra, kb, rb)


def image_kernel(block, pieces, probes, image, own, sem):
    rows = own.shape[0]
    copy = pltpu.make_async_copy(probes.at[pl.ds(block[0] * rows, rows)], own, sem)
    copy.start()
    total = pieces[0].astype(F32)
    for k in range(1, pieces.shape[0]):
        total = total + pieces[k].astype(F32)
    copy.wait()
    image[...] = own[...].astype(F32) + total.T


def make_image(block, pieces, probes):
    _, width, cells = pieces.shape
    return pl.pallas_call(
        image_kernel,
        in_specs=[
            pl.BlockSpec(memory_space=pltpu.SMEM),
            in_vmem(),
            pl.BlockSpec(memory_space=pltpu.HBM),
        ],
        out_specs=in_vmem(),
        out_shape=jax.ShapeDtypeStruct((cells, width), F32),
        scratch_shapes=[pltpu.VMEM((cells, width), BF16), pltpu.SemaphoreType.DMA],
        compiler_params=params(4),
        name="make_image",
    )(block, pieces, probes)


def gram_kernel(image, gram):
    gram[...] = exact_dot(image[...], image[...], ((0,), (0,)))


def make_gram(image):
    width = image.shape[1]
    return pl.pallas_call(
        gram_kernel,
        in_specs=[in_vmem()],
        out_specs=in_vmem(),
        out_shape=jax.ShapeDtypeStruct((width, width), F32),
        compiler_params=params(8),
        name="make_gram",
    )(image)


def spread_sum_kernel(pieces, out):
    total = pieces[0]
    for k in range(1, pieces.shape[0]):
        total = total + pieces[k]
    for k in range(out.shape[0]):
        out[k] = total


def spread_sum(pieces, copies):
    return pl.pallas_call(
        spread_sum_kernel,
        in_specs=[in_vmem()],
        out_specs=in_vmem(),
        out_shape=jax.ShapeDtypeStruct((copies,) + pieces.shape[1:], F32),
        compiler_params=params(4),
        name="spread_sum",
    )(pieces)


def eliminate(tiles, lane0):
    count, wide = len(tiles), len(tiles[0])
    sub = lax.broadcasted_iota(jnp.int32, (8, 128), 0)
    out = []
    for j in range(count):
        head = tiles[j]

        def columns(tile):
            first = lane0 + 8 * j
            return [
                jnp.broadcast_to(tile[0][:, first + k : first + k + 1], (8, 128)) for k in range(8)
            ]

        cols = columns(head)
        s = [[jnp.broadcast_to(cols[k][i : i + 1, :], (8, 128)) for k in range(i + 1)] for i in range(8)]
        low = [[None] * 8 for _ in range(8)]
        inv = [None] * 8
        for k in range(8):
            inv[k] = lax.rsqrt(s[k][k])
            for i in range(k + 1, 8):
                low[i][k] = s[i][k] * inv[k]
            for i in range(k + 1, 8):
                for m in range(k + 1, i + 1):
                    s[i][m] = s[i][m] - low[i][k] * low[m][k]
        u = []
        for i in range(8):
            parts = []
            for v in range(wide):
                a = jnp.broadcast_to(head[v][i : i + 1, :], (8, 128))
                for k in range(i):
                    a = a - low[i][k] * u[k][v]
                parts.append(a * inv[i])
            u.append(parts)
        rows = []
        for v in range(wide):
            t = u[0][v]
            for i in range(1, 8):
                t = jnp.where(sub == i, u[i][v], t)
            rows.append(t)
        out.append(rows)
        for r in range(j + 1, count):
            c = columns(tiles[r])
            l = []
            for i in range(8):
                a = c[i]
                for k in range(i):
                    a = a - low[i][k] * l[k]
                l.append(a * inv[i])
            new = []
            for v in range(wide):
                t = tiles[r][v]
                for i in range(8):
                    t = t - l[i] * u[i][v]
                new.append(t)
            tiles[r] = new
    return out


def factor_kernel(scale, gram, upper, high, low, work, inverse):
    n = gram.shape[0]
    panels = n // PANEL
    lane = lax.broadcasted_iota(jnp.int32, (8, 128), 1)
    sub = lax.broadcasted_iota(jnp.int32, (8, 128), 0)
    src = gram
    for p in range(panels):
        r0 = p * PANEL
        first, lane0 = r0 // 128, r0 % 128
        used = range(first, n // 128)
        tiles = []
        for t in range(PANEL // 8):
            row = src[r0 + 8 * t : r0 + 8 * t + 8, :]
            unit = jnp.where(lane == sub + 8 * t, 1.0, 0.0).astype(F32)
            tiles.append([row[:, 128 * v : 128 * v + 128] for v in used] + [unit])
        out = eliminate(tiles, lane0)
        rows = [jnp.concatenate([o[v] for o in out], axis=0) for v in range(len(used))]
        corner = jnp.concatenate([o[-1] for o in out], axis=0)[:, :PANEL]
        rows = [jnp.zeros((PANEL, 128), F32)] * first + rows
        u = jnp.concatenate(rows, axis=1)
        row_id = lax.broadcasted_iota(jnp.int32, (PANEL, n), 0) + r0
        col_id = lax.broadcasted_iota(jnp.int32, (PANEL, n), 1)
        u = jnp.where(col_id >= row_id, u, 0.0)
        work[r0 : r0 + PANEL, :] = u
        upper[r0 : r0 + PANEL, :] = u * (1.0 / scale)
        for q0 in range(r0 + PANEL, n, PANEL):
            update = exact_dot(u[:, q0 : q0 + PANEL], u, ((0,), (0,)))
            work[q0 : q0 + PANEL, :] = src[q0 : q0 + PANEL, :] - update
        src = work
        right = jnp.where(col_id == row_id, 1.0, 0.0).astype(F32)
        if p:
            right = right - exact_dot(work[0:r0, r0 : r0 + PANEL], inverse[0:r0, :], ((0,), (0,)))
        inverse[r0 : r0 + PANEL, :] = exact_dot(corner, right, ((1,), (0,)))
    turned = inverse[...].T * scale
    high[...] = turned.astype(BF16)
    low[...] = (turned - high[...].astype(F32)).astype(BF16)


def cholesky_and_inverse(gram, scale):
    n = gram.shape[0]
    full, half = (jax.ShapeDtypeStruct((n, n), t) for t in (F32, BF16))
    return pl.pallas_call(
        functools.partial(factor_kernel, scale),
        in_specs=[in_vmem()],
        out_specs=[in_vmem()] * 3,
        out_shape=(full, half, half),
        scratch_shapes=[pltpu.VMEM((n, n), F32)] * 2,
        compiler_params=params(8),
        name="cholesky_and_inverse",
    )(gram)


def basis_kernel(image, high, low, out):
    x = image[0, :, 0].reshape(out.shape)
    x_high = x.astype(BF16)
    x_low = (x - x_high.astype(F32)).astype(BF16)
    dot = functools.partial(jnp.dot, preferred_element_type=F32)
    out[...] = dot(x_high, high[...]) + (dot(x_high, low[...]) + dot(x_low, high[...]))


def make_basis(image, high, low):
    rows, width = image.shape[-2:]
    view = image.reshape(2, 4, 2, rows, width)
    return pl.pallas_call(
        basis_kernel,
        grid=(2, 2),
        in_specs=[
            pl.BlockSpec((1, 4, 1, rows, width), lambda h, o: (h, 0, o, 0, 0)),
            in_vmem(),
            in_vmem(),
        ],
        out_specs=pl.BlockSpec((4 * rows, width), lambda h, o: (2 * h + o, 0)),
        out_shape=jax.ShapeDtypeStruct((16 * rows, width), F32),
        compiler_params=params(16),
        name="make_basis",
    )(view, high, low)


def shifted(value, axis, steps):
    count = lax.axis_size(axis)
    leading, last = (max(0, -steps), min(count, count - steps))
    return lax.ppermute(value, axis, [(source, source + steps) for source in range(leading, last)])


def body(probes, weights, columns):
    rows, width = probes.shape
    w_local = weights[0]
    blocks, _, bs, _ = w_local.shape
    lower = shifted(probes, "brick", 1)
    higher = shifted(probes, "brick", -1)
    shape = (blocks, bs, width)
    own, below, above = apply_operator(
        columns.reshape(-1), w_local, lower.reshape(shape), probes.reshape(shape), higher.reshape(shape)
    )
    from_above = shifted(below, "brick", -1)
    from_below = shifted(above, "brick", 1)

    zh, zp = lax.axis_index("zh"), lax.axis_index("zp")
    odd = jnp.full((1,), zp, jnp.int32)
    keep_a, send_a, keep_b, send_b = split_halves(odd, own, from_above, from_below)
    n = lax.axis_size("zh") * lax.axis_size("zp")
    got_a = lax.ppermute(send_a, DEPTH, [(i, i ^ 1) for i in range(n)])
    got_b = lax.ppermute(send_b, DEPTH, [(i, (((i + 1) ^ 1) - 1) % n) for i in range(n)])
    pieces = lax.all_to_all(add_pairs(keep_a, got_a, keep_b, got_b), "zh", 0, 0)
    block = (zh // 4) * 8 + zp * 4 + zh % 4
    image = make_image(jnp.full((1,), block, jnp.int32), pieces, probes)
    whole_image = lax.all_gather(image, DEPTH)
    gram = make_gram(image)

    bricks = lax.axis_size("brick")
    share = lax.all_to_all(gram.reshape(bricks, width // bricks, width), "brick", 0, 0)
    share = lax.all_to_all(spread_sum(share, n), DEPTH, 0, 0)
    gram = lax.all_to_all(spread_sum(share, bricks), "brick", 0, 0).reshape(width, width)

    scale = math.sqrt(rows * bricks)
    upper, high, low = cholesky_and_inverse(gram, scale)
    return make_basis(whole_image, high, low), upper


def solution(mesh):
    deep = mesh.devices.reshape(mesh.devices.shape[0] // 2, 2, mesh.devices.shape[1])
    mesh = Mesh(deep, DEPTH + ("brick",))
    in_specs = (P("brick", None), P(DEPTH, "brick", None, None, None), P(DEPTH, "brick", None))
    out_specs = (P("brick", None), P())
    return jax.shard_map(body, mesh=mesh, in_specs=in_specs, out_specs=out_specs, check_vma=False)
```

time: 212 us -> 208 us (0.981)
  the two profiles are of different devices: /device:TPU:28 before, /device:TPU:12 now
where the time goes in v2:
time: 208 us; the launch traced here: 207 us
  waiting for transfers between devices  75.9 us (36%)
  blocking collectives  48.9 us (24%)
  starting transfers between devices  34.2 us (16%)
  Pallas kernels  26.3 us (13%)
  between operations  14.2 us (7%)
  local copies, waits for them, and re-layouts  7.74 us (4%)
    all_to_all x1, waiting for transfers between devices, body(): pieces = lax.all_to_all(add_pairs(keep_a, got_a, keep_b, got_b), 'zh', 0, 0)  29 us
    ppermute x4, waiting for transfers between devices, shifted(): lax.ppermute(value, axis, [(source, source + steps) for source in range(l...  26.3 us
    all_to_all x1, blocking collectives, body(): share = lax.all_to_all(spread_sum(share, n), DEPTH, 0, 0)  19.4 us
    all_to_all x1, blocking collectives, body(): lax.all_to_all(gram.reshape(bricks, width // bricks, width), 'brick', 0, 0)  16.6 us
    all_gather x1, waiting for transfers between devices, body(): whole_image = lax.all_gather(image, DEPTH)  15.6 us
    all_to_all x1, blocking collectives, body(): lax.all_to_all(spread_sum(share, bricks), 'brick', 0, 0)  12.9 us
    ppermute x4, starting transfers between devices, shifted(): lax.ppermute(value, axis, [(source, source + steps) for source in range(l...  11.2 us
    ppermute x1, starting transfers between devices, body(): lax.ppermute(send_b, DEPTH, [(i, ((i + 1 ^ 1) - 1) % n) for i in range(n)])  10.5 us
  transfers between devices with their start and end apart: 8, of which 7 were waited for; matrix products, arithmetic and copies ran while one was open for 0% of the time, Pallas kernels for 5%

profile of v2, /device:TPU:12, one launch (start us, length us, event | category | flops | bytes accessed | tf_op | source)
XLA Modules:
  0.0 207.2 jit_solution(5525246068808682774)
XLA Ops:
  7.2 1.9 collective-permute-start
  9.1 3.6 %collective-permute-start.1 = (bf16[2048,256]{1,0:T(8,128)(2,1)}, bf16[2048,256]{1,0:T(8,128)(2,1)S(1)}, u32[]{:S(2)}, u32[]{:S(2)}) collective-permute-start(bf16[2048,256]{1,0:T(8,128)(2,1)} %probes.1), channel_id=1, source_target_pairs={{1,0},{2,1},{3,2},{4,3},{5,4},{6,5},{7,6},{8,7},{9,8},{10,9},{11,1... | collective-permute-start | bytes 3145736 | tf_op jit(solution)/shard_map/ppermute | solution.py:344
  12.7 0.8 copy.6
  13.5 0.1 reshape.25.cols
  13.6 9.9 %collective-permute-done = bf16[2048,256]{1,0:T(8,128)(2,1)S(1)} collective-permute-done((bf16[2048,256]{1,0:T(8,128)(2,1)}, bf16[2048,256]{1,0:T(8,128)(2,1)S(1)}, u32[]{:S(2)}, u32[]{:S(2)}) %collective-permute-start) | collective-permute-done | bytes 1048608 | tf_op jit(solution)/shard_map/ppermute | solution.py:344
  23.5 1.9 collective-permute-done.1
  25.4 0.0 copy-start.4
  25.4 1.0 copy-done.4
  26.3 0.0 copy-start
  26.3 1.2 copy-done
  27.6 0.0 copy-start.2
  27.6 1.9 copy-done.2
  29.4 0.0 copy-start.5
  29.4 1.2 copy-done.5
  30.7 9.7 %normal_operator.1 = (f32[16,256,128]{2,1,0:T(8,128)S(1)}, bf16[16,256,128]{2,1,0:T(8,128)(2,1)}, bf16[16,256,128]{2,1,0:T(8,128)(2,1)}) custom-call(s32[24]{0:T(128)S(1)} %reshape.25.cols, bf16[8,3,256,256]{3,2,1,0:T(8,128)(2,1)S(1)} %bitcast.10, bf16[8,256,256]{2,1,0:T(8,128)(2,1)S(1)} %bitcast.12, bf16[8,256,256]{2,1,0:T(8,128)(2,1)S(1)} %bitcast.9, ...), custom_call_target="tpu_custom_call" | custom-call | tf_op jit(solution)/shard_map/normal_operator/pallas_call | solution.py:75
  40.4 3.7 %collective-permute-start.2 = (bf16[16,256,128]{2,1,0:T(8,128)(2,1)}, bf16[16,256,128]{2,1,0:T(8,128)(2,1)S(1)}, u32[]{:S(2)}, u32[]{:S(2)}) collective-permute-start(bf16[16,256,128]{2,1,0:T(8,128)(2,1)} %get-tuple-element.13), channel_id=1, source_target_pairs={{1,0},{2,1},{3,2},{4,3},{5,4},{6,5},{7,6},{8,7},{9,8},{10,9},{11,1... | collective-permute-start | bytes 3145736 | tf_op jit(solution)/shard_map/ppermute | solution.py:344
  44.1 1.9 collective-permute-start.3
  46.0 10.7 %collective-permute-done.2.above = bf16[16,256,128]{2,1,0:T(8,128)(2,1)S(1)} collective-permute-done((bf16[16,256,128]{2,1,0:T(8,128)(2,1)}, bf16[16,256,128]{2,1,0:T(8,128)(2,1)S(1)}, u32[]{:S(2)}, u32[]{:S(2)}) %collective-permute-start.2) | collective-permute-done | bytes 1048608 | tf_op jit(solution)/shard_map/ppermute | solution.py:344
  56.7 3.8 %collective-permute-done.3.below = bf16[16,256,128]{2,1,0:T(8,128)(2,1)} collective-permute-done((bf16[16,256,128]{2,1,0:T(8,128)(2,1)}, bf16[16,256,128]{2,1,0:T(8,128)(2,1)}, u32[]{:S(2)}, u32[]{:S(2)}) %collective-permute-start.3) | collective-permute-done | bytes 1048608 | tf_op jit(solution)/shard_map/ppermute | solution.py:344
  60.5 1.5 split_halves.1
  62.0 0.0 copy-start.1
  62.1 4.0 %collective-permute-start.4 = (bf16[4,256,128]{2,1,0:T(8,128)(2,1)S(1)}, bf16[4,256,128]{2,1,0:T(8,128)(2,1)S(1)}, u32[]{:S(2)}, u32[]{:S(2)}) collective-permute-start(bf16[4,256,128]{2,1,0:T(8,128)(2,1)S(1)} %get-tuple-element.16), channel_id=1, source_target_pairs={{0,32},{32,0},{64,96},{96,64},{128,160},{160,128},{192,224},{224,1... | collective-permute-start | bytes 786440 | tf_op jit(solution)/shard_map/ppermute | solution.py:364
  66.0 10.5 %collective-permute-start.5 = (bf16[4,256,128]{2,1,0:T(8,128)(2,1)S(1)}, bf16[4,256,128]{2,1,0:T(8,128)(2,1)S(1)}, u32[]{:S(2)}, u32[]{:S(2)}) collective-permute-start(bf16[4,256,128]{2,1,0:T(8,128)(2,1)S(1)} %get-tuple-element.18), channel_id=1, source_target_pairs={{0,480},{32,64},{64,32},{96,128},{128,96},{160,192},{192,160},{224... | collective-permute-start | bytes 786440 | tf_op jit(solution)/shard_map/ppermute | solution.py:365
  76.5 0.0 collective-permute-done.4.ra
  76.5 5.0 %collective-permute-done.5.rb = bf16[4,256,128]{2,1,0:T(8,128)(2,1)S(1)} collective-permute-done((bf16[4,256,128]{2,1,0:T(8,128)(2,1)S(1)}, bf16[4,256,128]{2,1,0:T(8,128)(2,1)S(1)}, u32[]{:S(2)}, u32[]{:S(2)}) %collective-permute-start.5) | collective-permute-done | bytes 262176 | tf_op jit(solution)/shard_map/ppermute | solution.py:365
  81.5 0.9 add_pairs.1
  82.4 8.6 %all-to-all-start = ((bf16[8,256,128]{2,1,0:T(8,128)(2,1)}), bf16[8,256,128]{2,1,0:T(8,128)(2,1)S(1)}, u32[]{:S(2)}, u32[]{:S(2)}) async-start(bf16[8,256,128]{2,1,0:T(8,128)(2,1)} %add_pairs.1), calls=%async_computation | async-start | bytes 1048576 | tf_op jit(solution)/shard_map/all_to_all | solution.py:366
  91.0 0.0 all-gather.3.cloned.1.call-start
  91.1 29.0 %all-to-all-done.pieces = bf16[8,256,128]{2,1,0:T(8,128)(2,1)S(1)} async-done(((bf16[8,256,128]{2,1,0:T(8,128)(2,1)}), bf16[8,256,128]{2,1,0:T(8,128)(2,1)S(1)}, u32[]{:S(2)}, u32[]{:S(2)}) %all-to-all-start) | async-done | bytes 524320 | tf_op jit(solution)/shard_map/all_to_all | solution.py:366
  120.1 0.0 copy-done.1
  120.1 0.9 make_image.1.image
  121.0 0.0 all-gather.3.cloned.1.call-update
  121.0 1.3 make_gram.1
  122.3 16.6 %all_to_all.20.pieces = f32[32,8,256]{2,1,0:T(8,128)S(1)} all-to-all(f32[32,8,256]{2,1,0:T(8,128)S(1)} %bitcast.15), channel_id=1, replica_groups=mesh['zh'=8,'zp'=2,'brick'=32] {'brick'}, dimensions={0} | all-to-all | bytes 524288 | tf_op jit(solution)/shard_map/all_to_all | solution.py:373
  138.9 19.4 %all_to_all.21.pieces = f32[16,8,256]{2,1,0:T(8,128)S(1)} all-to-all(f32[16,8,256]{2,1,0:T(8,128)S(1)} %spread_sum.2), channel_id=1, replica_groups=mesh['zh'=8,'zp'=2,'brick'=32] {'zh','zp'}, dimensions={0} | all-to-all | bytes 262144 | tf_op jit(solution)/shard_map/all_to_all | solution.py:374
  158.4 12.9 %all_to_all.22 = f32[32,8,256]{2,1,0:T(8,128)S(1)} all-to-all(f32[32,8,256]{2,1,0:T(8,128)S(1)} %spread_sum.3), channel_id=1, replica_groups=mesh['zh'=8,'zp'=2,'brick'=32] {'brick'}, dimensions={0} | all-to-all | bytes 524288 | tf_op jit(solution)/shard_map/all_to_all | solution.py:375
  171.2 9.0 %cholesky_and_inverse.1 = (f32[256,256]{1,0:T(8,128)}, bf16[256,256]{1,0:T(8,128)(2,1)S(1)}, bf16[256,256]{1,0:T(8,128)(2,1)S(1)}) custom-call(f32[256,256]{1,0:T(8,128)S(1)} %bitcast.14), custom_call_target="tpu_custom_call" | custom-call | tf_op jit(solution)/shard_map/cholesky_and_inverse/pallas_call | solution.py:304
  180.3 15.6 %all-gather.3.cloned.1.call-done = f32[2048,256]{1,0:T(8,128)} async-done(((f32[128,256]{1,0:T(8,128)}), f32[2048,256]{1,0:T(8,128)}) %all-gather.3.cloned.1.call-update) | async-done | bytes 2097168 | tf_op jit(solution)/shard_map/all_gather | solution.py:369
  195.9 0.0 copy-start.3
  195.9 1.6 copy-done.3
  197.5 2.9 %make_basis.1 = f32[2048,256]{1,0:T(8,128)} custom-call(f32[2,4,2,128,256]{4,3,2,1,0:T(8,128)S(1)} %bitcast.11, bf16[256,256]{1,0:T(8,128)(2,1)S(1)} %get-tuple-element.19.high, bf16[256,256]{1,0:T(8,128)(2,1)S(1)} %get-tuple-element.20.low), custom_call_target="tpu_custom_call" | custom-call | tf_op jit(solution)/shard_map/make_basis/pallas_call | solution.py:326
  (2 shorter events, 0.1 us)
Async XLA Ops:
  7.2 16.3 %collective-permute-start = (bf16[2048,256]{1,0:T(8,128)(2,1)}, bf16[2048,256]{1,0:T(8,128)(2,1)S(1)}, u32[]{:S(2)}, u32[]{:S(2)}) collective-permute-start(bf16[2048,256]{1,0:T(8,128)(2,1)} %probes.1), channel_id=1, source_target_pairs={{0,1},{1,2},{2,3},{3,4},{4,5},{5,6},{6,7},{7,8},{8,9},{9,10},{10,1... | collective-permute-start | bytes 3145736 | tf_op jit(solution)/shard_map/ppermute | solution.py:344
  9.1 16.3 %collective-permute-start.1 = (bf16[2048,256]{1,0:T(8,128)(2,1)}, bf16[2048,256]{1,0:T(8,128)(2,1)S(1)}, u32[]{:S(2)}, u32[]{:S(2)}) collective-permute-start(bf16[2048,256]{1,0:T(8,128)(2,1)} %probes.1), channel_id=1, source_target_pairs={{1,0},{2,1},{3,2},{4,3},{5,4},{6,5},{7,6},{8,7},{9,8},{10,9},{11,1... | collective-permute-start | bytes 3145736 | tf_op jit(solution)/shard_map/ppermute | solution.py:344
  25.4 1.0 copy-start.4
  26.3 1.2 copy-start
  27.6 1.9 copy-start.2
  29.4 1.2 copy-start.5
  40.4 16.3 %collective-permute-start.2 = (bf16[16,256,128]{2,1,0:T(8,128)(2,1)}, bf16[16,256,128]{2,1,0:T(8,128)(2,1)S(1)}, u32[]{:S(2)}, u32[]{:S(2)}) collective-permute-start(bf16[16,256,128]{2,1,0:T(8,128)(2,1)} %get-tuple-element.13), channel_id=1, source_target_pairs={{1,0},{2,1},{3,2},{4,3},{5,4},{6,5},{7,6},{8,7},{9,8},{10,9},{11,1... | collective-permute-start | bytes 3145736 | tf_op jit(solution)/shard_map/ppermute | solution.py:344
  44.1 16.4 %collective-permute-start.3 = (bf16[16,256,128]{2,1,0:T(8,128)(2,1)}, bf16[16,256,128]{2,1,0:T(8,128)(2,1)}, u32[]{:S(2)}, u32[]{:S(2)}) collective-permute-start(bf16[16,256,128]{2,1,0:T(8,128)(2,1)} %get-tuple-element.14), channel_id=1, source_target_pairs={{0,1},{1,2},{2,3},{3,4},{4,5},{5,6},{6,7},{7,8},{8,9},{9,10},{10,1... | collective-permute-start | bytes 3145736 | tf_op jit(solution)/shard_map/ppermute | solution.py:344
  62.0 58.0 %copy-start.1 = (bf16[2048,256]{1,0:T(8,128)(2,1)S(1)}, bf16[2048,256]{1,0:T(8,128)(2,1)}, u32[]{:S(2)}) copy-start(bf16[2048,256]{1,0:T(8,128)(2,1)} %probes.1) | copy-start | bytes 3145732
  62.1 14.5 %collective-permute-start.4 = (bf16[4,256,128]{2,1,0:T(8,128)(2,1)S(1)}, bf16[4,256,128]{2,1,0:T(8,128)(2,1)S(1)}, u32[]{:S(2)}, u32[]{:S(2)}) collective-permute-start(bf16[4,256,128]{2,1,0:T(8,128)(2,1)S(1)} %get-tuple-element.16), channel_id=1, source_target_pairs={{0,32},{32,0},{64,96},{96,64},{128,160},{160,128},{192,224},{224,1... | collective-permute-start | bytes 786440 | tf_op jit(solution)/shard_map/ppermute | solution.py:364
  66.0 15.5 %collective-permute-start.5 = (bf16[4,256,128]{2,1,0:T(8,128)(2,1)S(1)}, bf16[4,256,128]{2,1,0:T(8,128)(2,1)S(1)}, u32[]{:S(2)}, u32[]{:S(2)}) collective-permute-start(bf16[4,256,128]{2,1,0:T(8,128)(2,1)S(1)} %get-tuple-element.18), channel_id=1, source_target_pairs={{0,480},{32,64},{64,32},{96,128},{128,96},{160,192},{192,160},{224... | collective-permute-start | bytes 786440 | tf_op jit(solution)/shard_map/ppermute | solution.py:365
  82.4 37.6 %all-to-all-start = ((bf16[8,256,128]{2,1,0:T(8,128)(2,1)}), bf16[8,256,128]{2,1,0:T(8,128)(2,1)S(1)}, u32[]{:S(2)}, u32[]{:S(2)}) async-start(bf16[8,256,128]{2,1,0:T(8,128)(2,1)} %add_pairs.1), calls=%async_computation | async-start | bytes 1048576 | tf_op jit(solution)/shard_map/all_to_all | solution.py:366
  91.0 104.9 %all-gather.3.cloned.1.call-start = ((), (), s32[]{:S(2)}) async-start(), calls=%async_computation.4 | async-start | bytes 2228224 | tf_op jit(solution)/shard_map/all_gather | solution.py:369
  195.9 1.6 copy-start.3
Sparse Core Ops, SparseCore 0:
  121.1 74.7 all-gather.2

commit v3 on v2

--- a/solution.py
+++ b/solution.py
@@ -13,6 +13,7 @@
 BF16 = jnp.bfloat16
 PANEL = 64
 MIB = 1024 * 1024
+AHEAD = 4
 DEPTH = ("zh", "zp")
 
 
@@ -30,84 +31,136 @@
     return pltpu.CompilerParams(vmem_limit_bytes=mib * MIB)
 
 
-def operator_kernel(cols, w_hbm, low_ref, own_ref, high_ref, o_own, o_below, o_above, w_ref, s_below, s_above, sems):
-    blocks = own_ref.shape[0]
-
-    def fetch(r):
-        return pltpu.make_async_copy(w_hbm.at[r], w_ref.at[r], sems.at[r])
-
-    for r in range(blocks):
-        fetch(r).start()
-    s_below[...] = jnp.zeros_like(s_below)
-    s_above[...] = jnp.zeros_like(s_above)
-
-    def step(r, carry):
+def operator_kernel(
+    cols, odd, w_hbm, far_hbm, own_hbm, near_hbm, own_out, far_out, near_out,
+    w_ref, p_ref, s_own, s_far, s_near, h_far, h_near, d_ref, in_sems, out_sems,
+):
+    blocks = p_ref.shape[0]
+    dot = functools.partial(jnp.dot, preferred_element_type=F32)
+
+    def places(r):
         ids = [cols[3 * r + j] for j in range(3)]
         at_low = jnp.where(ids[0] < blocks, 0, jnp.where(ids[1] < blocks, 1, 2))
         at_high = jnp.where(ids[0] >= 2 * blocks, 0, jnp.where(ids[1] >= 2 * blocks, 1, 2))
         at_own = 3 - at_low - at_high
-        c_low = cols[3 * r + at_low]
-        c_high = cols[3 * r + at_high] - 2 * blocks
-        fetch(r).wait()
-        w_low, w_own, w_high = w_ref[r, at_low], w_ref[r, at_own], w_ref[r, at_high]
-        dot = functools.partial(jnp.dot, preferred_element_type=F32)
-        data = dot(w_low, low_ref[c_low]) + dot(w_own, own_ref[r]) + dot(w_high, high_ref[c_high])
-        data = data.T.astype(BF16)
-        term = dot(data, w_own)
-        o_own[2 * r] = term[:, :128]
-        o_own[2 * r + 1] = term[:, 128:]
-        s_below[c_low] += dot(data, w_low)
-        s_above[c_high] += dot(data, w_high)
+        low, high = cols[3 * r + at_low], cols[3 * r + at_high] - 2 * blocks
+        first = odd[0] == 0
+        at = (jnp.where(first, at_low, at_high), at_own, jnp.where(first, at_high, at_low))
+        return at, jnp.where(first, low, high), jnp.where(first, high, low)
+
+    def fetch(r):
+        at, far, near = places(r)
+        sources = ((far_hbm, far), (own_hbm, r), (near_hbm, near))
+        return [
+            pltpu.make_async_copy(w_hbm.at[r, at[j]], w_ref.at[r, j], in_sems.at[r, j])
+            for j in range(3)
+        ] + [
+            pltpu.make_async_copy(source.at[q], p_ref.at[r, j], in_sems.at[r, 3 + j])
+            for j, (source, q) in enumerate(sources)
+        ]
+
+    def weights_of(r):
+        return jnp.concatenate([w_ref[r, j] for j in range(3)], axis=1)
+
+    def data_of(r):
+        probes = jnp.concatenate([p_ref[r, j] for j in range(3)], axis=0)
+        return dot(weights_of(r), probes).astype(BF16).T
+
+    def own_copy(r):
+        return pltpu.make_async_copy(s_own.at[r], own_out.at[r], out_sems.at[r])
+
+    def put(r, terms):
+        _, far, near = places(r)
+        bs = terms.shape[1] // 3
+        s_own[r, 0] = terms[:, bs : bs + 128]
+        s_own[r, 1] = terms[:, bs + 128 : 2 * bs]
+        own_copy(r).start()
+        s_far[far] += terms[:, :bs]
+        s_near[near] += terms[:, 2 * bs :]
+
+    for r in range(AHEAD):
+        for copy in fetch(r):
+            copy.start()
+    s_far[...] = jnp.zeros_like(s_far)
+    s_near[...] = jnp.zeros_like(s_near)
+    for copy in fetch(0):
+        copy.wait()
+    d_ref[0] = data_of(0)
+
+    def step(r, carry):
+        @pl.when(r + AHEAD < blocks)
+        def _():
+            for copy in fetch(r + AHEAD):
+                copy.start()
+
+        for copy in fetch(r + 1):
+            copy.wait()
+        terms = dot(d_ref[r % 2], weights_of(r))
+        d_ref[(r + 1) % 2] = data_of(r + 1)
+        put(r, terms)
         return carry
 
-    lax.fori_loop(0, blocks, step, 0)
-    for q in range(blocks):
-        for field, out in ((s_below, o_below), (s_above, o_above)):
-            out[2 * q] = field[q, :, :128].astype(BF16)
-            out[2 * q + 1] = field[q, :, 128:].astype(BF16)
-
-
-def apply_operator(cols, weights, low, own, high):
+    lax.fori_loop(0, blocks - 1, step, 0)
+    put(blocks - 1, dot(d_ref[(blocks - 1) % 2], weights_of(blocks - 1)))
+    last = []
+    for k, (field, half, out) in enumerate(((s_far, h_far, far_out), (s_near, h_near, near_out))):
+        for q in range(blocks):
+            half[2 * q] = field[q, :, :128].astype(BF16)
+            half[2 * q + 1] = field[q, :, 128:].astype(BF16)
+            pair = pl.ds(2 * q, 2)
+            copy = pltpu.make_async_copy(half.at[pair], out.at[pair], out_sems.at[(k + 1) * blocks + q])
+            copy.start()
+            last.append(copy)
+    for r in range(blocks):
+        own_copy(r).wait()
+    for copy in last:
+        copy.wait()
+
+
+def apply_operator(cols, odd, weights, far, own, near):
     blocks, slots, bs, _ = weights.shape
     width = own.shape[-1]
     shape = (2 * blocks, width, bs // 2)
+    smem, hbm = pl.BlockSpec(memory_space=pltpu.SMEM), pl.BlockSpec(memory_space=pl.ANY)
     field = pltpu.VMEM((blocks, width, bs), F32)
-    return pl.pallas_call(
+    half = pltpu.VMEM(shape, BF16)
+    own_field, far_field, near_field = pl.pallas_call(
         operator_kernel,
-        in_specs=[
-            pl.BlockSpec(memory_space=pltpu.SMEM),
-            pl.BlockSpec(memory_space=pltpu.HBM),
-            in_vmem(),
-            in_vmem(),
-            in_vmem(),
-        ],
-        out_specs=[in_vmem()] * 3,
+        in_specs=[smem, smem] + [hbm] * 4,
+        out_specs=[hbm] * 3,
         out_shape=(
-            jax.ShapeDtypeStruct(shape, F32),
+            jax.ShapeDtypeStruct((blocks, 2, width, bs // 2), F32),
             jax.ShapeDtypeStruct(shape, BF16),
             jax.ShapeDtypeStruct(shape, BF16),
         ),
         scratch_shapes=[
             pltpu.VMEM(weights.shape, BF16),
+            pltpu.VMEM((blocks, 3, bs, width), BF16),
+            pltpu.VMEM((blocks, 2, width, bs // 2), F32),
             field,
             field,
-            pltpu.SemaphoreType.DMA((blocks,)),
+            half,
+            half,
+            pltpu.VMEM((2, width, bs), BF16),
+            pltpu.SemaphoreType.DMA((blocks, 6)),
+            pltpu.SemaphoreType.DMA((3 * blocks,)),
         ],
-        compiler_params=params(24),
+        compiler_params=params(60),
         name="normal_operator",
-    )(cols, weights, low, own, high)
-
-
-def halves_kernel(odd, own, above, below, keep_a, send_a, keep_b, send_b):
+    )(cols, odd, weights, far, own, near)
+    return own_field.reshape(shape), far_field, near_field
+
+
+def halves_kernel(odd, own, far, near, keep_a, send_a, keep_b, send_b):
     part = keep_a.shape[0]
     o = odd[0]
     for out, first in ((keep_a, o), (send_a, 1 - o), (keep_b, 2 + o), (send_b, 3 - o)):
         for i in range(part):
             p = part * first + i
-            out[i] = (own[p] + (above[p].astype(F32) + below[p].astype(F32))).astype(out.dtype)
-
-
-def split_halves(odd, own, above, below):
+            out[i] = (own[p] + (far[p].astype(F32) + near[p].astype(F32))).astype(out.dtype)
+
+
+def split_halves(odd, own, far, near):
     pieces, width, cells = own.shape
     kept, sent = (jax.ShapeDtypeStruct((pieces // 4, width, cells), t) for t in (F32, BF16))
     return pl.pallas_call(
@@ -117,7 +170,7 @@
         out_shape=(kept, sent, kept, sent),
         compiler_params=params(12),
         name="split_halves",
-    )(odd, own, above, below)
+    )(odd, own, far, near)
 
 
 def pairs_kernel(ka, ra, kb, rb, out):
@@ -333,33 +386,33 @@
         ],
         out_specs=pl.BlockSpec((4 * rows, width), lambda h, o: (2 * h + o, 0)),
         out_shape=jax.ShapeDtypeStruct((16 * rows, width), F32),
-        compiler_params=params(16),
+        compiler_params=params(60),
         name="make_basis",
     )(view, high, low)
 
 
-def shifted(value, axis, steps):
-    count = lax.axis_size(axis)
-    leading, last = (max(0, -steps), min(count, count - steps))
-    return lax.ppermute(value, axis, [(source, source + steps) for source in range(leading, last)])
+def paired(value, axis, first):
+    pairs = [(i, i + 1) for i in range(first, lax.axis_size(axis) - 1, 2)]
+    return lax.ppermute(value, axis, pairs + [(j, i) for i, j in pairs])
 
 
 def body(probes, weights, columns):
     rows, width = probes.shape
     w_local = weights[0]
     blocks, _, bs, _ = w_local.shape
-    lower = shifted(probes, "brick", 1)
-    higher = shifted(probes, "brick", -1)
+    far = paired(probes, "brick", 1)
+    near = paired(probes, "brick", 0)
     shape = (blocks, bs, width)
-    own, below, above = apply_operator(
-        columns.reshape(-1), w_local, lower.reshape(shape), probes.reshape(shape), higher.reshape(shape)
+    core = jnp.full((1,), lax.axis_index("brick") % 2, jnp.int32)
+    own, to_far, to_near = apply_operator(
+        columns.reshape(-1), core, w_local, far.reshape(shape), probes.reshape(shape), near.reshape(shape)
     )
-    from_above = shifted(below, "brick", -1)
-    from_below = shifted(above, "brick", 1)
+    from_far = paired(to_far, "brick", 1)
+    from_near = paired(to_near, "brick", 0)
 
     zh, zp = lax.axis_index("zh"), lax.axis_index("zp")
     odd = jnp.full((1,), zp, jnp.int32)
-    keep_a, send_a, keep_b, send_b = split_halves(odd, own, from_above, from_below)
+    keep_a, send_a, keep_b, send_b = split_halves(odd, own, from_far, from_near)
     n = lax.axis_size("zh") * lax.axis_size("zp")
     got_a = lax.ppermute(send_a, DEPTH, [(i, i ^ 1) for i in range(n)])
     got_b = lax.ppermute(send_b, DEPTH, [(i, (((i + 1) ^ 1) - 1) % n) for i in range(n)])

time: 208 us -> 196 us (0.942)
  waiting for transfers between devices: 75.9 us -> 72 us
  blocking collectives: 48.9 us -> 45.2 us
  local copies, waits for them, and re-layouts: 7.74 us -> 5.56 us
    ppermute x4, waiting for transfers between devices: 26.3 us -> 21 us  [paired(): return lax.ppermute(value, axis, pairs + [(j, i) for i, j in pairs])]
    all_to_all x1, blocking collectives: 16.6 us -> 13.2 us  [body(): lax.all_to_all(gram.reshape(bricks, width // bricks, width), 'brick', 0, 0)]
    unnamed x13, local copies, waits for them, and re-layouts: 7.66 us -> 4.97 us
  transfers between devices with their start and end apart: 8 -> 8, of which waited for: 7 -> 5; matrix products, arithmetic and copies ran while one was open for 0% -> 1% of each run, Pallas kernels for 5% -> 5%
where the time goes in v3:
time: 196 us; the launch traced here: 195 us
  waiting for transfers between devices  72 us (37%)
  blocking collectives  45.2 us (23%)
  starting transfers between devices  33.3 us (17%)
  Pallas kernels  24.7 us (13%)
  between operations  14.2 us (7%)
  local copies, waits for them, and re-layouts  5.56 us (3%)
    all_to_all x1, waiting for transfers between devices, body(): pieces = lax.all_to_all(add_pairs(keep_a, got_a, keep_b, got_b), 'zh', 0, 0)  30.3 us
    ppermute x4, waiting for transfers between devices, paired(): return lax.ppermute(value, axis, pairs + [(j, i) for i, j in pairs])  21 us
    all_to_all x1, blocking collectives, body(): share = lax.all_to_all(spread_sum(share, n), DEPTH, 0, 0)  19.2 us
    all_gather x1, waiting for transfers between devices, body(): whole_image = lax.all_gather(image, DEPTH)  14.4 us
    all_to_all x1, blocking collectives, body(): lax.all_to_all(gram.reshape(bricks, width // bricks, width), 'brick', 0, 0)  13.2 us
    all_to_all x1, blocking collectives, body(): lax.all_to_all(spread_sum(share, bricks), 'brick', 0, 0)  12.9 us
    ppermute x1, starting transfers between devices, body(): lax.ppermute(send_b, DEPTH, [(i, ((i + 1 ^ 1) - 1) % n) for i in range(n)])  10.6 us
    ppermute x4, starting transfers between devices, paired(): return lax.ppermute(value, axis, pairs + [(j, i) for i, j in pairs])  10.3 us
  transfers between devices with their start and end apart: 8, of which 5 were waited for; matrix products, arithmetic and copies ran while one was open for 1% of the time, Pallas kernels for 5%

profile of v3, /device:TPU:12, one launch (start us, length us, event | category | flops | bytes accessed | tf_op | source)
XLA Modules:
  0.0 195.0 jit_solution(4044435798177211392)
XLA Ops:
  7.2 1.9 collective-permute-start
  9.1 3.2 %collective-permute-start.1 = (bf16[2048,256]{1,0:T(8,128)(2,1)}, bf16[2048,256]{1,0:T(8,128)(2,1)S(1)}, u32[]{:S(2)}, u32[]{:S(2)}) collective-permute-start(bf16[2048,256]{1,0:T(8,128)(2,1)} %probes.1), channel_id=1, source_target_pairs={{0,1},{2,3},{4,5},{6,7},{8,9},{10,11},{12,13},{14,15},{16,17},{18,... | collective-permute-start | bytes 3145736 | tf_op jit(solution)/shard_map/ppermute | solution.py:396
  12.3 0.8 copy.6
  13.1 0.6 reshape.28.cols
  13.7 9.8 %collective-permute-done = bf16[2048,256]{1,0:T(8,128)(2,1)S(1)} collective-permute-done((bf16[2048,256]{1,0:T(8,128)(2,1)}, bf16[2048,256]{1,0:T(8,128)(2,1)S(1)}, u32[]{:S(2)}, u32[]{:S(2)}) %collective-permute-start) | collective-permute-done | bytes 1048608 | tf_op jit(solution)/shard_map/ppermute | solution.py:396
  23.5 0.0 copy-start.4
  23.5 0.0 collective-permute-done.1
  23.5 0.0 copy-start.5
  23.5 1.0 copy-done.4
  24.5 0.4 copy-done.5
  24.8 7.7 %normal_operator.1 = (f32[8,2,256,128]{3,2,1,0:T(8,128)}, bf16[16,256,128]{2,1,0:T(8,128)(2,1)}, bf16[16,256,128]{2,1,0:T(8,128)(2,1)}) custom-call(s32[24]{0:T(128)} %reshape.28.cols, s32[1]{0:T(128)} %bitcast.2.odd, bf16[8,3,256,256]{3,2,1,0:T(8,128)(2,1)} %bitcast.15, bf16[8,256,256]{2,1,0:T(8,128)(2,1)} %bitcast.17, bf16[8,256,256]{2,1,0:T(8,128)(2,1)} %bitcast.11, ...), custom_call_target="tpu_custom_call" | custom-call | tf_op jit(solution)/shard_map/normal_operator/pallas_call | solution.py:127
  32.6 2.2 %collective-permute-start.2 = (bf16[16,256,128]{2,1,0:T(8,128)(2,1)}, bf16[16,256,128]{2,1,0:T(8,128)(2,1)S(1)}, u32[]{:S(2)}, u32[]{:S(2)}) collective-permute-start(bf16[16,256,128]{2,1,0:T(8,128)(2,1)} %get-tuple-element.13), channel_id=1, source_target_pairs={{1,2},{3,4},{5,6},{7,8},{9,10},{11,12},{13,14},{15,16},{17,18},{19... | collective-permute-start | bytes 3145736 | tf_op jit(solution)/shard_map/ppermute | solution.py:396
  34.7 3.0 %collective-permute-start.3 = (bf16[16,256,128]{2,1,0:T(8,128)(2,1)}, bf16[16,256,128]{2,1,0:T(8,128)(2,1)S(1)}, u32[]{:S(2)}, u32[]{:S(2)}) collective-permute-start(bf16[16,256,128]{2,1,0:T(8,128)(2,1)} %get-tuple-element.14), channel_id=1, source_target_pairs={{0,1},{2,3},{4,5},{6,7},{8,9},{10,11},{12,13},{14,15},{16,17},{18,... | collective-permute-start | bytes 3145736 | tf_op jit(solution)/shard_map/ppermute | solution.py:396
  37.7 11.2 %collective-permute-done.2.far = bf16[16,256,128]{2,1,0:T(8,128)(2,1)S(1)} collective-permute-done((bf16[16,256,128]{2,1,0:T(8,128)(2,1)}, bf16[16,256,128]{2,1,0:T(8,128)(2,1)S(1)}, u32[]{:S(2)}, u32[]{:S(2)}) %collective-permute-start.2) | collective-permute-done | bytes 1048608 | tf_op jit(solution)/shard_map/ppermute | solution.py:396
  48.9 0.0 collective-permute-done.3.near
  48.9 0.0 copy-start.1
  48.9 1.6 copy-done.1
  50.5 0.3 split_halves.1
  50.8 0.0 copy-start
  50.8 4.0 %collective-permute-start.4 = (bf16[4,256,128]{2,1,0:T(8,128)(2,1)S(1)}, bf16[4,256,128]{2,1,0:T(8,128)(2,1)S(1)}, u32[]{:S(2)}, u32[]{:S(2)}) collective-permute-start(bf16[4,256,128]{2,1,0:T(8,128)(2,1)S(1)} %get-tuple-element.16), channel_id=1, source_target_pairs={{0,32},{32,0},{64,96},{96,64},{128,160},{160,128},{192,224},{224,1... | collective-permute-start | bytes 786440 | tf_op jit(solution)/shard_map/ppermute | solution.py:417
  54.8 10.6 %collective-permute-start.5 = (bf16[4,256,128]{2,1,0:T(8,128)(2,1)S(1)}, bf16[4,256,128]{2,1,0:T(8,128)(2,1)S(1)}, u32[]{:S(2)}, u32[]{:S(2)}) collective-permute-start(bf16[4,256,128]{2,1,0:T(8,128)(2,1)S(1)} %get-tuple-element.18), channel_id=1, source_target_pairs={{0,480},{32,64},{64,32},{96,128},{128,96},{160,192},{192,160},{224... | collective-permute-start | bytes 786440 | tf_op jit(solution)/shard_map/ppermute | solution.py:418
  65.3 0.0 collective-permute-done.4.ra
  65.3 6.3 %collective-permute-done.5.rb = bf16[4,256,128]{2,1,0:T(8,128)(2,1)S(1)} collective-permute-done((bf16[4,256,128]{2,1,0:T(8,128)(2,1)S(1)}, bf16[4,256,128]{2,1,0:T(8,128)(2,1)S(1)}, u32[]{:S(2)}, u32[]{:S(2)}) %collective-permute-start.5) | collective-permute-done | bytes 262176 | tf_op jit(solution)/shard_map/ppermute | solution.py:418
  71.6 0.9 add_pairs.1
  72.5 8.5 %all-to-all-start = ((bf16[8,256,128]{2,1,0:T(8,128)(2,1)}), bf16[8,256,128]{2,1,0:T(8,128)(2,1)S(1)}, u32[]{:S(2)}, u32[]{:S(2)}) async-start(bf16[8,256,128]{2,1,0:T(8,128)(2,1)} %add_pairs.1), calls=%async_computation | async-start | bytes 1048576 | tf_op jit(solution)/shard_map/all_to_all | solution.py:419
  81.0 0.0 all-gather.3.cloned.1.call-start
  81.1 30.3 %all-to-all-done.pieces = bf16[8,256,128]{2,1,0:T(8,128)(2,1)S(1)} async-done(((bf16[8,256,128]{2,1,0:T(8,128)(2,1)}), bf16[8,256,128]{2,1,0:T(8,128)(2,1)S(1)}, u32[]{:S(2)}, u32[]{:S(2)}) %all-to-all-start) | async-done | bytes 524320 | tf_op jit(solution)/shard_map/all_to_all | solution.py:419
  111.4 0.0 copy-done
  111.4 0.9 make_image.1.image
  112.3 0.0 all-gather.3.cloned.1.call-update
  112.4 1.3 make_gram.1
  113.7 13.2 %all_to_all.20.pieces = f32[32,8,256]{2,1,0:T(8,128)S(1)} all-to-all(f32[32,8,256]{2,1,0:T(8,128)S(1)} %bitcast.14), channel_id=1, replica_groups=mesh['zh'=8,'zp'=2,'brick'=32] {'brick'}, dimensions={0} | all-to-all | bytes 524288 | tf_op jit(solution)/shard_map/all_to_all | solution.py:426
  126.9 19.2 %all_to_all.21.pieces = f32[16,8,256]{2,1,0:T(8,128)S(1)} all-to-all(f32[16,8,256]{2,1,0:T(8,128)S(1)} %spread_sum.2), channel_id=1, replica_groups=mesh['zh'=8,'zp'=2,'brick'=32] {'zh','zp'}, dimensions={0} | all-to-all | bytes 262144 | tf_op jit(solution)/shard_map/all_to_all | solution.py:427
  146.1 12.9 %all_to_all.22 = f32[32,8,256]{2,1,0:T(8,128)S(1)} all-to-all(f32[32,8,256]{2,1,0:T(8,128)S(1)} %spread_sum.3), channel_id=1, replica_groups=mesh['zh'=8,'zp'=2,'brick'=32] {'brick'}, dimensions={0} | all-to-all | bytes 524288 | tf_op jit(solution)/shard_map/all_to_all | solution.py:428
  159.0 9.0 %cholesky_and_inverse.1 = (f32[256,256]{1,0:T(8,128)}, bf16[256,256]{1,0:T(8,128)(2,1)S(1)}, bf16[256,256]{1,0:T(8,128)(2,1)S(1)}) custom-call(f32[256,256]{1,0:T(8,128)S(1)} %bitcast.13), custom_call_target="tpu_custom_call" | custom-call | tf_op jit(solution)/shard_map/cholesky_and_inverse/pallas_call | solution.py:357
  168.0 0.0 copy-start.2
  168.0 0.6 copy-done.2
  168.6 0.0 copy-start.3
  168.6 0.6 copy-done.3
  169.3 14.4 %all-gather.3.cloned.1.call-done = f32[2048,256]{1,0:T(8,128)} async-done(((f32[128,256]{1,0:T(8,128)}), f32[2048,256]{1,0:T(8,128)}) %all-gather.3.cloned.1.call-update) | async-done | bytes 2097168 | tf_op jit(solution)/shard_map/all_gather | solution.py:422
  183.6 4.5 %make_basis.1 = f32[2048,256]{1,0:T(8,128)} custom-call(f32[2,4,2,128,256]{4,3,2,1,0:T(8,128)} %bitcast.16, bf16[256,256]{1,0:T(8,128)(2,1)} %copy-done.2, bf16[256,256]{1,0:T(8,128)(2,1)} %copy-done.3), custom_call_target="tpu_custom_call" | custom-call | tf_op jit(solution)/shard_map/make_basis/pallas_call | solution.py:379
  (2 shorter events, 0.1 us)
Async XLA Ops:
  7.2 16.3 %collective-permute-start = (bf16[2048,256]{1,0:T(8,128)(2,1)}, bf16[2048,256]{1,0:T(8,128)(2,1)S(1)}, u32[]{:S(2)}, u32[]{:S(2)}) collective-permute-start(bf16[2048,256]{1,0:T(8,128)(2,1)} %probes.1), channel_id=1, source_target_pairs={{1,2},{3,4},{5,6},{7,8},{9,10},{11,12},{13,14},{15,16},{17,18},{19... | collective-permute-start | bytes 3145736 | tf_op jit(solution)/shard_map/ppermute | solution.py:396
  9.1 14.4 %collective-permute-start.1 = (bf16[2048,256]{1,0:T(8,128)(2,1)}, bf16[2048,256]{1,0:T(8,128)(2,1)S(1)}, u32[]{:S(2)}, u32[]{:S(2)}) collective-permute-start(bf16[2048,256]{1,0:T(8,128)(2,1)} %probes.1), channel_id=1, source_target_pairs={{0,1},{2,3},{4,5},{6,7},{8,9},{10,11},{12,13},{14,15},{16,17},{18,... | collective-permute-start | bytes 3145736 | tf_op jit(solution)/shard_map/ppermute | solution.py:396
  23.5 1.0 copy-start.4
  23.5 1.3 copy-start.5
  32.6 16.3 %collective-permute-start.2 = (bf16[16,256,128]{2,1,0:T(8,128)(2,1)}, bf16[16,256,128]{2,1,0:T(8,128)(2,1)S(1)}, u32[]{:S(2)}, u32[]{:S(2)}) collective-permute-start(bf16[16,256,128]{2,1,0:T(8,128)(2,1)} %get-tuple-element.13), channel_id=1, source_target_pairs={{1,2},{3,4},{5,6},{7,8},{9,10},{11,12},{13,14},{15,16},{17,18},{19... | collective-permute-start | bytes 3145736 | tf_op jit(solution)/shard_map/ppermute | solution.py:396
  34.7 14.2 %collective-permute-start.3 = (bf16[16,256,128]{2,1,0:T(8,128)(2,1)}, bf16[16,256,128]{2,1,0:T(8,128)(2,1)S(1)}, u32[]{:S(2)}, u32[]{:S(2)}) collective-permute-start(bf16[16,256,128]{2,1,0:T(8,128)(2,1)} %get-tuple-element.14), channel_id=1, source_target_pairs={{0,1},{2,3},{4,5},{6,7},{8,9},{10,11},{12,13},{14,15},{16,17},{18,... | collective-permute-start | bytes 3145736 | tf_op jit(solution)/shard_map/ppermute | solution.py:396
  48.9 1.6 copy-start.1
  50.8 60.6 %copy-start = (bf16[2048,256]{1,0:T(8,128)(2,1)S(1)}, bf16[2048,256]{1,0:T(8,128)(2,1)}, u32[]{:S(2)}) copy-start(bf16[2048,256]{1,0:T(8,128)(2,1)} %probes.1) | copy-start | bytes 3145732
  50.8 14.5 %collective-permute-start.4 = (bf16[4,256,128]{2,1,0:T(8,128)(2,1)S(1)}, bf16[4,256,128]{2,1,0:T(8,128)(2,1)S(1)}, u32[]{:S(2)}, u32[]{:S(2)}) collective-permute-start(bf16[4,256,128]{2,1,0:T(8,128)(2,1)S(1)} %get-tuple-element.16), channel_id=1, source_target_pairs={{0,32},{32,0},{64,96},{96,64},{128,160},{160,128},{192,224},{224,1... | collective-permute-start | bytes 786440 | tf_op jit(solution)/shard_map/ppermute | solution.py:417
  54.8 16.9 %collective-permute-start.5 = (bf16[4,256,128]{2,1,0:T(8,128)(2,1)S(1)}, bf16[4,256,128]{2,1,0:T(8,128)(2,1)S(1)}, u32[]{:S(2)}, u32[]{:S(2)}) collective-permute-start(bf16[4,256,128]{2,1,0:T(8,128)(2,1)S(1)} %get-tuple-element.18), channel_id=1, source_target_pairs={{0,480},{32,64},{64,32},{96,128},{128,96},{160,192},{192,160},{224... | collective-permute-start | bytes 786440 | tf_op jit(solution)/shard_map/ppermute | solution.py:418
  72.5 38.9 %all-to-all-start = ((bf16[8,256,128]{2,1,0:T(8,128)(2,1)}), bf16[8,256,128]{2,1,0:T(8,128)(2,1)S(1)}, u32[]{:S(2)}, u32[]{:S(2)}) async-start(bf16[8,256,128]{2,1,0:T(8,128)(2,1)} %add_pairs.1), calls=%async_computation | async-start | bytes 1048576 | tf_op jit(solution)/shard_map/all_to_all | solution.py:419
  81.0 102.6 %all-gather.3.cloned.1.call-start = ((), (), s32[]{:S(2)}) async-start(), calls=%async_computation.4 | async-start | bytes 2228224 | tf_op jit(solution)/shard_map/all_gather | solution.py:422
  168.0 0.6 copy-start.2
  168.6 0.6 copy-start.3
Sparse Core Ops, SparseCore 0:
  112.5 71.0 all-gather.2

commit v4 on v2

--- a/solution.py
+++ b/solution.py
@@ -30,118 +30,147 @@
     return pltpu.CompilerParams(vmem_limit_bytes=mib * MIB)
 
 
-def operator_kernel(cols, w_hbm, low_ref, own_ref, high_ref, o_own, o_below, o_above, w_ref, s_below, s_above, sems):
+def places(cols, r, blocks):
+    ids = [cols[3 * r + j] for j in range(3)]
+    at_low = jnp.where(ids[0] < blocks, 0, jnp.where(ids[1] < blocks, 1, 2))
+    at_high = jnp.where(ids[0] >= 2 * blocks, 0, jnp.where(ids[1] >= 2 * blocks, 1, 2))
+    at_own = 3 - at_low - at_high
+    low, high = cols[3 * r + at_low], cols[3 * r + at_high] - 2 * blocks
+    first = lax.axis_index("brick") % 2 == 0
+    at = (jnp.where(first, at_low, at_high), at_own, jnp.where(first, at_high, at_low))
+    return at, jnp.where(first, low, high), jnp.where(first, high, low)
+
+
+def own_kernel(cols, w_ref, own_ref, w_out, data_out):
     blocks = own_ref.shape[0]
 
-    def fetch(r):
-        return pltpu.make_async_copy(w_hbm.at[r], w_ref.at[r], sems.at[r])
-
-    for r in range(blocks):
-        fetch(r).start()
-    s_below[...] = jnp.zeros_like(s_below)
-    s_above[...] = jnp.zeros_like(s_above)
-
     def step(r, carry):
-        ids = [cols[3 * r + j] for j in range(3)]
-        at_low = jnp.where(ids[0] < blocks, 0, jnp.where(ids[1] < blocks, 1, 2))
-        at_high = jnp.where(ids[0] >= 2 * blocks, 0, jnp.where(ids[1] >= 2 * blocks, 1, 2))
-        at_own = 3 - at_low - at_high
-        c_low = cols[3 * r + at_low]
-        c_high = cols[3 * r + at_high] - 2 * blocks
-        fetch(r).wait()
-        w_low, w_own, w_high = w_ref[r, at_low], w_ref[r, at_own], w_ref[r, at_high]
-        dot = functools.partial(jnp.dot, preferred_element_type=F32)
-        data = dot(w_low, low_ref[c_low]) + dot(w_own, own_ref[r]) + dot(w_high, high_ref[c_high])
-        data = data.T.astype(BF16)
-        term = dot(data, w_own)
-        o_own[2 * r] = term[:, :128]
-        o_own[2 * r + 1] = term[:, 128:]
-        s_below[c_low] += dot(data, w_low)
-        s_above[c_high] += dot(data, w_high)
+        at, _, _ = places(cols, r, blocks)
+        for j in range(3):
+            w_out[r, j] = w_ref[r, at[j]]
+        data_out[r] = jnp.dot(w_ref[r, at[1]], own_ref[r], preferred_element_type=F32)
         return carry
 
     lax.fori_loop(0, blocks, step, 0)
-    for q in range(blocks):
-        for field, out in ((s_below, o_below), (s_above, o_above)):
+
+
+def start_operator(cols, weights, own):
+    blocks, slots, bs, _ = weights.shape
+    width = own.shape[-1]
+    return pl.pallas_call(
+        own_kernel,
+        in_specs=[pl.BlockSpec(memory_space=pltpu.SMEM), in_vmem(), in_vmem()],
+        out_specs=[in_vmem()] * 2,
+        out_shape=(
+            jax.ShapeDtypeStruct(weights.shape, BF16),
+            jax.ShapeDtypeStruct((blocks, bs, width), F32),
+        ),
+        compiler_params=params(14),
+        cost_estimate=pl.CostEstimate(
+            flops=2 * blocks * bs * bs * width, bytes_accessed=9 * MIB, transcendentals=0
+        ),
+        name="own_data",
+    )(cols, weights, own)
+
+
+def operator_kernel(cols, w_ref, data_ref, far_ref, near_ref, own_out, far_out, near_out, s_far, s_near, d_ref):
+    blocks, _, bs, _ = w_ref.shape
+    dot = functools.partial(jnp.dot, preferred_element_type=F32)
+    s_far[...] = jnp.zeros_like(s_far)
+    s_near[...] = jnp.zeros_like(s_near)
+
+    def data_of(r):
+        _, far, near = places(cols, r, blocks)
+        w = jnp.concatenate([w_ref[r, 0], w_ref[r, 2]], axis=1)
+        probes = jnp.concatenate([far_ref[far], near_ref[near]], axis=0)
+        return (data_ref[r] + dot(w, probes)).astype(BF16).T
+
+    def put(r):
+        _, far, near = places(cols, r, blocks)
+        w = jnp.concatenate([w_ref[r, j] for j in range(3)], axis=1)
+        terms = dot(d_ref[r % 2], w)
+        own_out[2 * r] = terms[:, bs : bs + 128]
+        own_out[2 * r + 1] = terms[:, bs + 128 : 2 * bs]
+        s_far[far] += terms[:, :bs]
+        s_near[near] += terms[:, 2 * bs :]
+
+    d_ref[0] = data_of(0)
+
+    def step(r, carry):
+        later = data_of(r + 1)
+        put(r)
+        d_ref[(r + 1) % 2] = later
+        return carry
+
+    lax.fori_loop(0, blocks - 1, step, 0)
+    put(blocks - 1)
+    for field, out in ((s_far, far_out), (s_near, near_out)):
+        for q in range(blocks):
             out[2 * q] = field[q, :, :128].astype(BF16)
             out[2 * q + 1] = field[q, :, 128:].astype(BF16)
 
 
-def apply_operator(cols, weights, low, own, high):
-    blocks, slots, bs, _ = weights.shape
-    width = own.shape[-1]
+def finish_operator(cols, weights, data, far, near):
+    blocks, _, bs, _ = weights.shape
+    width = data.shape[-1]
     shape = (2 * blocks, width, bs // 2)
     field = pltpu.VMEM((blocks, width, bs), F32)
     return pl.pallas_call(
         operator_kernel,
-        in_specs=[
-            pl.BlockSpec(memory_space=pltpu.SMEM),
-            pl.BlockSpec(memory_space=pltpu.HBM),
-            in_vmem(),
-            in_vmem(),
-            in_vmem(),
-        ],
+        in_specs=[pl.BlockSpec(memory_space=pltpu.SMEM)] + [in_vmem()] * 4,
         out_specs=[in_vmem()] * 3,
         out_shape=(
             jax.ShapeDtypeStruct(shape, F32),
             jax.ShapeDtypeStruct(shape, BF16),
             jax.ShapeDtypeStruct(shape, BF16),
         ),
-        scratch_shapes=[
-            pltpu.VMEM(weights.shape, BF16),
-            field,
-            field,
-            pltpu.SemaphoreType.DMA((blocks,)),
-        ],
-        compiler_params=params(24),
+        scratch_shapes=[field, field, pltpu.VMEM((2, width, bs), BF16)],
+        compiler_params=params(20),
         name="normal_operator",
-    )(cols, weights, low, own, high)
-
-
-def halves_kernel(odd, own, above, below, keep_a, send_a, keep_b, send_b):
-    part = keep_a.shape[0]
-    o = odd[0]
-    for out, first in ((keep_a, o), (send_a, 1 - o), (keep_b, 2 + o), (send_b, 3 - o)):
-        for i in range(part):
-            p = part * first + i
-            out[i] = (own[p] + (above[p].astype(F32) + below[p].astype(F32))).astype(out.dtype)
-
-
-def split_halves(odd, own, above, below):
+    )(cols, weights, data, far, near)
+
+
+def halves_kernel(own, far, near, keep, send):
+    odd = lax.axis_index("zp")
+    for out, parity in ((keep, odd), (send, 1 - odd)):
+        for i in range(out.shape[0]):
+            p = 2 * i + parity
+            out[i] = (own[p] + (far[p].astype(F32) + near[p].astype(F32))).astype(out.dtype)
+
+
+def split_halves(own, far, near):
     pieces, width, cells = own.shape
-    kept, sent = (jax.ShapeDtypeStruct((pieces // 4, width, cells), t) for t in (F32, BF16))
+    kept, sent = (jax.ShapeDtypeStruct((pieces // 2, width, cells), t) for t in (F32, BF16))
     return pl.pallas_call(
         halves_kernel,
-        in_specs=[pl.BlockSpec(memory_space=pltpu.SMEM)] + [in_vmem()] * 3,
-        out_specs=[in_vmem()] * 4,
-        out_shape=(kept, sent, kept, sent),
+        in_specs=[in_vmem()] * 3,
+        out_specs=[in_vmem()] * 2,
+        out_shape=(kept, sent),
         compiler_params=params(12),
         name="split_halves",
-    )(odd, own, above, below)
-
-
-def pairs_kernel(ka, ra, kb, rb, out):
-    n = ka.shape[0]
-    for i in range(n):
-        out[i] = (ka[i] + ra[i].astype(F32)).astype(BF16)
-        out[n + i] = (kb[i] + rb[i].astype(F32)).astype(BF16)
-
-
-def add_pairs(ka, ra, kb, rb):
-    n, width, cells = ka.shape
-    return pl.pallas_call(
-        pairs_kernel,
-        in_specs=[in_vmem()] * 4,
+    )(own, far, near)
+
+
+def pair_kernel(keep, got, out):
+    for i in range(out.shape[0]):
+        out[i] = (keep[i] + got[i].astype(F32)).astype(BF16)
+
+
+def add_pair(keep, got):
+    return pl.pallas_call(
+        pair_kernel,
+        in_specs=[in_vmem()] * 2,
         out_specs=in_vmem(),
-        out_shape=jax.ShapeDtypeStruct((2 * n, width, cells), BF16),
+        out_shape=jax.ShapeDtypeStruct(keep.shape, BF16),
         compiler_params=params(8),
-        name="add_pairs",
-    )(ka, ra, kb, rb)
-
-
-def image_kernel(block, pieces, probes, image, own, sem):
+        name="add_pair",
+    )(keep, got)
+
+
+def image_kernel(pieces, probes, image, own, sem):
     rows = own.shape[0]
-    copy = pltpu.make_async_copy(probes.at[pl.ds(block[0] * rows, rows)], own, sem)
+    block = 2 * lax.axis_index("zh") + lax.axis_index("zp")
+    copy = pltpu.make_async_copy(probes.at[pl.ds(block * rows, rows)], own, sem)
     copy.start()
     total = pieces[0].astype(F32)
     for k in range(1, pieces.shape[0]):
@@ -150,21 +179,17 @@
     image[...] = own[...].astype(F32) + total.T
 
 
-def make_image(block, pieces, probes):
+def make_image(pieces, probes):
     _, width, cells = pieces.shape
     return pl.pallas_call(
         image_kernel,
-        in_specs=[
-            pl.BlockSpec(memory_space=pltpu.SMEM),
-            in_vmem(),
-            pl.BlockSpec(memory_space=pltpu.HBM),
-        ],
+        in_specs=[in_vmem(), pl.BlockSpec(memory_space=pltpu.HBM)],
         out_specs=in_vmem(),
         out_shape=jax.ShapeDtypeStruct((cells, width), F32),
         scratch_shapes=[pltpu.VMEM((cells, width), BF16), pltpu.SemaphoreType.DMA],
         compiler_params=params(4),
         name="make_image",
-    )(block, pieces, probes)
+    )(pieces, probes)
 
 
 def gram_kernel(image, gram):
@@ -313,7 +338,7 @@
 
 
 def basis_kernel(image, high, low, out):
-    x = image[0, :, 0].reshape(out.shape)
+    x = image[...]
     x_high = x.astype(BF16)
     x_low = (x - x_high.astype(F32)).astype(BF16)
     dot = functools.partial(jnp.dot, preferred_element_type=F32)
@@ -321,52 +346,42 @@
 
 
 def make_basis(image, high, low):
-    rows, width = image.shape[-2:]
-    view = image.reshape(2, 4, 2, rows, width)
+    rows, width = image.shape
+    half = pl.BlockSpec((rows // 2, width), lambda h: (h, 0))
     return pl.pallas_call(
         basis_kernel,
-        grid=(2, 2),
-        in_specs=[
-            pl.BlockSpec((1, 4, 1, rows, width), lambda h, o: (h, 0, o, 0, 0)),
-            in_vmem(),
-            in_vmem(),
-        ],
-        out_specs=pl.BlockSpec((4 * rows, width), lambda h, o: (2 * h + o, 0)),
-        out_shape=jax.ShapeDtypeStruct((16 * rows, width), F32),
-        compiler_params=params(16),
+        grid=(2,),
+        in_specs=[half, in_vmem(), in_vmem()],
+        out_specs=half,
+        out_shape=jax.ShapeDtypeStruct((rows, width), F32),
+        compiler_params=params(60),
         name="make_basis",
-    )(view, high, low)
-
-
-def shifted(value, axis, steps):
-    count = lax.axis_size(axis)
-    leading, last = (max(0, -steps), min(count, count - steps))
-    return lax.ppermute(value, axis, [(source, source + steps) for source in range(leading, last)])
+    )(image, high, low)
+
+
+def paired(value, axis, first):
+    pairs = [(i, i + 1) for i in range(first, lax.axis_size(axis) - 1, 2)]
+    return lax.ppermute(value, axis, pairs + [(j, i) for i, j in pairs])
 
 
 def body(probes, weights, columns):
     rows, width = probes.shape
     w_local = weights[0]
     blocks, _, bs, _ = w_local.shape
-    lower = shifted(probes, "brick", 1)
-    higher = shifted(probes, "brick", -1)
+    far = paired(probes, "brick", 1)
+    near = paired(probes, "brick", 0)
     shape = (blocks, bs, width)
-    own, below, above = apply_operator(
-        columns.reshape(-1), w_local, lower.reshape(shape), probes.reshape(shape), higher.reshape(shape)
-    )
-    from_above = shifted(below, "brick", -1)
-    from_below = shifted(above, "brick", 1)
-
-    zh, zp = lax.axis_index("zh"), lax.axis_index("zp")
-    odd = jnp.full((1,), zp, jnp.int32)
-    keep_a, send_a, keep_b, send_b = split_halves(odd, own, from_above, from_below)
+    cols = columns.reshape(-1)
+    w_sorted, own_data = start_operator(cols, w_local, probes.reshape(shape))
+    own, to_far, to_near = finish_operator(cols, w_sorted, own_data, far.reshape(shape), near.reshape(shape))
+    from_far = paired(to_far, "brick", 1)
+    from_near = paired(to_near, "brick", 0)
+
     n = lax.axis_size("zh") * lax.axis_size("zp")
-    got_a = lax.ppermute(send_a, DEPTH, [(i, i ^ 1) for i in range(n)])
-    got_b = lax.ppermute(send_b, DEPTH, [(i, (((i + 1) ^ 1) - 1) % n) for i in range(n)])
-    pieces = lax.all_to_all(add_pairs(keep_a, got_a, keep_b, got_b), "zh", 0, 0)
-    block = (zh // 4) * 8 + zp * 4 + zh % 4
-    image = make_image(jnp.full((1,), block, jnp.int32), pieces, probes)
-    whole_image = lax.all_gather(image, DEPTH)
+    keep, send = split_halves(own, from_far, from_near)
+    got = lax.ppermute(send, DEPTH, [(i, i ^ 1) for i in range(n)])
+    image = make_image(lax.all_to_all(add_pair(keep, got), "zh", 0, 0), probes)
+    whole_image = lax.all_gather(image, DEPTH, tiled=True)
     gram = make_gram(image)
 
     bricks = lax.axis_size("brick")

time: 208 us -> 189 us (0.909)
  blocking collectives: 48.9 us -> 90.9 us
  waiting for transfers between devices: 75.9 us -> 42.4 us
  starting transfers between devices: 34.2 us -> 14.3 us
  Pallas kernels: 26.3 us -> 21.3 us
  local copies, waits for them, and re-layouts: 7.74 us -> 5.27 us
    all_to_all x0 -> x1, blocking collectives: none -> 45 us  [body(): image = make_image(lax.all_to_all(add_pair(keep, got), 'zh', 0, 0), probes)]
    all_to_all x1 -> x0, waiting for transfers between devices: 29 us -> none  [body(): pieces = lax.all_to_all(add_pairs(keep_a, got_a, keep_b, got_b), 'zh', 0, 0)]
    ppermute x6 -> x5, starting transfers between devices: 25.6 us -> 14.2 us  [the longest x4 10.3 us: paired(): return lax.ppermute(value, axis, pairs + [(j, i) for i, j in pairs])]
    all_to_all x1 -> x0, starting transfers between devices: 8.55 us -> none  [body(): pieces = lax.all_to_all(add_pairs(keep_a, got_a, keep_b, got_b), 'zh', 0, 0)]
    pallas_call x5 -> x6, Pallas kernels: 15.9 us -> 10.9 us  [the longest x1 3.99 us: finish_operator(): pl.pallas_call(operator_kernel, in_specs=[pl.BlockSpec(memory_space=pltpu...]
    all_to_all x1, blocking collectives: 16.6 us -> 13.2 us  [body(): lax.all_to_all(gram.reshape(bricks, width // bricks, width), 'brick', 0, 0)]
    ppermute x6 -> x5, waiting for transfers between devices: 31.3 us -> 28.3 us  [the longest x4 16.1 us: paired(): return lax.ppermute(value, axis, pairs + [(j, i) for i, j in pairs])]
    unnamed x13 -> x11, local copies, waits for them, and re-layouts: 7.66 us -> 5.19 us
  transfers between devices with their start and end apart: 8 -> 6, of which waited for: 7 -> 4; matrix products, arithmetic and copies ran while one was open for 0% -> 0% of each run, Pallas kernels for 5% -> 7%
where the time goes in v4:
time: 189 us; the launch traced here: 188 us
  blocking collectives  90.9 us (48%)
  waiting for transfers between devices  42.4 us (22%)
  Pallas kernels  21.3 us (11%)
  starting transfers between devices  14.3 us (8%)
  between operations  14.1 us (7%)
  local copies, waits for them, and re-layouts  5.27 us (3%)
    all_to_all x1, blocking collectives, body(): image = make_image(lax.all_to_all(add_pair(keep, got), 'zh', 0, 0), probes)  45 us
    all_to_all x1, blocking collectives, body(): share = lax.all_to_all(spread_sum(share, n), DEPTH, 0, 0)  19.8 us
    ppermute x4, waiting for transfers between devices, paired(): return lax.ppermute(value, axis, pairs + [(j, i) for i, j in pairs])  16.1 us
    all_gather x1, waiting for transfers between devices, body(): whole_image = lax.all_gather(image, DEPTH, tiled=True)  14.1 us
    all_to_all x1, blocking collectives, body(): lax.all_to_all(gram.reshape(bricks, width // bricks, width), 'brick', 0, 0)  13.2 us
    all_to_all x1, blocking collectives, body(): lax.all_to_all(spread_sum(share, bricks), 'brick', 0, 0)  13 us
    ppermute x1, waiting for transfers between devices, body(): got = lax.ppermute(send, DEPTH, [(i, i ^ 1) for i in range(n)])  12.2 us
    ppermute x4, starting transfers between devices, paired(): return lax.ppermute(value, axis, pairs + [(j, i) for i, j in pairs])  10.3 us
  transfers between devices with their start and end apart: 6, of which 4 were waited for; matrix products, arithmetic and copies ran while one was open for 0% of the time, Pallas kernels for 7%

profile of v4, /device:TPU:12, one launch (start us, length us, event | category | flops | bytes accessed | tf_op | source)
XLA Modules:
  0.0 188.3 jit_solution(17726633858055109795)
XLA Ops:
  7.2 0.0 all-gather.2.cloned.1.call-start
  7.2 1.9 %collective-permute-start = (bf16[2048,256]{1,0:T(8,128)(2,1)}, bf16[2048,256]{1,0:T(8,128)(2,1)S(1)}, u32[]{:S(2)}, u32[]{:S(2)}) collective-permute-start(bf16[2048,256]{1,0:T(8,128)(2,1)} %probes.1), channel_id=1, source_target_pairs={{1,2},{3,4},{5,6},{7,8},{9,10},{11,12},{13,14},{15,16},{17,18},{19... | collective-permute-start | bytes 3145736 | tf_op jit(solution)/shard_map/ppermute | solution.py:364
  9.1 3.2 %collective-permute-start.1 = (bf16[2048,256]{1,0:T(8,128)(2,1)}, bf16[2048,256]{1,0:T(8,128)(2,1)S(1)}, u32[]{:S(2)}, u32[]{:S(2)}) collective-permute-start(bf16[2048,256]{1,0:T(8,128)(2,1)} %probes.1), channel_id=1, source_target_pairs={{0,1},{2,3},{4,5},{6,7},{8,9},{10,11},{12,13},{14,15},{16,17},{18,... | collective-permute-start | bytes 3145736 | tf_op jit(solution)/shard_map/ppermute | solution.py:364
  12.4 0.8 copy.6
  13.1 0.1 reshape.22.cols
  13.2 0.0 copy-start
  13.2 1.2 copy-done
  14.4 0.0 copy-start.2
  14.4 1.9 %copy-done.2 = bf16[1,8,3,256,256]{4,3,2,1,0:T(8,128)(2,1)S(1)} copy-done((bf16[1,8,3,256,256]{4,3,2,1,0:T(8,128)(2,1)S(1)}, bf16[1,8,3,256,256]{4,3,2,1,0:T(8,128)(2,1)}, u32[]{:S(2)}) %copy-start.2) | copy-done | bytes 3145752
  16.3 2.1 %own_data.1 = (bf16[8,3,256,256]{3,2,1,0:T(8,128)(2,1)S(1)}, f32[8,256,256]{2,1,0:T(8,128)S(1)}) custom-call(s32[24]{0:T(128)S(1)} %reshape.22.cols, bf16[8,3,256,256]{3,2,1,0:T(8,128)(2,1)S(1)} %bitcast.7, bf16[8,256,256]{2,1,0:T(8,128)(2,1)S(1)} %bitcast.6), custom_call_target="tpu_custom_call" | custom-call | flops 268435456 | bytes 9437184 | tf_op jit(solution)/shard_map/own_data/pallas_call | solution.py:60
  18.4 5.1 %collective-permute-done = bf16[2048,256]{1,0:T(8,128)(2,1)S(1)} collective-permute-done((bf16[2048,256]{1,0:T(8,128)(2,1)}, bf16[2048,256]{1,0:T(8,128)(2,1)S(1)}, u32[]{:S(2)}, u32[]{:S(2)}) %collective-permute-start) | collective-permute-done | bytes 1048608 | tf_op jit(solution)/shard_map/ppermute | solution.py:364
  23.5 0.0 collective-permute-done.1
  23.5 4.0 %normal_operator.1 = (f32[16,256,128]{2,1,0:T(8,128)S(1)}, bf16[16,256,128]{2,1,0:T(8,128)(2,1)S(1)}, bf16[16,256,128]{2,1,0:T(8,128)(2,1)S(1)}) custom-call(s32[24]{0:T(128)S(1)} %reshape.22.cols, bf16[8,3,256,256]{3,2,1,0:T(8,128)(2,1)S(1)} %get-tuple-element.12.w_ref, f32[8,256,256]{2,1,0:T(8,128)S(1)} %get-tuple-element.13.data_ref, ...), custom_call_target="tpu_custom_call" | custom-call | tf_op jit(solution)/shard_map/normal_operator/pallas_call | solution.py:118
  27.5 2.2 %collective-permute-start.2 = (bf16[16,256,128]{2,1,0:T(8,128)(2,1)S(1)}, bf16[16,256,128]{2,1,0:T(8,128)(2,1)S(1)}, u32[]{:S(2)}, u32[]{:S(2)}) collective-permute-start(bf16[16,256,128]{2,1,0:T(8,128)(2,1)S(1)} %get-tuple-element.15), channel_id=1, source_target_pairs={{1,2},{3,4},{5,6},{7,8},{9,10},{11,12},{13,14},{15,16},{17,18},{19... | collective-permute-start | bytes 3145736 | tf_op jit(solution)/shard_map/ppermute | solution.py:364
  29.7 3.0 %collective-permute-start.3 = (bf16[16,256,128]{2,1,0:T(8,128)(2,1)S(1)}, bf16[16,256,128]{2,1,0:T(8,128)(2,1)S(1)}, u32[]{:S(2)}, u32[]{:S(2)}) collective-permute-start(bf16[16,256,128]{2,1,0:T(8,128)(2,1)S(1)} %get-tuple-element.16), channel_id=1, source_target_pairs={{0,1},{2,3},{4,5},{6,7},{8,9},{10,11},{12,13},{14,15},{16,17},{18,... | collective-permute-start | bytes 3145736 | tf_op jit(solution)/shard_map/ppermute | solution.py:364
  32.7 11.0 %collective-permute-done.2.far = bf16[16,256,128]{2,1,0:T(8,128)(2,1)S(1)} collective-permute-done((bf16[16,256,128]{2,1,0:T(8,128)(2,1)S(1)}, bf16[16,256,128]{2,1,0:T(8,128)(2,1)S(1)}, u32[]{:S(2)}, u32[]{:S(2)}) %collective-permute-start.2) | collective-permute-done | bytes 1048608 | tf_op jit(solution)/shard_map/ppermute | solution.py:364
  43.7 0.0 collective-permute-done.3.near
  43.7 0.4 split_halves.1
  44.1 0.0 copy-start.1
  44.1 4.0 %collective-permute-start.4 = (bf16[8,256,128]{2,1,0:T(8,128)(2,1)S(1)}, bf16[8,256,128]{2,1,0:T(8,128)(2,1)S(1)}, u32[]{:S(2)}, u32[]{:S(2)}) collective-permute-start(bf16[8,256,128]{2,1,0:T(8,128)(2,1)S(1)} %get-tuple-element.18), channel_id=1, source_target_pairs={{0,32},{32,0},{64,96},{96,64},{128,160},{160,128},{192,224},{224,1... | collective-permute-start | bytes 1572872 | tf_op jit(solution)/shard_map/ppermute | solution.py:382
  48.0 12.2 %collective-permute-done.4.got = bf16[8,256,128]{2,1,0:T(8,128)(2,1)S(1)} collective-permute-done((bf16[8,256,128]{2,1,0:T(8,128)(2,1)S(1)}, bf16[8,256,128]{2,1,0:T(8,128)(2,1)S(1)}, u32[]{:S(2)}, u32[]{:S(2)}) %collective-permute-start.4) | collective-permute-done | bytes 524320 | tf_op jit(solution)/shard_map/ppermute | solution.py:382
  60.2 0.1 add_pair.1
  60.3 45.0 %all_to_all.20.pieces = bf16[8,256,128]{2,1,0:T(8,128)(2,1)S(1)} all-to-all(bf16[8,256,128]{2,1,0:T(8,128)(2,1)S(1)} %add_pair.1), channel_id=1, replica_groups=mesh['zh'=8,'zp'=2,'brick'=32] {'zh'}, dimensions={0} | all-to-all | bytes 1048576 | tf_op jit(solution)/shard_map/all_to_all | solution.py:383
  105.3 0.0 copy-done.1
  105.3 0.9 make_image.1.image
  106.2 0.0 all-gather.2.cloned.1.call-update
  106.2 1.3 make_gram.1
  107.6 13.2 %all_to_all.21.pieces = f32[32,8,256]{2,1,0:T(8,128)S(1)} all-to-all(f32[32,8,256]{2,1,0:T(8,128)S(1)} %bitcast.9), channel_id=1, replica_groups=mesh['zh'=8,'zp'=2,'brick'=32] {'brick'}, dimensions={0} | all-to-all | bytes 524288 | tf_op jit(solution)/shard_map/all_to_all | solution.py:388
  120.8 19.8 %all_to_all.22.pieces = f32[16,8,256]{2,1,0:T(8,128)S(1)} all-to-all(f32[16,8,256]{2,1,0:T(8,128)S(1)} %spread_sum.2), channel_id=1, replica_groups=mesh['zh'=8,'zp'=2,'brick'=32] {'zh','zp'}, dimensions={0} | all-to-all | bytes 262144 | tf_op jit(solution)/shard_map/all_to_all | solution.py:389
  140.6 13.0 %all_to_all.23 = f32[32,8,256]{2,1,0:T(8,128)S(1)} all-to-all(f32[32,8,256]{2,1,0:T(8,128)S(1)} %spread_sum.3), channel_id=1, replica_groups=mesh['zh'=8,'zp'=2,'brick'=32] {'brick'}, dimensions={0} | all-to-all | bytes 524288 | tf_op jit(solution)/shard_map/all_to_all | solution.py:390
  153.6 9.0 %cholesky_and_inverse.1 = (f32[256,256]{1,0:T(8,128)}, bf16[256,256]{1,0:T(8,128)(2,1)S(1)}, bf16[256,256]{1,0:T(8,128)(2,1)S(1)}) custom-call(f32[256,256]{1,0:T(8,128)S(1)} %bitcast.8), custom_call_target="tpu_custom_call" | custom-call | tf_op jit(solution)/shard_map/cholesky_and_inverse/pallas_call | solution.py:329
  162.6 0.0 copy-start.3
  162.6 0.6 copy-done.3
  163.2 0.0 copy-start.4
  163.2 0.7 copy-done.4
  163.9 14.1 %all-gather.2.cloned.1.call-done.image = f32[2048,256]{1,0:T(8,128)} async-done(((f32[128,256]{1,0:T(8,128)}), f32[2048,256]{1,0:T(8,128)}) %all-gather.2.cloned.1.call-update) | async-done | bytes 2097168 | tf_op jit(solution)/shard_map/all_gather | solution.py:384
  178.0 3.4 %make_basis.1 = f32[2048,256]{1,0:T(8,128)} custom-call(f32[2048,256]{1,0:T(8,128)} %all-gather.2.cloned.1.call-done.image, bf16[256,256]{1,0:T(8,128)(2,1)} %copy-done.3, bf16[256,256]{1,0:T(8,128)(2,1)} %copy-done.4), custom_call_target="tpu_custom_call" | custom-call | tf_op jit(solution)/shard_map/make_basis/pallas_call | solution.py:351
  (2 shorter events, 0.1 us)
Async XLA Ops:
  7.2 170.8 %all-gather.2.cloned.1.call-start = ((), (), s32[]{:S(2)}) async-start(), calls=%async_computation.4 | async-start | bytes 2228224 | tf_op jit(solution)/shard_map/all_gather | solution.py:384
  7.2 16.3 %collective-permute-start = (bf16[2048,256]{1,0:T(8,128)(2,1)}, bf16[2048,256]{1,0:T(8,128)(2,1)S(1)}, u32[]{:S(2)}, u32[]{:S(2)}) collective-permute-start(bf16[2048,256]{1,0:T(8,128)(2,1)} %probes.1), channel_id=1, source_target_pairs={{1,2},{3,4},{5,6},{7,8},{9,10},{11,12},{13,14},{15,16},{17,18},{19... | collective-permute-start | bytes 3145736 | tf_op jit(solution)/shard_map/ppermute | solution.py:364
  9.1 14.4 %collective-permute-start.1 = (bf16[2048,256]{1,0:T(8,128)(2,1)}, bf16[2048,256]{1,0:T(8,128)(2,1)S(1)}, u32[]{:S(2)}, u32[]{:S(2)}) collective-permute-start(bf16[2048,256]{1,0:T(8,128)(2,1)} %probes.1), channel_id=1, source_target_pairs={{0,1},{2,3},{4,5},{6,7},{8,9},{10,11},{12,13},{14,15},{16,17},{18,... | collective-permute-start | bytes 3145736 | tf_op jit(solution)/shard_map/ppermute | solution.py:364
  13.2 1.2 copy-start
  14.4 1.9 %copy-start.2 = (bf16[1,8,3,256,256]{4,3,2,1,0:T(8,128)(2,1)S(1)}, bf16[1,8,3,256,256]{4,3,2,1,0:T(8,128)(2,1)}, u32[]{:S(2)}) copy-start(bf16[1,8,3,256,256]{4,3,2,1,0:T(8,128)(2,1)} %param.4) | copy-start | bytes 9437188
  27.5 16.1 %collective-permute-start.2 = (bf16[16,256,128]{2,1,0:T(8,128)(2,1)S(1)}, bf16[16,256,128]{2,1,0:T(8,128)(2,1)S(1)}, u32[]{:S(2)}, u32[]{:S(2)}) collective-permute-start(bf16[16,256,128]{2,1,0:T(8,128)(2,1)S(1)} %get-tuple-element.15), channel_id=1, source_target_pairs={{1,2},{3,4},{5,6},{7,8},{9,10},{11,12},{13,14},{15,16},{17,18},{19... | collective-permute-start | bytes 3145736 | tf_op jit(solution)/shard_map/ppermute | solution.py:364
  29.7 14.0 %collective-permute-start.3 = (bf16[16,256,128]{2,1,0:T(8,128)(2,1)S(1)}, bf16[16,256,128]{2,1,0:T(8,128)(2,1)S(1)}, u32[]{:S(2)}, u32[]{:S(2)}) collective-permute-start(bf16[16,256,128]{2,1,0:T(8,128)(2,1)S(1)} %get-tuple-element.16), channel_id=1, source_target_pairs={{0,1},{2,3},{4,5},{6,7},{8,9},{10,11},{12,13},{14,15},{16,17},{18,... | collective-permute-start | bytes 3145736 | tf_op jit(solution)/shard_map/ppermute | solution.py:364
  44.1 61.2 %copy-start.1 = (bf16[2048,256]{1,0:T(8,128)(2,1)S(1)}, bf16[2048,256]{1,0:T(8,128)(2,1)}, u32[]{:S(2)}) copy-start(bf16[2048,256]{1,0:T(8,128)(2,1)} %probes.1) | copy-start | bytes 3145732
  44.1 16.2 %collective-permute-start.4 = (bf16[8,256,128]{2,1,0:T(8,128)(2,1)S(1)}, bf16[8,256,128]{2,1,0:T(8,128)(2,1)S(1)}, u32[]{:S(2)}, u32[]{:S(2)}) collective-permute-start(bf16[8,256,128]{2,1,0:T(8,128)(2,1)S(1)} %get-tuple-element.18), channel_id=1, source_target_pairs={{0,32},{32,0},{64,96},{96,64},{128,160},{160,128},{192,224},{224,1... | collective-permute-start | bytes 1572872 | tf_op jit(solution)/shard_map/ppermute | solution.py:382
  162.6 0.7 copy-start.3
  163.2 0.7 copy-start.4
Sparse Core Ops, SparseCore 0:
  106.4 71.5 all-gather.1

commit v5 on v4

--- a/solution.py
+++ b/solution.py
@@ -14,6 +14,8 @@
 PANEL = 64
 MIB = 1024 * 1024
 DEPTH = ("zh", "zp")
+TAIL = 16
+CODE_TOP = 32000.0
 
 
 def exact_dot(a, b, dims):
@@ -167,7 +169,7 @@
     )(keep, got)
 
 
-def image_kernel(pieces, probes, image, own, sem):
+def image_kernel(pieces, probes, image, coded, own, sem):
     rows = own.shape[0]
     block = 2 * lax.axis_index("zh") + lax.axis_index("zp")
     copy = pltpu.make_async_copy(probes.at[pl.ds(block * rows, rows)], own, sem)
@@ -176,7 +178,14 @@
     for k in range(1, pieces.shape[0]):
         total = total + pieces[k].astype(F32)
     copy.wait()
-    image[...] = own[...].astype(F32) + total.T
+    x = own[...].astype(F32) + total.T
+    image[...] = x
+    top = jnp.maximum(jnp.max(jnp.abs(x), axis=0, keepdims=True), 1e-30)
+    power = jnp.ceil(jnp.log(top) * (1.0 / math.log(2.0)))
+    whole = jnp.floor(x * (jnp.exp2(-power) * CODE_TOP) + 0.5)
+    coded[:rows] = whole.astype(jnp.int32).astype(jnp.int16)
+    tail = jnp.broadcast_to(power, (TAIL, x.shape[1]))
+    coded[rows:] = tail.astype(jnp.int32).astype(jnp.int16)
 
 
 def make_image(pieces, probes):
@@ -184,8 +193,11 @@
     return pl.pallas_call(
         image_kernel,
         in_specs=[in_vmem(), pl.BlockSpec(memory_space=pltpu.HBM)],
-        out_specs=in_vmem(),
-        out_shape=jax.ShapeDtypeStruct((cells, width), F32),
+        out_specs=[in_vmem()] * 2,
+        out_shape=(
+            jax.ShapeDtypeStruct((cells, width), F32),
+            jax.ShapeDtypeStruct((cells + TAIL, width), jnp.int16),
+        ),
         scratch_shapes=[pltpu.VMEM((cells, width), BF16), pltpu.SemaphoreType.DMA],
         compiler_params=params(4),
         name="make_image",
@@ -208,23 +220,49 @@
     )(image)
 
 
-def spread_sum_kernel(pieces, out):
+def spread_sum_kernel(pieces, held, got, out, joined):
     total = pieces[0]
     for k in range(1, pieces.shape[0]):
         total = total + pieces[k]
     for k in range(out.shape[0]):
         out[k] = total
-
-
-def spread_sum(pieces, copies):
+    copy_both(held, got, joined)
+
+
+def spread_sum(pieces, copies, held, got):
+    count = held.shape[0]
     return pl.pallas_call(
         spread_sum_kernel,
-        in_specs=[in_vmem()],
+        in_specs=[in_vmem()] * 3,
+        out_specs=[in_vmem()] * 2,
+        out_shape=(
+            jax.ShapeDtypeStruct((copies,) + pieces.shape[1:], F32),
+            jax.ShapeDtypeStruct((2 * count,) + held.shape[1:], held.dtype),
+        ),
+        compiler_params=params(6),
+        name="spread_sum",
+    )(pieces, held, got)
+
+
+def copy_both(held, got, joined):
+    count = held.shape[0]
+    joined[:count] = held[...]
+    joined[count:] = got[...]
+
+
+def join_kernel(held, got, gram, joined):
+    copy_both(held, got, joined)
+
+
+def join(held, got, gram):
+    return pl.pallas_call(
+        join_kernel,
+        in_specs=[in_vmem()] * 2 + [pl.BlockSpec(memory_space=pl.ANY)],
         out_specs=in_vmem(),
-        out_shape=jax.ShapeDtypeStruct((copies,) + pieces.shape[1:], F32),
-        compiler_params=params(4),
-        name="spread_sum",
-    )(pieces)
+        out_shape=jax.ShapeDtypeStruct((2 * held.shape[0],) + held.shape[1:], held.dtype),
+        compiler_params=params(6),
+        name="join",
+    )(held, got, gram)
 
 
 def eliminate(tiles, lane0):
@@ -337,26 +375,51 @@
     )(gram)
 
 
-def basis_kernel(image, high, low, out):
-    x = image[...]
-    x_high = x.astype(BF16)
-    x_low = (x - x_high.astype(F32)).astype(BF16)
+def basis_kernel(held, got, high, low, out, staged, sems):
+    count = held.shape[0]
+    rows, width = staged.shape[2:]
+    group = staged.shape[1]
+    here = 2 * lax.axis_index("zh") + lax.axis_index("zp")
     dot = functools.partial(jnp.dot, preferred_element_type=F32)
-    out[...] = dot(x_high, high[...]) + (dot(x_high, low[...]) + dot(x_low, high[...]))
-
-
-def make_basis(image, high, low):
-    rows, width = image.shape
-    half = pl.BlockSpec((rows // 2, width), lambda h: (h, 0))
+    copies = []
+    for g in range(staged.shape[0]):
+        parts = []
+        for i in range(group):
+            k = g * group + i
+            piece = (held if k < count else got).at[k % count]
+            power = piece[rows:].astype(jnp.int32).astype(F32)[:1]
+            parts.append(piece[:rows].astype(jnp.int32).astype(F32) * (jnp.exp2(power) * (1.0 / CODE_TOP)))
+        x = jnp.concatenate(parts, axis=0)
+        x_high = x.astype(BF16)
+        x_low = (x - x_high.astype(F32)).astype(BF16)
+        y = dot(x_high, high[...]) + (dot(x_high, low[...]) + dot(x_low, high[...]))
+        staged[g] = y.reshape(group, rows, width)
+        for i in range(group):
+            k = g * group + i
+            flip = 8 * (k & 1) + 4 * (k >> 1 & 1) + 2 * (k >> 2 & 1) + (k >> 3)
+            to = pl.ds(pl.multiple_of((here ^ flip) * rows, rows), rows)
+            copy = pltpu.make_async_copy(staged.at[g, i], out.at[to], sems.at[k])
+            copy.start()
+            copies.append(copy)
+    for copy in copies:
+        copy.wait()
+
+
+def make_basis(held, got, high, low):
+    count, rows, width = held.shape
+    rows -= TAIL
     return pl.pallas_call(
         basis_kernel,
-        grid=(2,),
-        in_specs=[half, in_vmem(), in_vmem()],
-        out_specs=half,
-        out_shape=jax.ShapeDtypeStruct((rows, width), F32),
-        compiler_params=params(60),
+        in_specs=[in_vmem()] * 4,
+        out_specs=pl.BlockSpec(memory_space=pltpu.HBM),
+        out_shape=jax.ShapeDtypeStruct((2 * count * rows, width), F32),
+        scratch_shapes=[
+            pltpu.VMEM((4, count // 2, rows, width), F32),
+            pltpu.SemaphoreType.DMA((2 * count,)),
+        ],
+        compiler_params=params(16),
         name="make_basis",
-    )(image, high, low)
+    )(held, got, high, low)
 
 
 def paired(value, axis, first):
@@ -380,18 +443,28 @@
     n = lax.axis_size("zh") * lax.axis_size("zp")
     keep, send = split_halves(own, from_far, from_near)
     got = lax.ppermute(send, DEPTH, [(i, i ^ 1) for i in range(n)])
-    image = make_image(lax.all_to_all(add_pair(keep, got), "zh", 0, 0), probes)
-    whole_image = lax.all_gather(image, DEPTH, tiled=True)
+    image, coded = make_image(lax.all_to_all(add_pair(keep, got), "zh", 0, 0), probes)
+
+    def swap(held, distance):
+        return lax.ppermute(held, DEPTH, [(i, i ^ distance) for i in range(n)])
+
+    held = coded[None]
+    got = swap(held, 8)
     gram = make_gram(image)
-
     bricks = lax.axis_size("brick")
     share = lax.all_to_all(gram.reshape(bricks, width // bricks, width), "brick", 0, 0)
-    share = lax.all_to_all(spread_sum(share, n), DEPTH, 0, 0)
-    gram = lax.all_to_all(spread_sum(share, bricks), "brick", 0, 0).reshape(width, width)
+    share, held = spread_sum(share, n, held, got)
+    got = swap(held, 4)
+    share = lax.all_to_all(share, DEPTH, 0, 0)
+    share, held = spread_sum(share, bricks, held, got)
+    got = swap(held, 2)
+    gram = lax.all_to_all(share, "brick", 0, 0).reshape(width, width)
+    held = join(held, got, gram)
+    got = swap(held, 1)
 
     scale = math.sqrt(rows * bricks)
     upper, high, low = cholesky_and_inverse(gram, scale)
-    return make_basis(whole_image, high, low), upper
+    return make_basis(held, got, high, low), upper
 
 
 def solution(mesh):

time: 189 us -> 195 us (1.032)
  the two profiles are of different devices: /device:TPU:12 before, /device:TPU:1 now
where the time goes in v5:
time: 195 us
  starting transfers between devices  57.8 us (30%)
  blocking collectives  57.7 us (30%)
  waiting for transfers between devices  54.3 us (28%)
  Pallas kernels  20 us (10%)
  local copies, waits for them, and re-layouts  3.96 us (2%)
    all_to_all x1, blocking collectives, body(): lax.all_to_all(add_pair(keep, got), 'zh', 0, 0)  41.2 us
    ppermute x4, waiting for transfers between devices, swap(): return lax.ppermute(held, DEPTH, [(i, i ^ distance) for i in range(n)])  35.3 us
    all_to_all x1, starting transfers between devices, body(): lax.all_to_all(gram.reshape(bricks, width // bricks, width), 'brick', 0, 0)  17.2 us
    all_to_all x1, blocking collectives, body(): gram = lax.all_to_all(share, 'brick', 0, 0).reshape(width, width)  16.5 us
    ppermute x4, starting transfers between devices, swap(): return lax.ppermute(held, DEPTH, [(i, i ^ distance) for i in range(n)])  16 us
    ppermute x4, starting transfers between devices, paired(): return lax.ppermute(value, axis, pairs + [(j, i) for i, j in pairs])  15.1 us
    ppermute x4, waiting for transfers between devices, paired(): return lax.ppermute(value, axis, pairs + [(j, i) for i, j in pairs])  12.5 us
    pallas_call x1, Pallas kernels, cholesky_and_inverse(): pl.pallas_call(functools.partial(factor_kernel, scale), in_specs=[in_vmem...  9 us
  transfers between devices with their start and end apart: 11, of which 6 were waited for; matrix products, arithmetic and copies ran while one was open for 0% of the time, Pallas kernels for 6%

profile of v5, /device:TPU:1, one launch (start us, length us, event | category | flops | bytes accessed | tf_op | source)
XLA Modules:
  0.0 194.6 jit_solution(5409790544639967826)
XLA Ops:
  0.6 4.5 %collective-permute-start = (bf16[2048,256]{1,0:T(8,128)(2,1)}, bf16[2048,256]{1,0:T(8,128)(2,1)S(1)}, u32[]{:S(2)}, u32[]{:S(2)}) collective-permute-start(bf16[2048,256]{1,0:T(8,128)(2,1)} %probes.1), channel_id=1, source_target_pairs={{1,2},{3,4},{5,6},{7,8},{9,10},{11,12},{13,14},{15,16},{17,18},{19... | collective-permute-start | bytes 3145736 | tf_op jit(solution)/shard_map/ppermute | solution.py:427
  5.1 5.0 %collective-permute-start.1 = (bf16[2048,256]{1,0:T(8,128)(2,1)}, bf16[2048,256]{1,0:T(8,128)(2,1)S(1)}, u32[]{:S(2)}, u32[]{:S(2)}) collective-permute-start(bf16[2048,256]{1,0:T(8,128)(2,1)} %probes.1), channel_id=1, source_target_pairs={{0,1},{2,3},{4,5},{6,7},{8,9},{10,11},{12,13},{14,15},{16,17},{18,... | collective-permute-start | bytes 3145736 | tf_op jit(solution)/shard_map/ppermute | solution.py:427
  10.2 0.8 copy.6
  10.9 0.1 reshape.22.cols
  11.0 0.0 copy-start
  11.0 1.2 copy-done
  12.2 0.0 copy-start.2
  12.2 1.9 copy-done.2
  14.1 2.1 %own_data.1 = (bf16[8,3,256,256]{3,2,1,0:T(8,128)(2,1)S(1)}, f32[8,256,256]{2,1,0:T(8,128)S(1)}) custom-call(s32[24]{0:T(128)S(1)} %reshape.22.cols, bf16[8,3,256,256]{3,2,1,0:T(8,128)(2,1)S(1)} %bitcast.8, bf16[8,256,256]{2,1,0:T(8,128)(2,1)S(1)} %bitcast.7), custom_call_target="tpu_custom_call" | custom-call | flops 268435456 | bytes 9437184 | tf_op jit(solution)/shard_map/own_data/pallas_call | solution.py:62
  16.2 1.6 collective-permute-done
  17.8 0.0 collective-permute-done.1
  17.8 4.0 %normal_operator.1 = (f32[16,256,128]{2,1,0:T(8,128)S(1)}, bf16[16,256,128]{2,1,0:T(8,128)(2,1)S(1)}, bf16[16,256,128]{2,1,0:T(8,128)(2,1)S(1)}) custom-call(s32[24]{0:T(128)S(1)} %reshape.22.cols, bf16[8,3,256,256]{3,2,1,0:T(8,128)(2,1)S(1)} %get-tuple-element.18.w_ref, f32[8,256,256]{2,1,0:T(8,128)S(1)} %get-tuple-element.19.data_ref, ...), custom_call_target="tpu_custom_call" | custom-call | tf_op jit(solution)/shard_map/normal_operator/pallas_call | solution.py:120
  21.8 3.6 %collective-permute-start.2 = (bf16[16,256,128]{2,1,0:T(8,128)(2,1)S(1)}, bf16[16,256,128]{2,1,0:T(8,128)(2,1)S(1)}, u32[]{:S(2)}, u32[]{:S(2)}) collective-permute-start(bf16[16,256,128]{2,1,0:T(8,128)(2,1)S(1)} %get-tuple-element.21), channel_id=1, source_target_pairs={{1,2},{3,4},{5,6},{7,8},{9,10},{11,12},{13,14},{15,16},{17,18},{19... | collective-permute-start | bytes 3145736 | tf_op jit(solution)/shard_map/ppermute | solution.py:427
  25.5 1.9 collective-permute-start.3
  27.4 10.8 %collective-permute-done.2.far = bf16[16,256,128]{2,1,0:T(8,128)(2,1)S(1)} collective-permute-done((bf16[16,256,128]{2,1,0:T(8,128)(2,1)S(1)}, bf16[16,256,128]{2,1,0:T(8,128)(2,1)S(1)}, u32[]{:S(2)}, u32[]{:S(2)}) %collective-permute-start.2) | collective-permute-done | bytes 1048608 | tf_op jit(solution)/shard_map/ppermute | solution.py:427
  38.2 0.0 collective-permute-done.3.near
  38.2 0.4 split_halves.1
  38.6 0.0 copy-start.1
  38.6 3.7 %collective-permute-start.4 = (bf16[8,256,128]{2,1,0:T(8,128)(2,1)S(1)}, bf16[8,256,128]{2,1,0:T(8,128)(2,1)S(1)}, u32[]{:S(2)}, u32[]{:S(2)}) collective-permute-start(bf16[8,256,128]{2,1,0:T(8,128)(2,1)S(1)} %get-tuple-element.24), channel_id=1, source_target_pairs={{0,32},{32,0},{64,96},{96,64},{128,160},{160,128},{192,224},{224,1... | collective-permute-start | bytes 1572872 | tf_op jit(solution)/shard_map/ppermute | solution.py:445
  42.3 6.6 %collective-permute-done.4.got = bf16[8,256,128]{2,1,0:T(8,128)(2,1)S(1)} collective-permute-done((bf16[8,256,128]{2,1,0:T(8,128)(2,1)S(1)}, bf16[8,256,128]{2,1,0:T(8,128)(2,1)S(1)}, u32[]{:S(2)}, u32[]{:S(2)}) %collective-permute-start.4) | collective-permute-done | bytes 524320 | tf_op jit(solution)/shard_map/ppermute | solution.py:445
  48.9 0.1 add_pair.1
  49.0 41.2 %all_to_all.20.pieces = bf16[8,256,128]{2,1,0:T(8,128)(2,1)S(1)} all-to-all(bf16[8,256,128]{2,1,0:T(8,128)(2,1)S(1)} %add_pair.1), channel_id=1, replica_groups=mesh['zh'=8,'zp'=2,'brick'=32] {'zh'}, dimensions={0} | all-to-all | bytes 1048576 | tf_op jit(solution)/shard_map/all_to_all | solution.py:446
  90.1 0.0 copy-done.1
  90.2 0.3 make_image.1
  90.5 1.1 make_gram.1
  91.6 17.2 %all-to-all-start.1 = ((f32[32,8,256]{2,1,0:T(8,128)}), f32[32,8,256]{2,1,0:T(8,128)S(1)}, u32[]{:S(2)}, u32[]{:S(2)}) async-start(f32[32,8,256]{2,1,0:T(8,128)} %bitcast.4), calls=%async_computation.1 | async-start | bytes 524288 | tf_op jit(solution)/shard_map/all_to_all | solution.py:455
  108.8 4.8 %collective-permute-start.5 = (s16[1,144,256]{2,1,0:T(8,128)(2,1)S(1)}, s16[1,144,256]{2,1,0:T(8,128)(2,1)S(1)}, u32[]{:S(2)}, u32[]{:S(2)}) collective-permute-start(s16[1,144,256]{2,1,0:T(8,128)(2,1)S(1)} %bitcast.13), channel_id=1, source_target_pairs={{0,256},{32,288},{64,320},{96,352},{128,384},{160,416},{192,448},{... | collective-permute-start | bytes 221192 | tf_op jit(solution)/shard_map/ppermute | solution.py:449
  113.5 12.0 %collective-permute-done.5.got = s16[1,144,256]{2,1,0:T(8,128)(2,1)S(1)} collective-permute-done((s16[1,144,256]{2,1,0:T(8,128)(2,1)S(1)}, s16[1,144,256]{2,1,0:T(8,128)(2,1)S(1)}, u32[]{:S(2)}, u32[]{:S(2)}) %collective-permute-start.5) | collective-permute-done | bytes 73760 | tf_op jit(solution)/shard_map/ppermute | solution.py:449
  125.6 0.0 all-to-all-done.1.pieces
  125.6 0.7 spread_sum.2
  126.3 5.9 %all-to-all-start.2 = ((f32[16,8,256]{2,1,0:T(8,128)}), f32[16,8,256]{2,1,0:T(8,128)S(1)}, u32[]{:S(2)}, u32[]{:S(2)}) async-start(f32[16,8,256]{2,1,0:T(8,128)} %get-tuple-element.27), calls=%async_computation.2 | async-start | bytes 262144 | tf_op jit(solution)/shard_map/all_to_all | solution.py:458
  132.2 7.2 %collective-permute-start.6 = (s16[2,144,256]{2,1,0:T(8,128)(2,1)S(1)}, s16[2,144,256]{2,1,0:T(8,128)(2,1)S(1)}, u32[]{:S(2)}, u32[]{:S(2)}) collective-permute-start(s16[2,144,256]{2,1,0:T(8,128)(2,1)S(1)} %get-tuple-element.28.held), channel_id=1, source_target_pairs={{0,128},{32,160},{64,192},{96,224},{128,0},{160,32},{192,64},{224,... | collective-permute-start | bytes 442376 | tf_op jit(solution)/shard_map/ppermute | solution.py:449
  139.3 17.7 %collective-permute-done.6.got = s16[2,144,256]{2,1,0:T(8,128)(2,1)S(1)} collective-permute-done((s16[2,144,256]{2,1,0:T(8,128)(2,1)S(1)}, s16[2,144,256]{2,1,0:T(8,128)(2,1)S(1)}, u32[]{:S(2)}, u32[]{:S(2)}) %collective-permute-start.6) | collective-permute-done | bytes 147488 | tf_op jit(solution)/shard_map/ppermute | solution.py:449
  157.1 0.0 all-to-all-done.2.pieces
  157.1 1.9 collective-permute-start.7
  159.1 16.5 %all_to_all.21 = f32[32,8,256]{2,1,0:T(8,128)S(1)} all-to-all(f32[32,8,256]{2,1,0:T(8,128)S(1)} %get-tuple-element.30), channel_id=1, replica_groups=mesh['zh'=8,'zp'=2,'brick'=32] {'brick'}, dimensions={0} | all-to-all | bytes 524288 | tf_op jit(solution)/shard_map/all_to_all | solution.py:461
  175.6 0.0 collective-permute-done.7.got
  175.6 2.1 %collective-permute-start.8 = (s16[8,144,256]{2,1,0:T(8,128)(2,1)S(1)}, s16[8,144,256]{2,1,0:T(8,128)(2,1)S(1)}, u32[]{:S(2)}, u32[]{:S(2)}) collective-permute-start(s16[8,144,256]{2,1,0:T(8,128)(2,1)S(1)} %join.1.held), channel_id=1, source_target_pairs={{0,32},{32,0},{64,96},{96,64},{128,160},{160,128},{192,224},{224,1... | collective-permute-start | bytes 1769480 | tf_op jit(solution)/shard_map/ppermute | solution.py:449
  177.7 9.0 %cholesky_and_inverse.1 = (f32[256,256]{1,0:T(8,128)}, bf16[256,256]{1,0:T(8,128)(2,1)S(1)}, bf16[256,256]{1,0:T(8,128)(2,1)S(1)}) custom-call(f32[256,256]{1,0:T(8,128)S(1)} %bitcast.10), custom_call_target="tpu_custom_call" | custom-call | tf_op jit(solution)/shard_map/cholesky_and_inverse/pallas_call | solution.py:367
  186.7 5.5 %collective-permute-done.8.got = s16[8,144,256]{2,1,0:T(8,128)(2,1)S(1)} collective-permute-done((s16[8,144,256]{2,1,0:T(8,128)(2,1)S(1)}, s16[8,144,256]{2,1,0:T(8,128)(2,1)S(1)}, u32[]{:S(2)}, u32[]{:S(2)}) %collective-permute-start.8) | collective-permute-done | bytes 589856 | tf_op jit(solution)/shard_map/ppermute | solution.py:449
  192.2 2.3 %make_basis.1 = f32[2048,256]{1,0:T(8,128)} custom-call(s16[8,144,256]{2,1,0:T(8,128)(2,1)S(1)} %join.1.held, s16[8,144,256]{2,1,0:T(8,128)(2,1)S(1)} %collective-permute-done.8.got, bf16[256,256]{1,0:T(8,128)(2,1)S(1)} %get-tuple-element.31.high, bf16[256,256]{1,0:T(8,128)(2,1)S(1)} %get-tuple-element.32.low), custom_call_target="tpu_custom_call" | custom-call | tf_op jit(solution)/shard_map/make_basis/pallas_call | solution.py:411
  (2 shorter events, 0.1 us)
Async XLA Ops:
  0.6 17.2 %collective-permute-start = (bf16[2048,256]{1,0:T(8,128)(2,1)}, bf16[2048,256]{1,0:T(8,128)(2,1)S(1)}, u32[]{:S(2)}, u32[]{:S(2)}) collective-permute-start(bf16[2048,256]{1,0:T(8,128)(2,1)} %probes.1), channel_id=1, source_target_pairs={{1,2},{3,4},{5,6},{7,8},{9,10},{11,12},{13,14},{15,16},{17,18},{19... | collective-permute-start | bytes 3145736 | tf_op jit(solution)/shard_map/ppermute | solution.py:427
  5.1 12.7 %collective-permute-start.1 = (bf16[2048,256]{1,0:T(8,128)(2,1)}, bf16[2048,256]{1,0:T(8,128)(2,1)S(1)}, u32[]{:S(2)}, u32[]{:S(2)}) collective-permute-start(bf16[2048,256]{1,0:T(8,128)(2,1)} %probes.1), channel_id=1, source_target_pairs={{0,1},{2,3},{4,5},{6,7},{8,9},{10,11},{12,13},{14,15},{16,17},{18,... | collective-permute-start | bytes 3145736 | tf_op jit(solution)/shard_map/ppermute | solution.py:427
  11.0 1.2 copy-start
  12.2 1.9 copy-start.2
  21.8 16.4 %collective-permute-start.2 = (bf16[16,256,128]{2,1,0:T(8,128)(2,1)S(1)}, bf16[16,256,128]{2,1,0:T(8,128)(2,1)S(1)}, u32[]{:S(2)}, u32[]{:S(2)}) collective-permute-start(bf16[16,256,128]{2,1,0:T(8,128)(2,1)S(1)} %get-tuple-element.21), channel_id=1, source_target_pairs={{1,2},{3,4},{5,6},{7,8},{9,10},{11,12},{13,14},{15,16},{17,18},{19... | collective-permute-start | bytes 3145736 | tf_op jit(solution)/shard_map/ppermute | solution.py:427
  25.5 12.8 %collective-permute-start.3 = (bf16[16,256,128]{2,1,0:T(8,128)(2,1)S(1)}, bf16[16,256,128]{2,1,0:T(8,128)(2,1)S(1)}, u32[]{:S(2)}, u32[]{:S(2)}) collective-permute-start(bf16[16,256,128]{2,1,0:T(8,128)(2,1)S(1)} %get-tuple-element.22), channel_id=1, source_target_pairs={{0,1},{2,3},{4,5},{6,7},{8,9},{10,11},{12,13},{14,15},{16,17},{18,... | collective-permute-start | bytes 3145736 | tf_op jit(solution)/shard_map/ppermute | solution.py:427
  38.6 51.5 %copy-start.1 = (bf16[2048,256]{1,0:T(8,128)(2,1)S(1)}, bf16[2048,256]{1,0:T(8,128)(2,1)}, u32[]{:S(2)}) copy-start(bf16[2048,256]{1,0:T(8,128)(2,1)} %probes.1) | copy-start | bytes 3145732
  38.6 10.2 %collective-permute-start.4 = (bf16[8,256,128]{2,1,0:T(8,128)(2,1)S(1)}, bf16[8,256,128]{2,1,0:T(8,128)(2,1)S(1)}, u32[]{:S(2)}, u32[]{:S(2)}) collective-permute-start(bf16[8,256,128]{2,1,0:T(8,128)(2,1)S(1)} %get-tuple-element.24), channel_id=1, source_target_pairs={{0,32},{32,0},{64,96},{96,64},{128,160},{160,128},{192,224},{224,1... | collective-permute-start | bytes 1572872 | tf_op jit(solution)/shard_map/ppermute | solution.py:445
  91.6 34.0 %all-to-all-start.1 = ((f32[32,8,256]{2,1,0:T(8,128)}), f32[32,8,256]{2,1,0:T(8,128)S(1)}, u32[]{:S(2)}, u32[]{:S(2)}) async-start(f32[32,8,256]{2,1,0:T(8,128)} %bitcast.4), calls=%async_computation.1 | async-start | bytes 524288 | tf_op jit(solution)/shard_map/all_to_all | solution.py:455
  108.8 16.8 %collective-permute-start.5 = (s16[1,144,256]{2,1,0:T(8,128)(2,1)S(1)}, s16[1,144,256]{2,1,0:T(8,128)(2,1)S(1)}, u32[]{:S(2)}, u32[]{:S(2)}) collective-permute-start(s16[1,144,256]{2,1,0:T(8,128)(2,1)S(1)} %bitcast.13), channel_id=1, source_target_pairs={{0,256},{32,288},{64,320},{96,352},{128,384},{160,416},{192,448},{... | collective-permute-start | bytes 221192 | tf_op jit(solution)/shard_map/ppermute | solution.py:449
  126.3 30.8 %all-to-all-start.2 = ((f32[16,8,256]{2,1,0:T(8,128)}), f32[16,8,256]{2,1,0:T(8,128)S(1)}, u32[]{:S(2)}, u32[]{:S(2)}) async-start(f32[16,8,256]{2,1,0:T(8,128)} %get-tuple-element.27), calls=%async_computation.2 | async-start | bytes 262144 | tf_op jit(solution)/shard_map/all_to_all | solution.py:458
  132.2 24.9 %collective-permute-start.6 = (s16[2,144,256]{2,1,0:T(8,128)(2,1)S(1)}, s16[2,144,256]{2,1,0:T(8,128)(2,1)S(1)}, u32[]{:S(2)}, u32[]{:S(2)}) collective-permute-start(s16[2,144,256]{2,1,0:T(8,128)(2,1)S(1)} %get-tuple-element.28.held), channel_id=1, source_target_pairs={{0,128},{32,160},{64,192},{96,224},{128,0},{160,32},{192,64},{224,... | collective-permute-start | bytes 442376 | tf_op jit(solution)/shard_map/ppermute | solution.py:449
  157.1 18.4 %collective-permute-start.7 = (s16[4,144,256]{2,1,0:T(8,128)(2,1)S(1)}, s16[4,144,256]{2,1,0:T(8,128)(2,1)S(1)}, u32[]{:S(2)}, u32[]{:S(2)}) collective-permute-start(s16[4,144,256]{2,1,0:T(8,128)(2,1)S(1)} %get-tuple-element.29.held), channel_id=1, source_target_pairs={{0,64},{32,96},{64,0},{96,32},{128,192},{160,224},{192,128},{224,1... | collective-permute-start | bytes 884744 | tf_op jit(solution)/shard_map/ppermute | solution.py:449
  175.6 16.6 %collective-permute-start.8 = (s16[8,144,256]{2,1,0:T(8,128)(2,1)S(1)}, s16[8,144,256]{2,1,0:T(8,128)(2,1)S(1)}, u32[]{:S(2)}, u32[]{:S(2)}) collective-permute-start(s16[8,144,256]{2,1,0:T(8,128)(2,1)S(1)} %join.1.held), channel_id=1, source_target_pairs={{0,32},{32,0},{64,96},{96,64},{128,160},{160,128},{192,224},{224,1... | collective-permute-start | bytes 1769480 | tf_op jit(solution)/shard_map/ppermute | solution.py:449

commit v6 on v4

--- a/solution.py
+++ b/solution.py
@@ -13,7 +13,13 @@
 BF16 = jnp.bfloat16
 PANEL = 64
 MIB = 1024 * 1024
-DEPTH = ("zh", "zp")
+DEPTH = ("za", "zb", "zc")
+TAIL = 16
+CODE_TOP = 32000.0
+
+
+def position():
+    return 4 * lax.axis_index("za") + 2 * lax.axis_index("zb") + lax.axis_index("zc")
 
 
 def exact_dot(a, b, dims):
@@ -131,7 +137,7 @@
 
 
 def halves_kernel(own, far, near, keep, send):
-    odd = lax.axis_index("zp")
+    odd = lax.axis_index("zc")
     for out, parity in ((keep, odd), (send, 1 - odd)):
         for i in range(out.shape[0]):
             p = 2 * i + parity
@@ -167,16 +173,23 @@
     )(keep, got)
 
 
-def image_kernel(pieces, probes, image, own, sem):
+def image_kernel(pieces, probes, image, coded, own, sem):
     rows = own.shape[0]
-    block = 2 * lax.axis_index("zh") + lax.axis_index("zp")
+    block = position()
     copy = pltpu.make_async_copy(probes.at[pl.ds(block * rows, rows)], own, sem)
     copy.start()
     total = pieces[0].astype(F32)
     for k in range(1, pieces.shape[0]):
         total = total + pieces[k].astype(F32)
     copy.wait()
-    image[...] = own[...].astype(F32) + total.T
+    x = own[...].astype(F32) + total.T
+    image[...] = x
+    top = jnp.maximum(jnp.max(jnp.abs(x), axis=0, keepdims=True), 1e-30)
+    power = jnp.ceil(jnp.log(top) * (1.0 / math.log(2.0)))
+    whole = jnp.floor(x * (jnp.exp2(-power) * CODE_TOP) + 0.5)
+    coded[:rows] = whole.astype(jnp.int32).astype(jnp.int16)
+    tail = jnp.broadcast_to(power, (TAIL, x.shape[1]))
+    coded[rows:] = tail.astype(jnp.int32).astype(jnp.int16)
 
 
 def make_image(pieces, probes):
@@ -184,8 +197,11 @@
     return pl.pallas_call(
         image_kernel,
         in_specs=[in_vmem(), pl.BlockSpec(memory_space=pltpu.HBM)],
-        out_specs=in_vmem(),
-        out_shape=jax.ShapeDtypeStruct((cells, width), F32),
+        out_specs=[in_vmem()] * 2,
+        out_shape=(
+            jax.ShapeDtypeStruct((cells, width), F32),
+            jax.ShapeDtypeStruct((cells + TAIL, width), jnp.int16),
+        ),
         scratch_shapes=[pltpu.VMEM((cells, width), BF16), pltpu.SemaphoreType.DMA],
         compiler_params=params(4),
         name="make_image",
@@ -208,12 +224,16 @@
     )(image)
 
 
-def spread_sum_kernel(pieces, out):
+def spread(pieces, out):
     total = pieces[0]
     for k in range(1, pieces.shape[0]):
         total = total + pieces[k]
     for k in range(out.shape[0]):
         out[k] = total
+
+
+def spread_sum_kernel(pieces, out):
+    spread(pieces, out)
 
 
 def spread_sum(pieces, copies):
@@ -337,26 +357,48 @@
     )(gram)
 
 
-def basis_kernel(image, high, low, out):
-    x = image[...]
-    x_high = x.astype(BF16)
-    x_low = (x - x_high.astype(F32)).astype(BF16)
+def basis_kernel(*refs):
+    parts, (high, low, out, staged, sems) = refs[:4], refs[4:]
+    rows, width = staged.shape[2:]
+    here = position()
     dot = functools.partial(jnp.dot, preferred_element_type=F32)
-    out[...] = dot(x_high, high[...]) + (dot(x_high, low[...]) + dot(x_low, high[...]))
-
-
-def make_basis(image, high, low):
-    rows, width = image.shape
-    half = pl.BlockSpec((rows // 2, width), lambda h: (h, 0))
+    copies = []
+    for g, part in enumerate(parts):
+        pieces = []
+        for i in range(4):
+            power = part[i, rows:].astype(jnp.int32).astype(F32)[:1]
+            piece = part[i, :rows].astype(jnp.int32).astype(F32)
+            pieces.append(piece * (jnp.exp2(power) * (1.0 / CODE_TOP)))
+        x = jnp.concatenate(pieces, axis=0)
+        x_high = x.astype(BF16)
+        x_low = (x - x_high.astype(F32)).astype(BF16)
+        y = dot(x_high, high[...]) + (dot(x_high, low[...]) + dot(x_low, high[...]))
+        staged[g] = y.reshape(4, rows, width)
+        for i in range(4):
+            source = 4 * i + ((here % 4) ^ g)
+            to = pl.ds(pl.multiple_of(source * rows, rows), rows)
+            copy = pltpu.make_async_copy(staged.at[g, i], out.at[to], sems.at[4 * g + i])
+            copy.start()
+            copies.append(copy)
+    for copy in copies:
+        copy.wait()
+
+
+def make_basis(parts, high, low):
+    count, rows, width = parts[0].shape
+    rows -= TAIL
     return pl.pallas_call(
         basis_kernel,
-        grid=(2,),
-        in_specs=[half, in_vmem(), in_vmem()],
-        out_specs=half,
-        out_shape=jax.ShapeDtypeStruct((rows, width), F32),
-        compiler_params=params(60),
+        in_specs=[in_vmem()] * 6,
+        out_specs=pl.BlockSpec(memory_space=pltpu.HBM),
+        out_shape=jax.ShapeDtypeStruct((4 * count * rows, width), F32),
+        scratch_shapes=[
+            pltpu.VMEM((4, count, rows, width), F32),
+            pltpu.SemaphoreType.DMA((4 * count,)),
+        ],
+        compiler_params=params(16),
         name="make_basis",
-    )(image, high, low)
+    )(*parts, high, low)
 
 
 def paired(value, axis, first):
@@ -377,25 +419,30 @@
     from_far = paired(to_far, "brick", 1)
     from_near = paired(to_near, "brick", 0)
 
-    n = lax.axis_size("zh") * lax.axis_size("zp")
+    n = lax.axis_size(DEPTH)
     keep, send = split_halves(own, from_far, from_near)
-    got = lax.ppermute(send, DEPTH, [(i, i ^ 1) for i in range(n)])
-    image = make_image(lax.all_to_all(add_pair(keep, got), "zh", 0, 0), probes)
-    whole_image = lax.all_gather(image, DEPTH, tiled=True)
+
+    def swap(held, distance):
+        return lax.ppermute(held, DEPTH, [(i, i ^ distance) for i in range(n)])
+
+    held = add_pair(keep, swap(send, 1))
+    image, coded = make_image(lax.all_to_all(held, ("za", "zb"), 0, 0), probes)
+
+    held = lax.all_gather(coded, "za")
     gram = make_gram(image)
-
     bricks = lax.axis_size("brick")
     share = lax.all_to_all(gram.reshape(bricks, width // bricks, width), "brick", 0, 0)
     share = lax.all_to_all(spread_sum(share, n), DEPTH, 0, 0)
+    parts = [held] + [swap(held, k) for k in (1, 2, 3)]
     gram = lax.all_to_all(spread_sum(share, bricks), "brick", 0, 0).reshape(width, width)
 
     scale = math.sqrt(rows * bricks)
     upper, high, low = cholesky_and_inverse(gram, scale)
-    return make_basis(whole_image, high, low), upper
+    return make_basis(parts, high, low), upper
 
 
 def solution(mesh):
-    deep = mesh.devices.reshape(mesh.devices.shape[0] // 2, 2, mesh.devices.shape[1])
+    deep = mesh.devices.reshape(mesh.devices.shape[0] // 4, 2, 2, mesh.devices.shape[1])
     mesh = Mesh(deep, DEPTH + ("brick",))
     in_specs = (P("brick", None), P(DEPTH, "brick", None, None, None), P(DEPTH, "brick", None))
     out_specs = (P("brick", None), P())

time: 189 us -> 183 us (0.968)
  the two profiles are of different devices: /device:TPU:12 before, /device:TPU:1 now
where the time goes in v6:
time: 183 us; the launch traced here: 182 us
  blocking collectives  107 us (58%)
  starting transfers between devices  32.4 us (18%)
  Pallas kernels  19.2 us (10%)
  waiting for transfers between devices  19 us (10%)
  local copies, waits for them, and re-layouts  3.96 us (2%)
    all_to_all x1, blocking collectives, body(): image, coded = make_image(lax.all_to_all(held, ('za', 'zb'), 0, 0), probes)  41.2 us
    all_to_all x1, blocking collectives, body(): lax.all_to_all(gram.reshape(bricks, width // bricks, width), 'brick', 0, 0)  25.9 us
    all_gather x1, blocking collectives, body(): held = lax.all_gather(coded, 'za')  24.8 us
    ppermute x4, starting transfers between devices, paired(): return lax.ppermute(value, axis, pairs + [(j, i) for i, j in pairs])  15.1 us
    all_to_all x1, blocking collectives, body(): lax.all_to_all(spread_sum(share, bricks), 'brick', 0, 0)  14.7 us
    ppermute x4, starting transfers between devices, swap(): return lax.ppermute(held, DEPTH, [(i, i ^ distance) for i in range(n)])  12.9 us
    ppermute x4, waiting for transfers between devices, paired(): return lax.ppermute(value, axis, pairs + [(j, i) for i, j in pairs])  12.5 us
    pallas_call x1, Pallas kernels, cholesky_and_inverse(): pl.pallas_call(functools.partial(factor_kernel, scale), in_specs=[in_vmem...  9 us
  transfers between devices with their start and end apart: 9, of which 3 were waited for; matrix products, arithmetic and copies ran while one was open for 0% of the time, Pallas kernels for 6%

profile of v6, /device:TPU:1, one launch (start us, length us, event | category | flops | bytes accessed | tf_op | source)
XLA Modules:
  0.0 182.1 jit_solution(4570460758875006245)
XLA Ops:
  0.6 4.5 %collective-permute-start = (bf16[2048,256]{1,0:T(8,128)(2,1)}, bf16[2048,256]{1,0:T(8,128)(2,1)S(1)}, u32[]{:S(2)}, u32[]{:S(2)}) collective-permute-start(bf16[2048,256]{1,0:T(8,128)(2,1)} %probes.1), channel_id=1, source_target_pairs={{1,2},{3,4},{5,6},{7,8},{9,10},{11,12},{13,14},{15,16},{17,18},{19... | collective-permute-start | bytes 3145736 | tf_op jit(solution)/shard_map/ppermute | solution.py:406
  5.1 5.0 %collective-permute-start.1 = (bf16[2048,256]{1,0:T(8,128)(2,1)}, bf16[2048,256]{1,0:T(8,128)(2,1)S(1)}, u32[]{:S(2)}, u32[]{:S(2)}) collective-permute-start(bf16[2048,256]{1,0:T(8,128)(2,1)} %probes.1), channel_id=1, source_target_pairs={{0,1},{2,3},{4,5},{6,7},{8,9},{10,11},{12,13},{14,15},{16,17},{18,... | collective-permute-start | bytes 3145736 | tf_op jit(solution)/shard_map/ppermute | solution.py:406
  10.2 0.8 copy.6
  10.9 0.1 reshape.22.cols
  11.0 0.0 copy-start
  11.0 1.2 copy-done
  12.2 0.0 copy-start.2
  12.2 1.9 %copy-done.2 = bf16[1,8,3,256,256]{4,3,2,1,0:T(8,128)(2,1)S(1)} copy-done((bf16[1,8,3,256,256]{4,3,2,1,0:T(8,128)(2,1)S(1)}, bf16[1,8,3,256,256]{4,3,2,1,0:T(8,128)(2,1)}, u32[]{:S(2)}) %copy-start.2) | copy-done | bytes 3145752
  14.1 2.1 %own_data.1 = (bf16[8,3,256,256]{3,2,1,0:T(8,128)(2,1)S(1)}, f32[8,256,256]{2,1,0:T(8,128)S(1)}) custom-call(s32[24]{0:T(128)S(1)} %reshape.22.cols, bf16[8,3,256,256]{3,2,1,0:T(8,128)(2,1)S(1)} %bitcast.8, bf16[8,256,256]{2,1,0:T(8,128)(2,1)S(1)} %bitcast.7), custom_call_target="tpu_custom_call" | custom-call | flops 268435456 | bytes 9437184 | tf_op jit(solution)/shard_map/own_data/pallas_call | solution.py:66
  16.2 1.6 collective-permute-done
  17.8 0.0 collective-permute-done.1
  17.8 4.0 %normal_operator.1 = (f32[16,256,128]{2,1,0:T(8,128)S(1)}, bf16[16,256,128]{2,1,0:T(8,128)(2,1)S(1)}, bf16[16,256,128]{2,1,0:T(8,128)(2,1)S(1)}) custom-call(s32[24]{0:T(128)S(1)} %reshape.22.cols, bf16[8,3,256,256]{3,2,1,0:T(8,128)(2,1)S(1)} %get-tuple-element.14.w_ref, f32[8,256,256]{2,1,0:T(8,128)S(1)} %get-tuple-element.15.data_ref, ...), custom_call_target="tpu_custom_call" | custom-call | tf_op jit(solution)/shard_map/normal_operator/pallas_call | solution.py:124
  21.8 3.6 %collective-permute-start.2 = (bf16[16,256,128]{2,1,0:T(8,128)(2,1)S(1)}, bf16[16,256,128]{2,1,0:T(8,128)(2,1)S(1)}, u32[]{:S(2)}, u32[]{:S(2)}) collective-permute-start(bf16[16,256,128]{2,1,0:T(8,128)(2,1)S(1)} %get-tuple-element.17), channel_id=1, source_target_pairs={{1,2},{3,4},{5,6},{7,8},{9,10},{11,12},{13,14},{15,16},{17,18},{19... | collective-permute-start | bytes 3145736 | tf_op jit(solution)/shard_map/ppermute | solution.py:406
  25.5 1.9 %collective-permute-start.3 = (bf16[16,256,128]{2,1,0:T(8,128)(2,1)S(1)}, bf16[16,256,128]{2,1,0:T(8,128)(2,1)S(1)}, u32[]{:S(2)}, u32[]{:S(2)}) collective-permute-start(bf16[16,256,128]{2,1,0:T(8,128)(2,1)S(1)} %get-tuple-element.18), channel_id=1, source_target_pairs={{0,1},{2,3},{4,5},{6,7},{8,9},{10,11},{12,13},{14,15},{16,17},{18,... | collective-permute-start | bytes 3145736 | tf_op jit(solution)/shard_map/ppermute | solution.py:406
  27.4 10.8 %collective-permute-done.2.far = bf16[16,256,128]{2,1,0:T(8,128)(2,1)S(1)} collective-permute-done((bf16[16,256,128]{2,1,0:T(8,128)(2,1)S(1)}, bf16[16,256,128]{2,1,0:T(8,128)(2,1)S(1)}, u32[]{:S(2)}, u32[]{:S(2)}) %collective-permute-start.2) | collective-permute-done | bytes 1048608 | tf_op jit(solution)/shard_map/ppermute | solution.py:406
  38.2 0.0 collective-permute-done.3.near
  38.2 0.4 split_halves.1
  38.6 0.0 copy-start.1
  38.6 3.7 %collective-permute-start.4 = (bf16[8,256,128]{2,1,0:T(8,128)(2,1)S(1)}, bf16[8,256,128]{2,1,0:T(8,128)(2,1)S(1)}, u32[]{:S(2)}, u32[]{:S(2)}) collective-permute-start(bf16[8,256,128]{2,1,0:T(8,128)(2,1)S(1)} %get-tuple-element.20), channel_id=1, source_target_pairs={{0,32},{32,0},{64,96},{96,64},{128,160},{160,128},{192,224},{224,1... | collective-permute-start | bytes 1572872 | tf_op jit(solution)/shard_map/ppermute | solution.py:426
  42.3 6.6 %collective-permute-done.4.got = bf16[8,256,128]{2,1,0:T(8,128)(2,1)S(1)} collective-permute-done((bf16[8,256,128]{2,1,0:T(8,128)(2,1)S(1)}, bf16[8,256,128]{2,1,0:T(8,128)(2,1)S(1)}, u32[]{:S(2)}, u32[]{:S(2)}) %collective-permute-start.4) | collective-permute-done | bytes 524320 | tf_op jit(solution)/shard_map/ppermute | solution.py:426
  48.9 0.1 add_pair.1
  49.0 41.2 %all_to_all.20.pieces = bf16[8,256,128]{2,1,0:T(8,128)(2,1)S(1)} all-to-all(bf16[8,256,128]{2,1,0:T(8,128)(2,1)S(1)} %add_pair.1), channel_id=1, replica_groups=mesh['za'=4,'zb'=2,'zc'=2,'brick'=32] {'za','zb'}, dimensions={0} | all-to-all | bytes 1048576 | tf_op jit(solution)/shard_map/all_to_all | solution.py:429
  90.1 0.0 copy-done.1
  90.2 0.3 make_image.1
  90.5 0.4 make_gram.1
  90.9 25.9 %all_to_all.21.pieces = f32[32,8,256]{2,1,0:T(8,128)S(1)} all-to-all(f32[32,8,256]{2,1,0:T(8,128)S(1)} %bitcast.14), channel_id=1, replica_groups=mesh['za'=4,'zb'=2,'zc'=2,'brick'=32] {'brick'}, dimensions={0} | all-to-all | bytes 524288 | tf_op jit(solution)/shard_map/all_to_all | solution.py:434
  116.8 0.7 spread_sum.2
  117.5 4.4 %all-to-all-start.2 = ((f32[16,8,256]{2,1,0:T(8,128)}), f32[16,8,256]{2,1,0:T(8,128)S(1)}, u32[]{:S(2)}, u32[]{:S(2)}) async-start(f32[16,8,256]{2,1,0:T(8,128)} %spread_sum.2), calls=%async_computation.2 | async-start | bytes 262144 | tf_op jit(solution)/shard_map/all_to_all | solution.py:435
  121.9 24.8 %all-gather = s16[576,256]{1,0:T(8,128)(2,1)S(1)} all-gather(s16[144,256]{1,0:T(8,128)(2,1)S(1)} %get-tuple-element.21), channel_id=2, replica_groups=mesh['za'=4,'zb'=2,'zc'=2,'brick'=32] {'za'}, dimensions={0}, use_global_device_ids=true | all-gather | bytes 368640 | tf_op jit(solution)/shard_map/all_gather | solution.py:431
  146.7 4.3 %collective-permute-start.7 = (s16[4,144,256]{2,1,0:T(8,128)(2,1)S(1)}, s16[4,144,256]{2,1,0:T(8,128)(2,1)S(1)}, u32[]{:S(2)}, u32[]{:S(2)}) collective-permute-start(s16[4,144,256]{2,1,0:T(8,128)(2,1)S(1)} %bitcast.9), channel_id=1, source_target_pairs={{0,96},{32,64},{64,32},{96,0},{128,224},{160,192},{192,160},{224,1... | collective-permute-start | bytes 884744 | tf_op jit(solution)/shard_map/ppermute | solution.py:426
  150.9 2.1 %collective-permute-start.6 = (s16[4,144,256]{2,1,0:T(8,128)(2,1)S(1)}, s16[4,144,256]{2,1,0:T(8,128)(2,1)S(1)}, u32[]{:S(2)}, u32[]{:S(2)}) collective-permute-start(s16[4,144,256]{2,1,0:T(8,128)(2,1)S(1)} %bitcast.10), channel_id=1, source_target_pairs={{0,64},{32,96},{64,0},{96,32},{128,192},{160,224},{192,128},{224,1... | collective-permute-start | bytes 884744 | tf_op jit(solution)/shard_map/ppermute | solution.py:426
  153.0 2.9 %collective-permute-start.5 = (s16[4,144,256]{2,1,0:T(8,128)(2,1)S(1)}, s16[4,144,256]{2,1,0:T(8,128)(2,1)S(1)}, u32[]{:S(2)}, u32[]{:S(2)}) collective-permute-start(s16[4,144,256]{2,1,0:T(8,128)(2,1)S(1)} %bitcast.11), channel_id=1, source_target_pairs={{0,32},{32,0},{64,96},{96,64},{128,160},{160,128},{192,224},{224,1... | collective-permute-start | bytes 884744 | tf_op jit(solution)/shard_map/ppermute | solution.py:426
  155.9 0.0 all-to-all-done.2.pieces
  156.0 14.7 %all_to_all.22 = f32[32,8,256]{2,1,0:T(8,128)S(1)} all-to-all(f32[32,8,256]{2,1,0:T(8,128)S(1)} %spread_sum.3), channel_id=1, replica_groups=mesh['za'=4,'zb'=2,'zc'=2,'brick'=32] {'brick'}, dimensions={0} | all-to-all | bytes 524288 | tf_op jit(solution)/shard_map/all_to_all | solution.py:437
  170.7 9.0 %cholesky_and_inverse.1 = (f32[256,256]{1,0:T(8,128)}, bf16[256,256]{1,0:T(8,128)(2,1)S(1)}, bf16[256,256]{1,0:T(8,128)(2,1)S(1)}) custom-call(f32[256,256]{1,0:T(8,128)S(1)} %bitcast.13), custom_call_target="tpu_custom_call" | custom-call | tf_op jit(solution)/shard_map/cholesky_and_inverse/pallas_call | solution.py:349
  179.7 0.0 collective-permute-done.7.refs_3_
  179.7 0.0 collective-permute-done.6.refs_2_
  179.7 0.0 collective-permute-done.5.refs_1_
  179.7 2.3 %make_basis.1 = f32[2048,256]{1,0:T(8,128)} custom-call(s16[4,144,256]{2,1,0:T(8,128)(2,1)S(1)} %bitcast.12, s16[4,144,256]{2,1,0:T(8,128)(2,1)S(1)} %collective-permute-done.5.refs_1_, s16[4,144,256]{2,1,0:T(8,128)(2,1)S(1)} %collective-permute-done.6.refs_2_, s16[4,144,256]{2,1,0:T(8,128)(2,1)S(1)} %collective-permute-done.7.refs_3_, ...), custom_call_target="tpu_custom_call" | custom-call | tf_op jit(solution)/shard_map/make_basis/pallas_call | solution.py:390
  (1 shorter events, 0.0 us)
Async XLA Ops:
  0.6 17.2 %collective-permute-start = (bf16[2048,256]{1,0:T(8,128)(2,1)}, bf16[2048,256]{1,0:T(8,128)(2,1)S(1)}, u32[]{:S(2)}, u32[]{:S(2)}) collective-permute-start(bf16[2048,256]{1,0:T(8,128)(2,1)} %probes.1), channel_id=1, source_target_pairs={{1,2},{3,4},{5,6},{7,8},{9,10},{11,12},{13,14},{15,16},{17,18},{19... | collective-permute-start | bytes 3145736 | tf_op jit(solution)/shard_map/ppermute | solution.py:406
  5.1 12.7 %collective-permute-start.1 = (bf16[2048,256]{1,0:T(8,128)(2,1)}, bf16[2048,256]{1,0:T(8,128)(2,1)S(1)}, u32[]{:S(2)}, u32[]{:S(2)}) collective-permute-start(bf16[2048,256]{1,0:T(8,128)(2,1)} %probes.1), channel_id=1, source_target_pairs={{0,1},{2,3},{4,5},{6,7},{8,9},{10,11},{12,13},{14,15},{16,17},{18,... | collective-permute-start | bytes 3145736 | tf_op jit(solution)/shard_map/ppermute | solution.py:406
  11.0 1.2 copy-start
  12.2 1.9 %copy-start.2 = (bf16[1,8,3,256,256]{4,3,2,1,0:T(8,128)(2,1)S(1)}, bf16[1,8,3,256,256]{4,3,2,1,0:T(8,128)(2,1)}, u32[]{:S(2)}) copy-start(bf16[1,8,3,256,256]{4,3,2,1,0:T(8,128)(2,1)} %param.4) | copy-start | bytes 9437188
  21.8 16.4 %collective-permute-start.2 = (bf16[16,256,128]{2,1,0:T(8,128)(2,1)S(1)}, bf16[16,256,128]{2,1,0:T(8,128)(2,1)S(1)}, u32[]{:S(2)}, u32[]{:S(2)}) collective-permute-start(bf16[16,256,128]{2,1,0:T(8,128)(2,1)S(1)} %get-tuple-element.17), channel_id=1, source_target_pairs={{1,2},{3,4},{5,6},{7,8},{9,10},{11,12},{13,14},{15,16},{17,18},{19... | collective-permute-start | bytes 3145736 | tf_op jit(solution)/shard_map/ppermute | solution.py:406
  25.5 12.8 %collective-permute-start.3 = (bf16[16,256,128]{2,1,0:T(8,128)(2,1)S(1)}, bf16[16,256,128]{2,1,0:T(8,128)(2,1)S(1)}, u32[]{:S(2)}, u32[]{:S(2)}) collective-permute-start(bf16[16,256,128]{2,1,0:T(8,128)(2,1)S(1)} %get-tuple-element.18), channel_id=1, source_target_pairs={{0,1},{2,3},{4,5},{6,7},{8,9},{10,11},{12,13},{14,15},{16,17},{18,... | collective-permute-start | bytes 3145736 | tf_op jit(solution)/shard_map/ppermute | solution.py:406
  38.6 51.5 %copy-start.1 = (bf16[2048,256]{1,0:T(8,128)(2,1)S(1)}, bf16[2048,256]{1,0:T(8,128)(2,1)}, u32[]{:S(2)}) copy-start(bf16[2048,256]{1,0:T(8,128)(2,1)} %probes.1) | copy-start | bytes 3145732
  38.6 10.2 %collective-permute-start.4 = (bf16[8,256,128]{2,1,0:T(8,128)(2,1)S(1)}, bf16[8,256,128]{2,1,0:T(8,128)(2,1)S(1)}, u32[]{:S(2)}, u32[]{:S(2)}) collective-permute-start(bf16[8,256,128]{2,1,0:T(8,128)(2,1)S(1)} %get-tuple-element.20), channel_id=1, source_target_pairs={{0,32},{32,0},{64,96},{96,64},{128,160},{160,128},{192,224},{224,1... | collective-permute-start | bytes 1572872 | tf_op jit(solution)/shard_map/ppermute | solution.py:426
  117.5 38.5 %all-to-all-start.2 = ((f32[16,8,256]{2,1,0:T(8,128)}), f32[16,8,256]{2,1,0:T(8,128)S(1)}, u32[]{:S(2)}, u32[]{:S(2)}) async-start(f32[16,8,256]{2,1,0:T(8,128)} %spread_sum.2), calls=%async_computation.2 | async-start | bytes 262144 | tf_op jit(solution)/shard_map/all_to_all | solution.py:435
  146.7 33.0 %collective-permute-start.7 = (s16[4,144,256]{2,1,0:T(8,128)(2,1)S(1)}, s16[4,144,256]{2,1,0:T(8,128)(2,1)S(1)}, u32[]{:S(2)}, u32[]{:S(2)}) collective-permute-start(s16[4,144,256]{2,1,0:T(8,128)(2,1)S(1)} %bitcast.9), channel_id=1, source_target_pairs={{0,96},{32,64},{64,32},{96,0},{128,224},{160,192},{192,160},{224,1... | collective-permute-start | bytes 884744 | tf_op jit(solution)/shard_map/ppermute | solution.py:426
  150.9 28.7 %collective-permute-start.6 = (s16[4,144,256]{2,1,0:T(8,128)(2,1)S(1)}, s16[4,144,256]{2,1,0:T(8,128)(2,1)S(1)}, u32[]{:S(2)}, u32[]{:S(2)}) collective-permute-start(s16[4,144,256]{2,1,0:T(8,128)(2,1)S(1)} %bitcast.10), channel_id=1, source_target_pairs={{0,64},{32,96},{64,0},{96,32},{128,192},{160,224},{192,128},{224,1... | collective-permute-start | bytes 884744 | tf_op jit(solution)/shard_map/ppermute | solution.py:426
  153.0 26.7 %collective-permute-start.5 = (s16[4,144,256]{2,1,0:T(8,128)(2,1)S(1)}, s16[4,144,256]{2,1,0:T(8,128)(2,1)S(1)}, u32[]{:S(2)}, u32[]{:S(2)}) collective-permute-start(s16[4,144,256]{2,1,0:T(8,128)(2,1)S(1)} %bitcast.11), channel_id=1, source_target_pairs={{0,32},{32,0},{64,96},{96,64},{128,160},{160,128},{192,224},{224,1... | collective-permute-start | bytes 884744 | tf_op jit(solution)/shard_map/ppermute | solution.py:426

commit v7 on v6

--- a/solution.py
+++ b/solution.py
@@ -79,7 +79,9 @@
     )(cols, weights, own)
 
 
-def operator_kernel(cols, w_ref, data_ref, far_ref, near_ref, own_out, far_out, near_out, s_far, s_near, d_ref):
+def operator_kernel(
+    cols, w_ref, data_ref, far_ref, near_ref, own_out, far_first, far_last, near_out, s_far, s_near, d_ref
+):
     blocks, _, bs, _ = w_ref.shape
     dot = functools.partial(jnp.dot, preferred_element_type=F32)
     s_far[...] = jnp.zeros_like(s_far)
@@ -110,24 +112,28 @@
 
     lax.fori_loop(0, blocks - 1, step, 0)
     put(blocks - 1)
-    for field, out in ((s_far, far_out), (s_near, near_out)):
-        for q in range(blocks):
-            out[2 * q] = field[q, :, :128].astype(BF16)
-            out[2 * q + 1] = field[q, :, 128:].astype(BF16)
+    half = blocks // 2
+    for q in range(blocks):
+        far_out = far_first if q < half else far_last
+        for out, k, field in ((far_out, q % half, s_far), (near_out, q, s_near)):
+            out[2 * k] = field[q, :, :128].astype(BF16)
+            out[2 * k + 1] = field[q, :, 128:].astype(BF16)
 
 
 def finish_operator(cols, weights, data, far, near):
     blocks, _, bs, _ = weights.shape
     width = data.shape[-1]
     shape = (2 * blocks, width, bs // 2)
+    half = jax.ShapeDtypeStruct((blocks, width, bs // 2), BF16)
     field = pltpu.VMEM((blocks, width, bs), F32)
     return pl.pallas_call(
         operator_kernel,
         in_specs=[pl.BlockSpec(memory_space=pltpu.SMEM)] + [in_vmem()] * 4,
-        out_specs=[in_vmem()] * 3,
+        out_specs=[in_vmem()] * 4,
         out_shape=(
             jax.ShapeDtypeStruct(shape, F32),
-            jax.ShapeDtypeStruct(shape, BF16),
+            half,
+            half,
             jax.ShapeDtypeStruct(shape, BF16),
         ),
         scratch_shapes=[field, field, pltpu.VMEM((2, width, bs), BF16)],
@@ -136,41 +142,45 @@
     )(cols, weights, data, far, near)
 
 
-def halves_kernel(own, far, near, keep, send):
+def parity_kernel(first, own, far, near, keep, send):
     odd = lax.axis_index("zc")
     for out, parity in ((keep, odd), (send, 1 - odd)):
         for i in range(out.shape[0]):
             p = 2 * i + parity
-            out[i] = (own[p] + (far[p].astype(F32) + near[p].astype(F32))).astype(out.dtype)
-
-
-def split_halves(own, far, near):
-    pieces, width, cells = own.shape
+            total = far[p].astype(F32) + near[first + p].astype(F32)
+            out[i] = (own[first + p] + total).astype(out.dtype)
+
+
+def split_parity(first, own, far, near):
+    pieces, width, cells = far.shape
     kept, sent = (jax.ShapeDtypeStruct((pieces // 2, width, cells), t) for t in (F32, BF16))
     return pl.pallas_call(
-        halves_kernel,
+        functools.partial(parity_kernel, first),
         in_specs=[in_vmem()] * 3,
         out_specs=[in_vmem()] * 2,
         out_shape=(kept, sent),
         compiler_params=params(12),
-        name="split_halves",
+        name="split_parity",
     )(own, far, near)
 
 
-def pair_kernel(keep, got, out):
-    for i in range(out.shape[0]):
+def pair_kernel(keep, got, keep_last, got_last, out):
+    n = keep.shape[0]
+    for i in range(n):
         out[i] = (keep[i] + got[i].astype(F32)).astype(BF16)
-
-
-def add_pair(keep, got):
+        out[n + i] = (keep_last[i] + got_last[i].astype(F32)).astype(BF16)
+
+
+def add_pair(*halves):
+    n, width, cells = halves[0].shape
     return pl.pallas_call(
         pair_kernel,
-        in_specs=[in_vmem()] * 2,
+        in_specs=[in_vmem()] * 4,
         out_specs=in_vmem(),
-        out_shape=jax.ShapeDtypeStruct(keep.shape, BF16),
+        out_shape=jax.ShapeDtypeStruct((2 * n, width, cells), BF16),
         compiler_params=params(8),
         name="add_pair",
-    )(keep, got)
+    )(*halves)
 
 
 def image_kernel(pieces, probes, image, coded, own, sem):
@@ -415,17 +425,20 @@
     shape = (blocks, bs, width)
     cols = columns.reshape(-1)
     w_sorted, own_data = start_operator(cols, w_local, probes.reshape(shape))
-    own, to_far, to_near = finish_operator(cols, w_sorted, own_data, far.reshape(shape), near.reshape(shape))
-    from_far = paired(to_far, "brick", 1)
-    from_near = paired(to_near, "brick", 0)
+    own, *to_far, to_near = finish_operator(cols, w_sorted, own_data, far.reshape(shape), near.reshape(shape))
 
     n = lax.axis_size(DEPTH)
-    keep, send = split_halves(own, from_far, from_near)
 
     def swap(held, distance):
         return lax.ppermute(held, DEPTH, [(i, i ^ distance) for i in range(n)])
 
-    held = add_pair(keep, swap(send, 1))
+    from_far = [paired(to_far[0], "brick", 1), paired(to_far[1], "brick", 1)]
+    from_near = paired(to_near, "brick", 0)
+    halves = []
+    for k, part in enumerate(from_far):
+        keep, send = split_parity(k * part.shape[0], own, part, from_near)
+        halves += [keep, swap(send, 1)]
+    held = add_pair(*halves)
     image, coded = make_image(lax.all_to_all(held, ("za", "zb"), 0, 0), probes)
 
     held = lax.all_gather(coded, "za")

time: 183 us -> 182 us (level)
  starting transfers between devices: 32.4 us -> 39.7 us
  waiting for transfers between devices: 19 us -> 12.1 us
  blocking collectives: 107 us -> 105 us
    ppermute x4 -> x5, waiting for transfers between devices: 12.5 us -> 8.34 us  [paired(): return lax.ppermute(value, axis, pairs + [(j, i) for i, j in pairs])]
    ppermute x4 -> x5, starting transfers between devices: 12.9 us -> 16.6 us  [swap(): return lax.ppermute(held, DEPTH, [(i, i ^ distance) for i in range(n)])]
    ppermute x4 -> x5, waiting for transfers between devices: 6.56 us -> 3.75 us  [swap(): return lax.ppermute(held, DEPTH, [(i, i ^ distance) for i in range(n)])]
    all_to_all x1, blocking collectives: 41.2 us -> 39 us  [body(): image, coded = make_image(lax.all_to_all(held, ('za', 'zb'), 0, 0), probes)]
    ppermute x4 -> x5, starting transfers between devices: 15.1 us -> 17.1 us  [paired(): return lax.ppermute(value, axis, pairs + [(j, i) for i, j in pairs])]
  transfers between devices with their start and end apart: 9 -> 11, of which waited for: 3 -> 4; matrix products, arithmetic and copies ran while one was open for 0% -> 0% of each run, Pallas kernels for 6% -> 6%
where the time goes in v7:
time: 182 us; the launch traced here: 181 us
  blocking collectives  105 us (58%)
  starting transfers between devices  39.7 us (22%)
  Pallas kernels  19.2 us (11%)
  waiting for transfers between devices  12.1 us (7%)
  local copies, waits for them, and re-layouts  3.96 us (2%)
    all_to_all x1, blocking collectives, body(): image, coded = make_image(lax.all_to_all(held, ('za', 'zb'), 0, 0), probes)  39 us
    all_to_all x1, blocking collectives, body(): lax.all_to_all(gram.reshape(bricks, width // bricks, width), 'brick', 0, 0)  26.9 us
    all_gather x1, blocking collectives, body(): held = lax.all_gather(coded, 'za')  24.8 us
    ppermute x5, starting transfers between devices, paired(): return lax.ppermute(value, axis, pairs + [(j, i) for i, j in pairs])  17.1 us
    ppermute x5, starting transfers between devices, swap(): return lax.ppermute(held, DEPTH, [(i, i ^ distance) for i in range(n)])  16.6 us
    all_to_all x1, blocking collectives, body(): lax.all_to_all(spread_sum(share, bricks), 'brick', 0, 0)  14.7 us
    pallas_call x1, Pallas kernels, cholesky_and_inverse(): pl.pallas_call(functools.partial(factor_kernel, scale), in_specs=[in_vmem...  9 us
    ppermute x5, waiting for transfers between devices, paired(): return lax.ppermute(value, axis, pairs + [(j, i) for i, j in pairs])  8.34 us
  transfers between devices with their start and end apart: 11, of which 4 were waited for; matrix products, arithmetic and copies ran while one was open for 0% of the time, Pallas kernels for 6%

profile of v7, /device:TPU:1, one launch (start us, length us, event | category | flops | bytes accessed | tf_op | source)
XLA Modules:
  0.0 181.3 jit_solution(2550896779108802209)
XLA Ops:
  0.6 4.5 %collective-permute-start = (bf16[2048,256]{1,0:T(8,128)(2,1)}, bf16[2048,256]{1,0:T(8,128)(2,1)S(1)}, u32[]{:S(2)}, u32[]{:S(2)}) collective-permute-start(bf16[2048,256]{1,0:T(8,128)(2,1)} %probes.1), channel_id=1, source_target_pairs={{1,2},{3,4},{5,6},{7,8},{9,10},{11,12},{13,14},{15,16},{17,18},{19... | collective-permute-start | bytes 3145736 | tf_op jit(solution)/shard_map/ppermute | solution.py:416
  5.1 5.0 %collective-permute-start.1 = (bf16[2048,256]{1,0:T(8,128)(2,1)}, bf16[2048,256]{1,0:T(8,128)(2,1)S(1)}, u32[]{:S(2)}, u32[]{:S(2)}) collective-permute-start(bf16[2048,256]{1,0:T(8,128)(2,1)} %probes.1), channel_id=1, source_target_pairs={{0,1},{2,3},{4,5},{6,7},{8,9},{10,11},{12,13},{14,15},{16,17},{18,... | collective-permute-start | bytes 3145736 | tf_op jit(solution)/shard_map/ppermute | solution.py:416
  10.2 0.8 copy.6
  10.9 0.1 reshape.22.cols
  11.0 0.0 copy-start
  11.0 1.2 copy-done
  12.2 0.0 copy-start.2
  12.2 1.9 %copy-done.2 = bf16[1,8,3,256,256]{4,3,2,1,0:T(8,128)(2,1)S(1)} copy-done((bf16[1,8,3,256,256]{4,3,2,1,0:T(8,128)(2,1)S(1)}, bf16[1,8,3,256,256]{4,3,2,1,0:T(8,128)(2,1)}, u32[]{:S(2)}) %copy-start.2) | copy-done | bytes 3145752
  14.1 2.1 %own_data.1 = (bf16[8,3,256,256]{3,2,1,0:T(8,128)(2,1)S(1)}, f32[8,256,256]{2,1,0:T(8,128)S(1)}) custom-call(s32[24]{0:T(128)S(1)} %reshape.22.cols, bf16[8,3,256,256]{3,2,1,0:T(8,128)(2,1)S(1)} %bitcast.8, bf16[8,256,256]{2,1,0:T(8,128)(2,1)S(1)} %bitcast.7), custom_call_target="tpu_custom_call" | custom-call | flops 268435456 | bytes 9437184 | tf_op jit(solution)/shard_map/own_data/pallas_call | solution.py:66
  16.2 1.6 collective-permute-done
  17.8 0.0 collective-permute-done.1
  17.8 4.0 %normal_operator.1 = (f32[16,256,128]{2,1,0:T(8,128)S(1)}, bf16[8,256,128]{2,1,0:T(8,128)(2,1)S(1)}, bf16[8,256,128]{2,1,0:T(8,128)(2,1)S(1)}, bf16[16,256,128]{2,1,0:T(8,128)(2,1)S(1)}) custom-call(s32[24]{0:T(128)S(1)} %reshape.22.cols, bf16[8,3,256,256]{3,2,1,0:T(8,128)(2,1)S(1)} %get-tuple-element.17.w_ref, ...), custom_call_target="tpu_custom_call" | custom-call | tf_op jit(solution)/shard_map/normal_operator/pallas_call | solution.py:129
  21.8 1.9 %collective-permute-start.3 = (bf16[16,256,128]{2,1,0:T(8,128)(2,1)S(1)}, bf16[16,256,128]{2,1,0:T(8,128)(2,1)S(1)}, u32[]{:S(2)}, u32[]{:S(2)}) collective-permute-start(bf16[16,256,128]{2,1,0:T(8,128)(2,1)S(1)} %get-tuple-element.21), channel_id=1, source_target_pairs={{0,1},{2,3},{4,5},{6,7},{8,9},{10,11},{12,13},{14,15},{16,17},{18,... | collective-permute-start | bytes 3145736 | tf_op jit(solution)/shard_map/ppermute | solution.py:416
  23.8 3.7 %collective-permute-start.5 = (bf16[8,256,128]{2,1,0:T(8,128)(2,1)S(1)}, bf16[8,256,128]{2,1,0:T(8,128)(2,1)S(1)}, u32[]{:S(2)}, u32[]{:S(2)}) collective-permute-start(bf16[8,256,128]{2,1,0:T(8,128)(2,1)S(1)} %get-tuple-element.24), channel_id=1, source_target_pairs={{1,2},{3,4},{5,6},{7,8},{9,10},{11,12},{13,14},{15,16},{17,18},{19... | collective-permute-start | bytes 1572872 | tf_op jit(solution)/shard_map/ppermute | solution.py:416
  27.5 1.9 %collective-permute-start.2 = (bf16[8,256,128]{2,1,0:T(8,128)(2,1)S(1)}, bf16[8,256,128]{2,1,0:T(8,128)(2,1)S(1)}, u32[]{:S(2)}, u32[]{:S(2)}) collective-permute-start(bf16[8,256,128]{2,1,0:T(8,128)(2,1)S(1)} %get-tuple-element.20), channel_id=1, source_target_pairs={{1,2},{3,4},{5,6},{7,8},{9,10},{11,12},{13,14},{15,16},{17,18},{19... | collective-permute-start | bytes 1572872 | tf_op jit(solution)/shard_map/ppermute | solution.py:416
  29.4 5.1 %collective-permute-done.5.far = bf16[8,256,128]{2,1,0:T(8,128)(2,1)S(1)} collective-permute-done((bf16[8,256,128]{2,1,0:T(8,128)(2,1)S(1)}, bf16[8,256,128]{2,1,0:T(8,128)(2,1)S(1)}, u32[]{:S(2)}, u32[]{:S(2)}) %collective-permute-start.5) | collective-permute-done | bytes 524320 | tf_op jit(solution)/shard_map/ppermute | solution.py:416
  34.6 0.0 collective-permute-done.3.near
  34.6 0.2 split_parity.3
  34.8 3.6 %collective-permute-start.6 = (bf16[4,256,128]{2,1,0:T(8,128)(2,1)S(1)}, bf16[4,256,128]{2,1,0:T(8,128)(2,1)S(1)}, u32[]{:S(2)}, u32[]{:S(2)}) collective-permute-start(bf16[4,256,128]{2,1,0:T(8,128)(2,1)S(1)} %get-tuple-element.26), channel_id=1, source_target_pairs={{0,32},{32,0},{64,96},{96,64},{128,160},{160,128},{192,224},{224,1... | collective-permute-start | bytes 786440 | tf_op jit(solution)/shard_map/ppermute | solution.py:433
  38.4 1.6 collective-permute-done.2.far
  40.0 0.2 split_parity.2
  40.2 0.0 copy-start.1
  40.2 3.7 %collective-permute-start.4 = (bf16[4,256,128]{2,1,0:T(8,128)(2,1)S(1)}, bf16[4,256,128]{2,1,0:T(8,128)(2,1)S(1)}, u32[]{:S(2)}, u32[]{:S(2)}) collective-permute-start(bf16[4,256,128]{2,1,0:T(8,128)(2,1)S(1)} %get-tuple-element.23), channel_id=1, source_target_pairs={{0,32},{32,0},{64,96},{96,64},{128,160},{160,128},{192,224},{224,1... | collective-permute-start | bytes 786440 | tf_op jit(solution)/shard_map/ppermute | solution.py:433
  43.9 0.0 collective-permute-done.6.got_last
  43.9 3.7 %collective-permute-done.4.got = bf16[4,256,128]{2,1,0:T(8,128)(2,1)S(1)} collective-permute-done((bf16[4,256,128]{2,1,0:T(8,128)(2,1)S(1)}, bf16[4,256,128]{2,1,0:T(8,128)(2,1)S(1)}, u32[]{:S(2)}, u32[]{:S(2)}) %collective-permute-start.4) | collective-permute-done | bytes 262176 | tf_op jit(solution)/shard_map/ppermute | solution.py:433
  47.6 0.1 add_pair.1
  47.7 39.0 %all_to_all.20.pieces = bf16[8,256,128]{2,1,0:T(8,128)(2,1)S(1)} all-to-all(bf16[8,256,128]{2,1,0:T(8,128)(2,1)S(1)} %add_pair.1), channel_id=1, replica_groups=mesh['za'=4,'zb'=2,'zc'=2,'brick'=32] {'za','zb'}, dimensions={0} | all-to-all | bytes 1048576 | tf_op jit(solution)/shard_map/all_to_all | solution.py:442
  86.7 0.0 copy-done.1
  86.7 0.3 make_image.1
  87.0 0.4 make_gram.1
  87.4 26.9 %all_to_all.21.pieces = f32[32,8,256]{2,1,0:T(8,128)S(1)} all-to-all(f32[32,8,256]{2,1,0:T(8,128)S(1)} %bitcast.14), channel_id=1, replica_groups=mesh['za'=4,'zb'=2,'zc'=2,'brick'=32] {'brick'}, dimensions={0} | all-to-all | bytes 524288 | tf_op jit(solution)/shard_map/all_to_all | solution.py:447
  114.3 0.7 spread_sum.2
  115.0 6.0 %all-to-all-start.2 = ((f32[16,8,256]{2,1,0:T(8,128)}), f32[16,8,256]{2,1,0:T(8,128)S(1)}, u32[]{:S(2)}, u32[]{:S(2)}) async-start(f32[16,8,256]{2,1,0:T(8,128)} %spread_sum.2), calls=%async_computation.2 | async-start | bytes 262144 | tf_op jit(solution)/shard_map/all_to_all | solution.py:448
  121.0 24.8 %all-gather = s16[576,256]{1,0:T(8,128)(2,1)S(1)} all-gather(s16[144,256]{1,0:T(8,128)(2,1)S(1)} %get-tuple-element.27), channel_id=2, replica_groups=mesh['za'=4,'zb'=2,'zc'=2,'brick'=32] {'za'}, dimensions={0}, use_global_device_ids=true | all-gather | bytes 368640 | tf_op jit(solution)/shard_map/all_gather | solution.py:444
  145.8 4.3 %collective-permute-start.9 = (s16[4,144,256]{2,1,0:T(8,128)(2,1)S(1)}, s16[4,144,256]{2,1,0:T(8,128)(2,1)S(1)}, u32[]{:S(2)}, u32[]{:S(2)}) collective-permute-start(s16[4,144,256]{2,1,0:T(8,128)(2,1)S(1)} %bitcast.9), channel_id=1, source_target_pairs={{0,96},{32,64},{64,32},{96,0},{128,224},{160,192},{192,160},{224,1... | collective-permute-start | bytes 884744 | tf_op jit(solution)/shard_map/ppermute | solution.py:433
  150.1 2.1 %collective-permute-start.8 = (s16[4,144,256]{2,1,0:T(8,128)(2,1)S(1)}, s16[4,144,256]{2,1,0:T(8,128)(2,1)S(1)}, u32[]{:S(2)}, u32[]{:S(2)}) collective-permute-start(s16[4,144,256]{2,1,0:T(8,128)(2,1)S(1)} %bitcast.10), channel_id=1, source_target_pairs={{0,64},{32,96},{64,0},{96,32},{128,192},{160,224},{192,128},{224,1... | collective-permute-start | bytes 884744 | tf_op jit(solution)/shard_map/ppermute | solution.py:433
  152.2 2.9 %collective-permute-start.7 = (s16[4,144,256]{2,1,0:T(8,128)(2,1)S(1)}, s16[4,144,256]{2,1,0:T(8,128)(2,1)S(1)}, u32[]{:S(2)}, u32[]{:S(2)}) collective-permute-start(s16[4,144,256]{2,1,0:T(8,128)(2,1)S(1)} %bitcast.11), channel_id=1, source_target_pairs={{0,32},{32,0},{64,96},{96,64},{128,160},{160,128},{192,224},{224,1... | collective-permute-start | bytes 884744 | tf_op jit(solution)/shard_map/ppermute | solution.py:433
  155.1 0.0 all-to-all-done.2.pieces
  155.2 14.7 %all_to_all.22 = f32[32,8,256]{2,1,0:T(8,128)S(1)} all-to-all(f32[32,8,256]{2,1,0:T(8,128)S(1)} %spread_sum.3), channel_id=1, replica_groups=mesh['za'=4,'zb'=2,'zc'=2,'brick'=32] {'brick'}, dimensions={0} | all-to-all | bytes 524288 | tf_op jit(solution)/shard_map/all_to_all | solution.py:450
  169.8 9.0 %cholesky_and_inverse.1 = (f32[256,256]{1,0:T(8,128)}, bf16[256,256]{1,0:T(8,128)(2,1)S(1)}, bf16[256,256]{1,0:T(8,128)(2,1)S(1)}) custom-call(f32[256,256]{1,0:T(8,128)S(1)} %bitcast.13), custom_call_target="tpu_custom_call" | custom-call | tf_op jit(solution)/shard_map/cholesky_and_inverse/pallas_call | solution.py:359
  178.8 0.0 collective-permute-done.9.refs_3_
  178.8 0.0 collective-permute-done.8.refs_2_
  178.8 0.0 collective-permute-done.7.refs_1_
  178.9 2.3 %make_basis.1 = f32[2048,256]{1,0:T(8,128)} custom-call(s16[4,144,256]{2,1,0:T(8,128)(2,1)S(1)} %bitcast.12, s16[4,144,256]{2,1,0:T(8,128)(2,1)S(1)} %collective-permute-done.7.refs_1_, s16[4,144,256]{2,1,0:T(8,128)(2,1)S(1)} %collective-permute-done.8.refs_2_, s16[4,144,256]{2,1,0:T(8,128)(2,1)S(1)} %collective-permute-done.9.refs_3_, ...), custom_call_target="tpu_custom_call" | custom-call | tf_op jit(solution)/shard_map/make_basis/pallas_call | solution.py:400
  (1 shorter events, 0.0 us)
Async XLA Ops:
  0.6 17.2 %collective-permute-start = (bf16[2048,256]{1,0:T(8,128)(2,1)}, bf16[2048,256]{1,0:T(8,128)(2,1)S(1)}, u32[]{:S(2)}, u32[]{:S(2)}) collective-permute-start(bf16[2048,256]{1,0:T(8,128)(2,1)} %probes.1), channel_id=1, source_target_pairs={{1,2},{3,4},{5,6},{7,8},{9,10},{11,12},{13,14},{15,16},{17,18},{19... | collective-permute-start | bytes 3145736 | tf_op jit(solution)/shard_map/ppermute | solution.py:416
  5.1 12.7 %collective-permute-start.1 = (bf16[2048,256]{1,0:T(8,128)(2,1)}, bf16[2048,256]{1,0:T(8,128)(2,1)S(1)}, u32[]{:S(2)}, u32[]{:S(2)}) collective-permute-start(bf16[2048,256]{1,0:T(8,128)(2,1)} %probes.1), channel_id=1, source_target_pairs={{0,1},{2,3},{4,5},{6,7},{8,9},{10,11},{12,13},{14,15},{16,17},{18,... | collective-permute-start | bytes 3145736 | tf_op jit(solution)/shard_map/ppermute | solution.py:416
  11.0 1.2 copy-start
  12.2 1.9 %copy-start.2 = (bf16[1,8,3,256,256]{4,3,2,1,0:T(8,128)(2,1)S(1)}, bf16[1,8,3,256,256]{4,3,2,1,0:T(8,128)(2,1)}, u32[]{:S(2)}) copy-start(bf16[1,8,3,256,256]{4,3,2,1,0:T(8,128)(2,1)} %param.4) | copy-start | bytes 9437188
  21.8 12.8 %collective-permute-start.3 = (bf16[16,256,128]{2,1,0:T(8,128)(2,1)S(1)}, bf16[16,256,128]{2,1,0:T(8,128)(2,1)S(1)}, u32[]{:S(2)}, u32[]{:S(2)}) collective-permute-start(bf16[16,256,128]{2,1,0:T(8,128)(2,1)S(1)} %get-tuple-element.21), channel_id=1, source_target_pairs={{0,1},{2,3},{4,5},{6,7},{8,9},{10,11},{12,13},{14,15},{16,17},{18,... | collective-permute-start | bytes 3145736 | tf_op jit(solution)/shard_map/ppermute | solution.py:416
  23.8 10.8 %collective-permute-start.5 = (bf16[8,256,128]{2,1,0:T(8,128)(2,1)S(1)}, bf16[8,256,128]{2,1,0:T(8,128)(2,1)S(1)}, u32[]{:S(2)}, u32[]{:S(2)}) collective-permute-start(bf16[8,256,128]{2,1,0:T(8,128)(2,1)S(1)} %get-tuple-element.24), channel_id=1, source_target_pairs={{1,2},{3,4},{5,6},{7,8},{9,10},{11,12},{13,14},{15,16},{17,18},{19... | collective-permute-start | bytes 1572872 | tf_op jit(solution)/shard_map/ppermute | solution.py:416
  27.5 12.5 %collective-permute-start.2 = (bf16[8,256,128]{2,1,0:T(8,128)(2,1)S(1)}, bf16[8,256,128]{2,1,0:T(8,128)(2,1)S(1)}, u32[]{:S(2)}, u32[]{:S(2)}) collective-permute-start(bf16[8,256,128]{2,1,0:T(8,128)(2,1)S(1)} %get-tuple-element.20), channel_id=1, source_target_pairs={{1,2},{3,4},{5,6},{7,8},{9,10},{11,12},{13,14},{15,16},{17,18},{19... | collective-permute-start | bytes 1572872 | tf_op jit(solution)/shard_map/ppermute | solution.py:416
  34.8 9.1 %collective-permute-start.6 = (bf16[4,256,128]{2,1,0:T(8,128)(2,1)S(1)}, bf16[4,256,128]{2,1,0:T(8,128)(2,1)S(1)}, u32[]{:S(2)}, u32[]{:S(2)}) collective-permute-start(bf16[4,256,128]{2,1,0:T(8,128)(2,1)S(1)} %get-tuple-element.26), channel_id=1, source_target_pairs={{0,32},{32,0},{64,96},{96,64},{128,160},{160,128},{192,224},{224,1... | collective-permute-start | bytes 786440 | tf_op jit(solution)/shard_map/ppermute | solution.py:433
  40.2 46.5 %copy-start.1 = (bf16[2048,256]{1,0:T(8,128)(2,1)S(1)}, bf16[2048,256]{1,0:T(8,128)(2,1)}, u32[]{:S(2)}) copy-start(bf16[2048,256]{1,0:T(8,128)(2,1)} %probes.1) | copy-start | bytes 3145732
  40.2 7.4 %collective-permute-start.4 = (bf16[4,256,128]{2,1,0:T(8,128)(2,1)S(1)}, bf16[4,256,128]{2,1,0:T(8,128)(2,1)S(1)}, u32[]{:S(2)}, u32[]{:S(2)}) collective-permute-start(bf16[4,256,128]{2,1,0:T(8,128)(2,1)S(1)} %get-tuple-element.23), channel_id=1, source_target_pairs={{0,32},{32,0},{64,96},{96,64},{128,160},{160,128},{192,224},{224,1... | collective-permute-start | bytes 786440 | tf_op jit(solution)/shard_map/ppermute | solution.py:433
  115.0 40.2 %all-to-all-start.2 = ((f32[16,8,256]{2,1,0:T(8,128)}), f32[16,8,256]{2,1,0:T(8,128)S(1)}, u32[]{:S(2)}, u32[]{:S(2)}) async-start(f32[16,8,256]{2,1,0:T(8,128)} %spread_sum.2), calls=%async_computation.2 | async-start | bytes 262144 | tf_op jit(solution)/shard_map/all_to_all | solution.py:448
  145.8 33.0 %collective-permute-start.9 = (s16[4,144,256]{2,1,0:T(8,128)(2,1)S(1)}, s16[4,144,256]{2,1,0:T(8,128)(2,1)S(1)}, u32[]{:S(2)}, u32[]{:S(2)}) collective-permute-start(s16[4,144,256]{2,1,0:T(8,128)(2,1)S(1)} %bitcast.9), channel_id=1, source_target_pairs={{0,96},{32,64},{64,32},{96,0},{128,224},{160,192},{192,160},{224,1... | collective-permute-start | bytes 884744 | tf_op jit(solution)/shard_map/ppermute | solution.py:433
  150.1 28.7 %collective-permute-start.8 = (s16[4,144,256]{2,1,0:T(8,128)(2,1)S(1)}, s16[4,144,256]{2,1,0:T(8,128)(2,1)S(1)}, u32[]{:S(2)}, u32[]{:S(2)}) collective-permute-start(s16[4,144,256]{2,1,0:T(8,128)(2,1)S(1)} %bitcast.10), channel_id=1, source_target_pairs={{0,64},{32,96},{64,0},{96,32},{128,192},{160,224},{192,128},{224,1... | collective-permute-start | bytes 884744 | tf_op jit(solution)/shard_map/ppermute | solution.py:433
  152.2 26.7 %collective-permute-start.7 = (s16[4,144,256]{2,1,0:T(8,128)(2,1)S(1)}, s16[4,144,256]{2,1,0:T(8,128)(2,1)S(1)}, u32[]{:S(2)}, u32[]{:S(2)}) collective-permute-start(s16[4,144,256]{2,1,0:T(8,128)(2,1)S(1)} %bitcast.11), channel_id=1, source_target_pairs={{0,32},{32,0},{64,96},{96,64},{128,160},{160,128},{192,224},{224,1... | collective-permute-start | bytes 884744 | tf_op jit(solution)/shard_map/ppermute | solution.py:433

commit v8 on v7

--- a/solution.py
+++ b/solution.py
@@ -80,7 +80,7 @@
 
 
 def operator_kernel(
-    cols, w_ref, data_ref, far_ref, near_ref, own_out, far_first, far_last, near_out, s_far, s_near, d_ref
+    cols, w_ref, data_ref, far_ref, near_ref, own_out, far_first, far_last, near_first, near_last, s_far, s_near, d_ref
 ):
     blocks, _, bs, _ = w_ref.shape
     dot = functools.partial(jnp.dot, preferred_element_type=F32)
@@ -114,8 +114,9 @@
     put(blocks - 1)
     half = blocks // 2
     for q in range(blocks):
-        far_out = far_first if q < half else far_last
-        for out, k, field in ((far_out, q % half, s_far), (near_out, q, s_near)):
+        outs = (far_first, near_first) if q < half else (far_last, near_last)
+        for out, field in zip(outs, (s_far, s_near)):
+            k = q % half
             out[2 * k] = field[q, :, :128].astype(BF16)
             out[2 * k + 1] = field[q, :, 128:].astype(BF16)
 
@@ -129,12 +130,13 @@
     return pl.pallas_call(
         operator_kernel,
         in_specs=[pl.BlockSpec(memory_space=pltpu.SMEM)] + [in_vmem()] * 4,
-        out_specs=[in_vmem()] * 4,
+        out_specs=[in_vmem()] * 5,
         out_shape=(
             jax.ShapeDtypeStruct(shape, F32),
             half,
             half,
-            jax.ShapeDtypeStruct(shape, BF16),
+            half,
+            half,
         ),
         scratch_shapes=[field, field, pltpu.VMEM((2, width, bs), BF16)],
         compiler_params=params(20),
@@ -147,7 +149,7 @@
     for out, parity in ((keep, odd), (send, 1 - odd)):
         for i in range(out.shape[0]):
             p = 2 * i + parity
-            total = far[p].astype(F32) + near[first + p].astype(F32)
+            total = far[p].astype(F32) + near[p].astype(F32)
             out[i] = (own[first + p] + total).astype(out.dtype)
 
 
@@ -425,18 +427,18 @@
     shape = (blocks, bs, width)
     cols = columns.reshape(-1)
     w_sorted, own_data = start_operator(cols, w_local, probes.reshape(shape))
-    own, *to_far, to_near = finish_operator(cols, w_sorted, own_data, far.reshape(shape), near.reshape(shape))
+    own, *sent = finish_operator(cols, w_sorted, own_data, far.reshape(shape), near.reshape(shape))
 
     n = lax.axis_size(DEPTH)
 
     def swap(held, distance):
         return lax.ppermute(held, DEPTH, [(i, i ^ distance) for i in range(n)])
 
-    from_far = [paired(to_far[0], "brick", 1), paired(to_far[1], "brick", 1)]
-    from_near = paired(to_near, "brick", 0)
+    from_far = [paired(part, "brick", 1) for part in sent[:2]]
+    from_near = [paired(part, "brick", 0) for part in sent[2:]]
     halves = []
     for k, part in enumerate(from_far):
-        keep, send = split_parity(k * part.shape[0], own, part, from_near)
+        keep, send = split_parity(k * part.shape[0], own, part, from_near[k])
         halves += [keep, swap(send, 1)]
     held = add_pair(*halves)
     image, coded = make_image(lax.all_to_all(held, ("za", "zb"), 0, 0), probes)

time: 182 us -> 181 us (level)
  starting transfers between devices: 39.7 us -> 42.5 us
  waiting for transfers between devices: 12.1 us -> 9.88 us
    ppermute x5 -> x6, waiting for transfers between devices: 8.34 us -> 2.95 us  [paired(): return lax.ppermute(value, axis, pairs + [(j, i) for i, j in pairs])]
    ppermute x5 -> x6, starting transfers between devices: 17.1 us -> 20.5 us  [paired(): return lax.ppermute(value, axis, pairs + [(j, i) for i, j in pairs])]
    ppermute x5, waiting for transfers between devices: 3.75 us -> 6.92 us  [swap(): return lax.ppermute(held, DEPTH, [(i, i ^ distance) for i in range(n)])]
    all_to_all x1, blocking collectives: 26.9 us -> 24.6 us  [body(): lax.all_to_all(gram.reshape(bricks, width // bricks, width), 'brick', 0, 0)]
  transfers between devices with their start and end apart: 11 -> 12, of which waited for: 4 -> 4; matrix products, arithmetic and copies ran while one was open for 0% -> 0% of each run, Pallas kernels for 6% -> 6%
where the time goes in v8:
time: 181 us; the launch traced here: 180 us
  blocking collectives  104 us (57%)
  starting transfers between devices  42.5 us (23%)
  Pallas kernels  19.2 us (11%)
  waiting for transfers between devices  9.88 us (5%)
  local copies, waits for them, and re-layouts  3.96 us (2%)
    all_to_all x1, blocking collectives, body(): image, coded = make_image(lax.all_to_all(held, ('za', 'zb'), 0, 0), probes)  39.6 us
    all_gather x1, blocking collectives, body(): held = lax.all_gather(coded, 'za')  24.8 us
    all_to_all x1, blocking collectives, body(): lax.all_to_all(gram.reshape(bricks, width // bricks, width), 'brick', 0, 0)  24.6 us
    ppermute x6, starting transfers between devices, paired(): return lax.ppermute(value, axis, pairs + [(j, i) for i, j in pairs])  20.5 us
    ppermute x5, starting transfers between devices, swap(): return lax.ppermute(held, DEPTH, [(i, i ^ distance) for i in range(n)])  16.5 us
    all_to_all x1, blocking collectives, body(): lax.all_to_all(spread_sum(share, bricks), 'brick', 0, 0)  14.7 us
    pallas_call x1, Pallas kernels, cholesky_and_inverse(): pl.pallas_call(functools.partial(factor_kernel, scale), in_specs=[in_vmem...  9 us
    ppermute x5, waiting for transfers between devices, swap(): return lax.ppermute(held, DEPTH, [(i, i ^ distance) for i in range(n)])  6.92 us
  transfers between devices with their start and end apart: 12, of which 4 were waited for; matrix products, arithmetic and copies ran while one was open for 0% of the time, Pallas kernels for 6%

profile of v8, /device:TPU:1, one launch (start us, length us, event | category | flops | bytes accessed | tf_op | source)
XLA Modules:
  0.0 180.3 jit_solution(17262261465289944764)
XLA Ops:
  0.6 4.5 %collective-permute-start = (bf16[2048,256]{1,0:T(8,128)(2,1)}, bf16[2048,256]{1,0:T(8,128)(2,1)S(1)}, u32[]{:S(2)}, u32[]{:S(2)}) collective-permute-start(bf16[2048,256]{1,0:T(8,128)(2,1)} %probes.1), channel_id=1, source_target_pairs={{1,2},{3,4},{5,6},{7,8},{9,10},{11,12},{13,14},{15,16},{17,18},{19... | collective-permute-start | bytes 3145736 | tf_op jit(solution)/shard_map/ppermute | solution.py:418
  5.1 5.0 %collective-permute-start.1 = (bf16[2048,256]{1,0:T(8,128)(2,1)}, bf16[2048,256]{1,0:T(8,128)(2,1)S(1)}, u32[]{:S(2)}, u32[]{:S(2)}) collective-permute-start(bf16[2048,256]{1,0:T(8,128)(2,1)} %probes.1), channel_id=1, source_target_pairs={{0,1},{2,3},{4,5},{6,7},{8,9},{10,11},{12,13},{14,15},{16,17},{18,... | collective-permute-start | bytes 3145736 | tf_op jit(solution)/shard_map/ppermute | solution.py:418
  10.2 0.8 copy.6
  10.9 0.1 reshape.22.cols
  11.0 0.0 copy-start
  11.0 1.2 copy-done
  12.2 0.0 copy-start.2
  12.2 1.9 %copy-done.2 = bf16[1,8,3,256,256]{4,3,2,1,0:T(8,128)(2,1)S(1)} copy-done((bf16[1,8,3,256,256]{4,3,2,1,0:T(8,128)(2,1)S(1)}, bf16[1,8,3,256,256]{4,3,2,1,0:T(8,128)(2,1)}, u32[]{:S(2)}) %copy-start.2) | copy-done | bytes 3145752
  14.1 2.1 %own_data.1 = (bf16[8,3,256,256]{3,2,1,0:T(8,128)(2,1)S(1)}, f32[8,256,256]{2,1,0:T(8,128)S(1)}) custom-call(s32[24]{0:T(128)S(1)} %reshape.22.cols, bf16[8,3,256,256]{3,2,1,0:T(8,128)(2,1)S(1)} %bitcast.8, bf16[8,256,256]{2,1,0:T(8,128)(2,1)S(1)} %bitcast.7), custom_call_target="tpu_custom_call" | custom-call | flops 268435456 | bytes 9437184 | tf_op jit(solution)/shard_map/own_data/pallas_call | solution.py:66
  16.2 1.6 collective-permute-done
  17.8 0.0 collective-permute-done.1
  17.8 4.0 %normal_operator.1 = (f32[16,256,128]{2,1,0:T(8,128)S(1)}, bf16[8,256,128]{2,1,0:T(8,128)(2,1)S(1)}, bf16[8,256,128]{2,1,0:T(8,128)(2,1)S(1)}, bf16[8,256,128]{2,1,0:T(8,128)(2,1)S(1)}, bf16[8,256,128]{2,1,0:T(8,128)(2,1)S(1)}) custom-call(s32[24]{0:T(128)S(1)} %reshape.22.cols, bf16[8,3,256,256]{3,2,1,0:T(8,128)(2,1)S(1)} %get-tuple-element.18.w_ref, ...), custom_call_target="tpu_custom_call" | custom-call | tf_op jit(solution)/shard_map/normal_operator/pallas_call | solution.py:130
  21.8 3.6 %collective-permute-start.2 = (bf16[8,256,128]{2,1,0:T(8,128)(2,1)S(1)}, bf16[8,256,128]{2,1,0:T(8,128)(2,1)S(1)}, u32[]{:S(2)}, u32[]{:S(2)}) collective-permute-start(bf16[8,256,128]{2,1,0:T(8,128)(2,1)S(1)} %get-tuple-element.21), channel_id=1, source_target_pairs={{1,2},{3,4},{5,6},{7,8},{9,10},{11,12},{13,14},{15,16},{17,18},{19... | collective-permute-start | bytes 1572872 | tf_op jit(solution)/shard_map/ppermute | solution.py:418
  25.5 1.9 %collective-permute-start.3 = (bf16[8,256,128]{2,1,0:T(8,128)(2,1)S(1)}, bf16[8,256,128]{2,1,0:T(8,128)(2,1)S(1)}, u32[]{:S(2)}, u32[]{:S(2)}) collective-permute-start(bf16[8,256,128]{2,1,0:T(8,128)(2,1)S(1)} %get-tuple-element.22), channel_id=1, source_target_pairs={{0,1},{2,3},{4,5},{6,7},{8,9},{10,11},{12,13},{14,15},{16,17},{18,... | collective-permute-start | bytes 1572872 | tf_op jit(solution)/shard_map/ppermute | solution.py:418
  27.4 3.5 %collective-permute-start.5 = (bf16[8,256,128]{2,1,0:T(8,128)(2,1)S(1)}, bf16[8,256,128]{2,1,0:T(8,128)(2,1)S(1)}, u32[]{:S(2)}, u32[]{:S(2)}) collective-permute-start(bf16[8,256,128]{2,1,0:T(8,128)(2,1)S(1)} %get-tuple-element.25), channel_id=1, source_target_pairs={{1,2},{3,4},{5,6},{7,8},{9,10},{11,12},{13,14},{15,16},{17,18},{19... | collective-permute-start | bytes 1572872 | tf_op jit(solution)/shard_map/ppermute | solution.py:418
  30.9 1.9 %collective-permute-start.6 = (bf16[8,256,128]{2,1,0:T(8,128)(2,1)S(1)}, bf16[8,256,128]{2,1,0:T(8,128)(2,1)S(1)}, u32[]{:S(2)}, u32[]{:S(2)}) collective-permute-start(bf16[8,256,128]{2,1,0:T(8,128)(2,1)S(1)} %get-tuple-element.26), channel_id=1, source_target_pairs={{0,1},{2,3},{4,5},{6,7},{8,9},{10,11},{12,13},{14,15},{16,17},{18,... | collective-permute-start | bytes 1572872 | tf_op jit(solution)/shard_map/ppermute | solution.py:418
  32.8 0.0 collective-permute-done.2.far
  32.8 0.0 collective-permute-done.3.near
  32.9 0.2 split_parity.2
  33.1 3.5 %collective-permute-start.4 = (bf16[4,256,128]{2,1,0:T(8,128)(2,1)S(1)}, bf16[4,256,128]{2,1,0:T(8,128)(2,1)S(1)}, u32[]{:S(2)}, u32[]{:S(2)}) collective-permute-start(bf16[4,256,128]{2,1,0:T(8,128)(2,1)S(1)} %get-tuple-element.24), channel_id=1, source_target_pairs={{0,32},{32,0},{64,96},{96,64},{128,160},{160,128},{192,224},{224,1... | collective-permute-start | bytes 786440 | tf_op jit(solution)/shard_map/ppermute | solution.py:435
  36.6 1.3 collective-permute-done.5.far
  37.9 0.0 collective-permute-done.6.near
  37.9 0.2 split_parity.3
  38.1 0.0 copy-start.1
  38.1 3.7 %collective-permute-start.7 = (bf16[4,256,128]{2,1,0:T(8,128)(2,1)S(1)}, bf16[4,256,128]{2,1,0:T(8,128)(2,1)S(1)}, u32[]{:S(2)}, u32[]{:S(2)}) collective-permute-start(bf16[4,256,128]{2,1,0:T(8,128)(2,1)S(1)} %get-tuple-element.28), channel_id=1, source_target_pairs={{0,32},{32,0},{64,96},{96,64},{128,160},{160,128},{192,224},{224,1... | collective-permute-start | bytes 786440 | tf_op jit(solution)/shard_map/ppermute | solution.py:435
  41.8 0.9 collective-permute-done.4.got
  42.7 6.0 %collective-permute-done.7.got_last = bf16[4,256,128]{2,1,0:T(8,128)(2,1)S(1)} collective-permute-done((bf16[4,256,128]{2,1,0:T(8,128)(2,1)S(1)}, bf16[4,256,128]{2,1,0:T(8,128)(2,1)S(1)}, u32[]{:S(2)}, u32[]{:S(2)}) %collective-permute-start.7) | collective-permute-done | bytes 262176 | tf_op jit(solution)/shard_map/ppermute | solution.py:435
  48.7 0.1 add_pair.1
  48.8 39.6 %all_to_all.20.pieces = bf16[8,256,128]{2,1,0:T(8,128)(2,1)S(1)} all-to-all(bf16[8,256,128]{2,1,0:T(8,128)(2,1)S(1)} %add_pair.1), channel_id=1, replica_groups=mesh['za'=4,'zb'=2,'zc'=2,'brick'=32] {'za','zb'}, dimensions={0} | all-to-all | bytes 1048576 | tf_op jit(solution)/shard_map/all_to_all | solution.py:444
  88.5 0.0 copy-done.1
  88.5 0.3 make_image.1
  88.8 0.4 make_gram.1
  89.2 24.6 %all_to_all.21.pieces = f32[32,8,256]{2,1,0:T(8,128)S(1)} all-to-all(f32[32,8,256]{2,1,0:T(8,128)S(1)} %bitcast.14), channel_id=1, replica_groups=mesh['za'=4,'zb'=2,'zc'=2,'brick'=32] {'brick'}, dimensions={0} | all-to-all | bytes 524288 | tf_op jit(solution)/shard_map/all_to_all | solution.py:449
  113.8 0.7 spread_sum.2
  114.5 5.5 %all-to-all-start.2 = ((f32[16,8,256]{2,1,0:T(8,128)}), f32[16,8,256]{2,1,0:T(8,128)S(1)}, u32[]{:S(2)}, u32[]{:S(2)}) async-start(f32[16,8,256]{2,1,0:T(8,128)} %spread_sum.2), calls=%async_computation.2 | async-start | bytes 262144 | tf_op jit(solution)/shard_map/all_to_all | solution.py:450
  120.0 24.8 %all-gather = s16[576,256]{1,0:T(8,128)(2,1)S(1)} all-gather(s16[144,256]{1,0:T(8,128)(2,1)S(1)} %get-tuple-element.29), channel_id=2, replica_groups=mesh['za'=4,'zb'=2,'zc'=2,'brick'=32] {'za'}, dimensions={0}, use_global_device_ids=true | all-gather | bytes 368640 | tf_op jit(solution)/shard_map/all_gather | solution.py:446
  144.8 4.3 %collective-permute-start.10 = (s16[4,144,256]{2,1,0:T(8,128)(2,1)S(1)}, s16[4,144,256]{2,1,0:T(8,128)(2,1)S(1)}, u32[]{:S(2)}, u32[]{:S(2)}) collective-permute-start(s16[4,144,256]{2,1,0:T(8,128)(2,1)S(1)} %bitcast.9), channel_id=1, source_target_pairs={{0,96},{32,64},{64,32},{96,0},{128,224},{160,192},{192,160},{224,1... | collective-permute-start | bytes 884744 | tf_op jit(solution)/shard_map/ppermute | solution.py:435
  149.1 2.1 %collective-permute-start.9 = (s16[4,144,256]{2,1,0:T(8,128)(2,1)S(1)}, s16[4,144,256]{2,1,0:T(8,128)(2,1)S(1)}, u32[]{:S(2)}, u32[]{:S(2)}) collective-permute-start(s16[4,144,256]{2,1,0:T(8,128)(2,1)S(1)} %bitcast.10), channel_id=1, source_target_pairs={{0,64},{32,96},{64,0},{96,32},{128,192},{160,224},{192,128},{224,1... | collective-permute-start | bytes 884744 | tf_op jit(solution)/shard_map/ppermute | solution.py:435
  151.2 2.9 %collective-permute-start.8 = (s16[4,144,256]{2,1,0:T(8,128)(2,1)S(1)}, s16[4,144,256]{2,1,0:T(8,128)(2,1)S(1)}, u32[]{:S(2)}, u32[]{:S(2)}) collective-permute-start(s16[4,144,256]{2,1,0:T(8,128)(2,1)S(1)} %bitcast.11), channel_id=1, source_target_pairs={{0,32},{32,0},{64,96},{96,64},{128,160},{160,128},{192,224},{224,1... | collective-permute-start | bytes 884744 | tf_op jit(solution)/shard_map/ppermute | solution.py:435
  154.1 0.0 all-to-all-done.2.pieces
  154.2 14.7 %all_to_all.22 = f32[32,8,256]{2,1,0:T(8,128)S(1)} all-to-all(f32[32,8,256]{2,1,0:T(8,128)S(1)} %spread_sum.3), channel_id=1, replica_groups=mesh['za'=4,'zb'=2,'zc'=2,'brick'=32] {'brick'}, dimensions={0} | all-to-all | bytes 524288 | tf_op jit(solution)/shard_map/all_to_all | solution.py:452
  168.8 9.0 %cholesky_and_inverse.1 = (f32[256,256]{1,0:T(8,128)}, bf16[256,256]{1,0:T(8,128)(2,1)S(1)}, bf16[256,256]{1,0:T(8,128)(2,1)S(1)}) custom-call(f32[256,256]{1,0:T(8,128)S(1)} %bitcast.13), custom_call_target="tpu_custom_call" | custom-call | tf_op jit(solution)/shard_map/cholesky_and_inverse/pallas_call | solution.py:361
  177.8 0.0 collective-permute-done.10.refs_3_
  177.9 0.0 collective-permute-done.9.refs_2_
  177.9 0.0 collective-permute-done.8.refs_1_
  177.9 2.3 %make_basis.1 = f32[2048,256]{1,0:T(8,128)} custom-call(s16[4,144,256]{2,1,0:T(8,128)(2,1)S(1)} %bitcast.12, s16[4,144,256]{2,1,0:T(8,128)(2,1)S(1)} %collective-permute-done.8.refs_1_, s16[4,144,256]{2,1,0:T(8,128)(2,1)S(1)} %collective-permute-done.9.refs_2_, s16[4,144,256]{2,1,0:T(8,128)(2,1)S(1)} %collective-permute-done.10.refs_3_, ...), custom_call_target="tpu_custom_call" | custom-call | tf_op jit(solution)/shard_map/make_basis/pallas_call | solution.py:402
  (1 shorter events, 0.0 us)
Async XLA Ops:
  0.6 17.2 %collective-permute-start = (bf16[2048,256]{1,0:T(8,128)(2,1)}, bf16[2048,256]{1,0:T(8,128)(2,1)S(1)}, u32[]{:S(2)}, u32[]{:S(2)}) collective-permute-start(bf16[2048,256]{1,0:T(8,128)(2,1)} %probes.1), channel_id=1, source_target_pairs={{1,2},{3,4},{5,6},{7,8},{9,10},{11,12},{13,14},{15,16},{17,18},{19... | collective-permute-start | bytes 3145736 | tf_op jit(solution)/shard_map/ppermute | solution.py:418
  5.1 12.7 %collective-permute-start.1 = (bf16[2048,256]{1,0:T(8,128)(2,1)}, bf16[2048,256]{1,0:T(8,128)(2,1)S(1)}, u32[]{:S(2)}, u32[]{:S(2)}) collective-permute-start(bf16[2048,256]{1,0:T(8,128)(2,1)} %probes.1), channel_id=1, source_target_pairs={{0,1},{2,3},{4,5},{6,7},{8,9},{10,11},{12,13},{14,15},{16,17},{18,... | collective-permute-start | bytes 3145736 | tf_op jit(solution)/shard_map/ppermute | solution.py:418
  11.0 1.2 copy-start
  12.2 1.9 %copy-start.2 = (bf16[1,8,3,256,256]{4,3,2,1,0:T(8,128)(2,1)S(1)}, bf16[1,8,3,256,256]{4,3,2,1,0:T(8,128)(2,1)}, u32[]{:S(2)}) copy-start(bf16[1,8,3,256,256]{4,3,2,1,0:T(8,128)(2,1)} %param.4) | copy-start | bytes 9437188
  21.8 11.0 %collective-permute-start.2 = (bf16[8,256,128]{2,1,0:T(8,128)(2,1)S(1)}, bf16[8,256,128]{2,1,0:T(8,128)(2,1)S(1)}, u32[]{:S(2)}, u32[]{:S(2)}) collective-permute-start(bf16[8,256,128]{2,1,0:T(8,128)(2,1)S(1)} %get-tuple-element.21), channel_id=1, source_target_pairs={{1,2},{3,4},{5,6},{7,8},{9,10},{11,12},{13,14},{15,16},{17,18},{19... | collective-permute-start | bytes 1572872 | tf_op jit(solution)/shard_map/ppermute | solution.py:418
  25.5 7.4 %collective-permute-start.3 = (bf16[8,256,128]{2,1,0:T(8,128)(2,1)S(1)}, bf16[8,256,128]{2,1,0:T(8,128)(2,1)S(1)}, u32[]{:S(2)}, u32[]{:S(2)}) collective-permute-start(bf16[8,256,128]{2,1,0:T(8,128)(2,1)S(1)} %get-tuple-element.22), channel_id=1, source_target_pairs={{0,1},{2,3},{4,5},{6,7},{8,9},{10,11},{12,13},{14,15},{16,17},{18,... | collective-permute-start | bytes 1572872 | tf_op jit(solution)/shard_map/ppermute | solution.py:418
  27.4 10.5 %collective-permute-start.5 = (bf16[8,256,128]{2,1,0:T(8,128)(2,1)S(1)}, bf16[8,256,128]{2,1,0:T(8,128)(2,1)S(1)}, u32[]{:S(2)}, u32[]{:S(2)}) collective-permute-start(bf16[8,256,128]{2,1,0:T(8,128)(2,1)S(1)} %get-tuple-element.25), channel_id=1, source_target_pairs={{1,2},{3,4},{5,6},{7,8},{9,10},{11,12},{13,14},{15,16},{17,18},{19... | collective-permute-start | bytes 1572872 | tf_op jit(solution)/shard_map/ppermute | solution.py:418
  30.9 7.0 %collective-permute-start.6 = (bf16[8,256,128]{2,1,0:T(8,128)(2,1)S(1)}, bf16[8,256,128]{2,1,0:T(8,128)(2,1)S(1)}, u32[]{:S(2)}, u32[]{:S(2)}) collective-permute-start(bf16[8,256,128]{2,1,0:T(8,128)(2,1)S(1)} %get-tuple-element.26), channel_id=1, source_target_pairs={{0,1},{2,3},{4,5},{6,7},{8,9},{10,11},{12,13},{14,15},{16,17},{18,... | collective-permute-start | bytes 1572872 | tf_op jit(solution)/shard_map/ppermute | solution.py:418
  33.1 9.7 %collective-permute-start.4 = (bf16[4,256,128]{2,1,0:T(8,128)(2,1)S(1)}, bf16[4,256,128]{2,1,0:T(8,128)(2,1)S(1)}, u32[]{:S(2)}, u32[]{:S(2)}) collective-permute-start(bf16[4,256,128]{2,1,0:T(8,128)(2,1)S(1)} %get-tuple-element.24), channel_id=1, source_target_pairs={{0,32},{32,0},{64,96},{96,64},{128,160},{160,128},{192,224},{224,1... | collective-permute-start | bytes 786440 | tf_op jit(solution)/shard_map/ppermute | solution.py:435
  38.1 50.3 %copy-start.1 = (bf16[2048,256]{1,0:T(8,128)(2,1)S(1)}, bf16[2048,256]{1,0:T(8,128)(2,1)}, u32[]{:S(2)}) copy-start(bf16[2048,256]{1,0:T(8,128)(2,1)} %probes.1) | copy-start | bytes 3145732
  38.1 10.6 %collective-permute-start.7 = (bf16[4,256,128]{2,1,0:T(8,128)(2,1)S(1)}, bf16[4,256,128]{2,1,0:T(8,128)(2,1)S(1)}, u32[]{:S(2)}, u32[]{:S(2)}) collective-permute-start(bf16[4,256,128]{2,1,0:T(8,128)(2,1)S(1)} %get-tuple-element.28), channel_id=1, source_target_pairs={{0,32},{32,0},{64,96},{96,64},{128,160},{160,128},{192,224},{224,1... | collective-permute-start | bytes 786440 | tf_op jit(solution)/shard_map/ppermute | solution.py:435
  114.5 39.6 %all-to-all-start.2 = ((f32[16,8,256]{2,1,0:T(8,128)}), f32[16,8,256]{2,1,0:T(8,128)S(1)}, u32[]{:S(2)}, u32[]{:S(2)}) async-start(f32[16,8,256]{2,1,0:T(8,128)} %spread_sum.2), calls=%async_computation.2 | async-start | bytes 262144 | tf_op jit(solution)/shard_map/all_to_all | solution.py:450
  144.8 33.0 %collective-permute-start.10 = (s16[4,144,256]{2,1,0:T(8,128)(2,1)S(1)}, s16[4,144,256]{2,1,0:T(8,128)(2,1)S(1)}, u32[]{:S(2)}, u32[]{:S(2)}) collective-permute-start(s16[4,144,256]{2,1,0:T(8,128)(2,1)S(1)} %bitcast.9), channel_id=1, source_target_pairs={{0,96},{32,64},{64,32},{96,0},{128,224},{160,192},{192,160},{224,1... | collective-permute-start | bytes 884744 | tf_op jit(solution)/shard_map/ppermute | solution.py:435
  149.1 28.7 %collective-permute-start.9 = (s16[4,144,256]{2,1,0:T(8,128)(2,1)S(1)}, s16[4,144,256]{2,1,0:T(8,128)(2,1)S(1)}, u32[]{:S(2)}, u32[]{:S(2)}) collective-permute-start(s16[4,144,256]{2,1,0:T(8,128)(2,1)S(1)} %bitcast.10), channel_id=1, source_target_pairs={{0,64},{32,96},{64,0},{96,32},{128,192},{160,224},{192,128},{224,1... | collective-permute-start | bytes 884744 | tf_op jit(solution)/shard_map/ppermute | solution.py:435
  151.2 26.7 %collective-permute-start.8 = (s16[4,144,256]{2,1,0:T(8,128)(2,1)S(1)}, s16[4,144,256]{2,1,0:T(8,128)(2,1)S(1)}, u32[]{:S(2)}, u32[]{:S(2)}) collective-permute-start(s16[4,144,256]{2,1,0:T(8,128)(2,1)S(1)} %bitcast.11), channel_id=1, source_target_pairs={{0,32},{32,0},{64,96},{96,64},{128,160},{160,128},{192,224},{224,1... | collective-permute-start | bytes 884744 | tf_op jit(solution)/shard_map/ppermute | solution.py:435

commit v9 on v8

--- a/solution.py
+++ b/solution.py
@@ -448,7 +448,8 @@
     bricks = lax.axis_size("brick")
     share = lax.all_to_all(gram.reshape(bricks, width // bricks, width), "brick", 0, 0)
     share = lax.all_to_all(spread_sum(share, n), DEPTH, 0, 0)
-    parts = [held] + [swap(held, k) for k in (1, 2, 3)]
+    parts = [held] + [swap(held, k) for k in (1, 2)]
+    parts.append(swap(parts[2], 1))
     gram = lax.all_to_all(spread_sum(share, bricks), "brick", 0, 0).reshape(width, width)
 
     scale = math.sqrt(rows * bricks)

time: 181 us -> 191 us (1.055)
  waiting for transfers between devices: 9.88 us -> 21.1 us
    ppermute x5, waiting for transfers between devices: 6.92 us -> 18.2 us  [swap(): return lax.ppermute(held, DEPTH, [(i, i ^ distance) for i in range(n)])]
  transfers between devices with their start and end apart: 12 -> 12, of which waited for: 4 -> 5; matrix products, arithmetic and copies ran while one was open for 0% -> 0% of each run, Pallas kernels for 6% -> 6%
where the time goes in v9:
time: 191 us; the launch traced here: 190 us
  blocking collectives  103 us (54%)
  starting transfers between devices  41.6 us (22%)
  waiting for transfers between devices  21.1 us (11%)
  Pallas kernels  19.2 us (10%)
  local copies, waits for them, and re-layouts  3.96 us (2%)
    all_to_all x1, blocking collectives, body(): image, coded = make_image(lax.all_to_all(held, ('za', 'zb'), 0, 0), probes)  39.6 us
    all_gather x1, blocking collectives, body(): held = lax.all_gather(coded, 'za')  24.8 us
    all_to_all x1, blocking collectives, body(): lax.all_to_all(gram.reshape(bricks, width // bricks, width), 'brick', 0, 0)  24.6 us
    ppermute x6, starting transfers between devices, paired(): return lax.ppermute(value, axis, pairs + [(j, i) for i, j in pairs])  20.5 us
    ppermute x5, waiting for transfers between devices, swap(): return lax.ppermute(held, DEPTH, [(i, i ^ distance) for i in range(n)])  18.2 us
    ppermute x5, starting transfers between devices, swap(): return lax.ppermute(held, DEPTH, [(i, i ^ distance) for i in range(n)])  15.6 us
    all_to_all x1, blocking collectives, body(): lax.all_to_all(spread_sum(share, bricks), 'brick', 0, 0)  13.9 us
    pallas_call x1, Pallas kernels, cholesky_and_inverse(): pl.pallas_call(functools.partial(factor_kernel, scale), in_specs=[in_vmem...  9 us
  transfers between devices with their start and end apart: 12, of which 5 were waited for; matrix products, arithmetic and copies ran while one was open for 0% of the time, Pallas kernels for 6%

profile of v9, /device:TPU:1, one launch (start us, length us, event | category | flops | bytes accessed | tf_op | source)
XLA Modules:
  0.0 189.9 jit_solution(1802078214509236877)
XLA Ops:
  0.6 4.5 %collective-permute-start = (bf16[2048,256]{1,0:T(8,128)(2,1)}, bf16[2048,256]{1,0:T(8,128)(2,1)S(1)}, u32[]{:S(2)}, u32[]{:S(2)}) collective-permute-start(bf16[2048,256]{1,0:T(8,128)(2,1)} %probes.1), channel_id=1, source_target_pairs={{1,2},{3,4},{5,6},{7,8},{9,10},{11,12},{13,14},{15,16},{17,18},{19... | collective-permute-start | bytes 3145736 | tf_op jit(solution)/shard_map/ppermute | solution.py:418
  5.1 5.0 %collective-permute-start.1 = (bf16[2048,256]{1,0:T(8,128)(2,1)}, bf16[2048,256]{1,0:T(8,128)(2,1)S(1)}, u32[]{:S(2)}, u32[]{:S(2)}) collective-permute-start(bf16[2048,256]{1,0:T(8,128)(2,1)} %probes.1), channel_id=1, source_target_pairs={{0,1},{2,3},{4,5},{6,7},{8,9},{10,11},{12,13},{14,15},{16,17},{18,... | collective-permute-start | bytes 3145736 | tf_op jit(solution)/shard_map/ppermute | solution.py:418
  10.2 0.8 copy.6
  10.9 0.1 reshape.22.cols
  11.0 0.0 copy-start
  11.0 1.2 copy-done
  12.2 0.0 copy-start.2
  12.2 1.9 copy-done.2
  14.1 2.1 %own_data.1 = (bf16[8,3,256,256]{3,2,1,0:T(8,128)(2,1)S(1)}, f32[8,256,256]{2,1,0:T(8,128)S(1)}) custom-call(s32[24]{0:T(128)S(1)} %reshape.22.cols, bf16[8,3,256,256]{3,2,1,0:T(8,128)(2,1)S(1)} %bitcast.8, bf16[8,256,256]{2,1,0:T(8,128)(2,1)S(1)} %bitcast.7), custom_call_target="tpu_custom_call" | custom-call | flops 268435456 | bytes 9437184 | tf_op jit(solution)/shard_map/own_data/pallas_call | solution.py:66
  16.2 1.6 collective-permute-done
  17.8 0.0 collective-permute-done.1
  17.8 4.0 %normal_operator.1 = (f32[16,256,128]{2,1,0:T(8,128)S(1)}, bf16[8,256,128]{2,1,0:T(8,128)(2,1)S(1)}, bf16[8,256,128]{2,1,0:T(8,128)(2,1)S(1)}, bf16[8,256,128]{2,1,0:T(8,128)(2,1)S(1)}, bf16[8,256,128]{2,1,0:T(8,128)(2,1)S(1)}) custom-call(s32[24]{0:T(128)S(1)} %reshape.22.cols, bf16[8,3,256,256]{3,2,1,0:T(8,128)(2,1)S(1)} %get-tuple-element.18.w_ref, ...), custom_call_target="tpu_custom_call" | custom-call | tf_op jit(solution)/shard_map/normal_operator/pallas_call | solution.py:130
  21.8 3.6 %collective-permute-start.2 = (bf16[8,256,128]{2,1,0:T(8,128)(2,1)S(1)}, bf16[8,256,128]{2,1,0:T(8,128)(2,1)S(1)}, u32[]{:S(2)}, u32[]{:S(2)}) collective-permute-start(bf16[8,256,128]{2,1,0:T(8,128)(2,1)S(1)} %get-tuple-element.21), channel_id=1, source_target_pairs={{1,2},{3,4},{5,6},{7,8},{9,10},{11,12},{13,14},{15,16},{17,18},{19... | collective-permute-start | bytes 1572872 | tf_op jit(solution)/shard_map/ppermute | solution.py:418
  25.5 1.9 %collective-permute-start.3 = (bf16[8,256,128]{2,1,0:T(8,128)(2,1)S(1)}, bf16[8,256,128]{2,1,0:T(8,128)(2,1)S(1)}, u32[]{:S(2)}, u32[]{:S(2)}) collective-permute-start(bf16[8,256,128]{2,1,0:T(8,128)(2,1)S(1)} %get-tuple-element.22), channel_id=1, source_target_pairs={{0,1},{2,3},{4,5},{6,7},{8,9},{10,11},{12,13},{14,15},{16,17},{18,... | collective-permute-start | bytes 1572872 | tf_op jit(solution)/shard_map/ppermute | solution.py:418
  27.4 3.5 %collective-permute-start.5 = (bf16[8,256,128]{2,1,0:T(8,128)(2,1)S(1)}, bf16[8,256,128]{2,1,0:T(8,128)(2,1)S(1)}, u32[]{:S(2)}, u32[]{:S(2)}) collective-permute-start(bf16[8,256,128]{2,1,0:T(8,128)(2,1)S(1)} %get-tuple-element.25), channel_id=1, source_target_pairs={{1,2},{3,4},{5,6},{7,8},{9,10},{11,12},{13,14},{15,16},{17,18},{19... | collective-permute-start | bytes 1572872 | tf_op jit(solution)/shard_map/ppermute | solution.py:418
  30.9 1.9 %collective-permute-start.6 = (bf16[8,256,128]{2,1,0:T(8,128)(2,1)S(1)}, bf16[8,256,128]{2,1,0:T(8,128)(2,1)S(1)}, u32[]{:S(2)}, u32[]{:S(2)}) collective-permute-start(bf16[8,256,128]{2,1,0:T(8,128)(2,1)S(1)} %get-tuple-element.26), channel_id=1, source_target_pairs={{0,1},{2,3},{4,5},{6,7},{8,9},{10,11},{12,13},{14,15},{16,17},{18,... | collective-permute-start | bytes 1572872 | tf_op jit(solution)/shard_map/ppermute | solution.py:418
  32.8 0.0 collective-permute-done.2.far
  32.8 0.0 collective-permute-done.3.near
  32.9 0.2 split_parity.2
  33.1 3.5 %collective-permute-start.4 = (bf16[4,256,128]{2,1,0:T(8,128)(2,1)S(1)}, bf16[4,256,128]{2,1,0:T(8,128)(2,1)S(1)}, u32[]{:S(2)}, u32[]{:S(2)}) collective-permute-start(bf16[4,256,128]{2,1,0:T(8,128)(2,1)S(1)} %get-tuple-element.24), channel_id=1, source_target_pairs={{0,32},{32,0},{64,96},{96,64},{128,160},{160,128},{192,224},{224,1... | collective-permute-start | bytes 786440 | tf_op jit(solution)/shard_map/ppermute | solution.py:435
  36.6 1.3 collective-permute-done.5.far
  37.9 0.0 collective-permute-done.6.near
  37.9 0.2 split_parity.3
  38.1 0.0 copy-start.1
  38.1 3.7 %collective-permute-start.7 = (bf16[4,256,128]{2,1,0:T(8,128)(2,1)S(1)}, bf16[4,256,128]{2,1,0:T(8,128)(2,1)S(1)}, u32[]{:S(2)}, u32[]{:S(2)}) collective-permute-start(bf16[4,256,128]{2,1,0:T(8,128)(2,1)S(1)} %get-tuple-element.28), channel_id=1, source_target_pairs={{0,32},{32,0},{64,96},{96,64},{128,160},{160,128},{192,224},{224,1... | collective-permute-start | bytes 786440 | tf_op jit(solution)/shard_map/ppermute | solution.py:435
  41.8 0.9 collective-permute-done.4.got
  42.7 6.0 %collective-permute-done.7.got_last = bf16[4,256,128]{2,1,0:T(8,128)(2,1)S(1)} collective-permute-done((bf16[4,256,128]{2,1,0:T(8,128)(2,1)S(1)}, bf16[4,256,128]{2,1,0:T(8,128)(2,1)S(1)}, u32[]{:S(2)}, u32[]{:S(2)}) %collective-permute-start.7) | collective-permute-done | bytes 262176 | tf_op jit(solution)/shard_map/ppermute | solution.py:435
  48.7 0.1 add_pair.1
  48.8 39.6 %all_to_all.20.pieces = bf16[8,256,128]{2,1,0:T(8,128)(2,1)S(1)} all-to-all(bf16[8,256,128]{2,1,0:T(8,128)(2,1)S(1)} %add_pair.1), channel_id=1, replica_groups=mesh['za'=4,'zb'=2,'zc'=2,'brick'=32] {'za','zb'}, dimensions={0} | all-to-all | bytes 1048576 | tf_op jit(solution)/shard_map/all_to_all | solution.py:444
  88.5 0.0 copy-done.1
  88.5 0.3 make_image.1
  88.8 0.4 make_gram.1
  89.2 24.6 %all_to_all.21.pieces = f32[32,8,256]{2,1,0:T(8,128)S(1)} all-to-all(f32[32,8,256]{2,1,0:T(8,128)S(1)} %bitcast.13), channel_id=1, replica_groups=mesh['za'=4,'zb'=2,'zc'=2,'brick'=32] {'brick'}, dimensions={0} | all-to-all | bytes 524288 | tf_op jit(solution)/shard_map/all_to_all | solution.py:449
  113.8 0.7 spread_sum.2
  114.5 5.5 %all-to-all-start.2 = ((f32[16,8,256]{2,1,0:T(8,128)}), f32[16,8,256]{2,1,0:T(8,128)S(1)}, u32[]{:S(2)}, u32[]{:S(2)}) async-start(f32[16,8,256]{2,1,0:T(8,128)} %spread_sum.2), calls=%async_computation.2 | async-start | bytes 262144 | tf_op jit(solution)/shard_map/all_to_all | solution.py:450
  120.0 24.8 %all-gather = s16[576,256]{1,0:T(8,128)(2,1)S(1)} all-gather(s16[144,256]{1,0:T(8,128)(2,1)S(1)} %get-tuple-element.29), channel_id=2, replica_groups=mesh['za'=4,'zb'=2,'zc'=2,'brick'=32] {'za'}, dimensions={0}, use_global_device_ids=true | all-gather | bytes 368640 | tf_op jit(solution)/shard_map/all_gather | solution.py:446
  144.8 4.4 %collective-permute-start.9 = (s16[4,144,256]{2,1,0:T(8,128)(2,1)S(1)}, s16[4,144,256]{2,1,0:T(8,128)(2,1)S(1)}, u32[]{:S(2)}, u32[]{:S(2)}) collective-permute-start(s16[4,144,256]{2,1,0:T(8,128)(2,1)S(1)} %bitcast.9), channel_id=1, source_target_pairs={{0,64},{32,96},{64,0},{96,32},{128,192},{160,224},{192,128},{224,1... | collective-permute-start | bytes 884744 | tf_op jit(solution)/shard_map/ppermute | solution.py:435
  149.2 2.1 %collective-permute-start.8 = (s16[4,144,256]{2,1,0:T(8,128)(2,1)S(1)}, s16[4,144,256]{2,1,0:T(8,128)(2,1)S(1)}, u32[]{:S(2)}, u32[]{:S(2)}) collective-permute-start(s16[4,144,256]{2,1,0:T(8,128)(2,1)S(1)} %bitcast.10), channel_id=1, source_target_pairs={{0,32},{32,0},{64,96},{96,64},{128,160},{160,128},{192,224},{224,1... | collective-permute-start | bytes 884744 | tf_op jit(solution)/shard_map/ppermute | solution.py:435
  151.3 11.3 %collective-permute-done.9.refs_2_ = s16[4,144,256]{2,1,0:T(8,128)(2,1)S(1)} collective-permute-done((s16[4,144,256]{2,1,0:T(8,128)(2,1)S(1)}, s16[4,144,256]{2,1,0:T(8,128)(2,1)S(1)}, u32[]{:S(2)}, u32[]{:S(2)}) %collective-permute-start.9) | collective-permute-done | bytes 294944 | tf_op jit(solution)/shard_map/ppermute | solution.py:435
  162.6 1.9 %collective-permute-start.10 = (s16[4,144,256]{2,1,0:T(8,128)(2,1)S(1)}, s16[4,144,256]{2,1,0:T(8,128)(2,1)S(1)}, u32[]{:S(2)}, u32[]{:S(2)}) collective-permute-start(s16[4,144,256]{2,1,0:T(8,128)(2,1)S(1)} %collective-permute-done.9.refs_2_), channel_id=1, source_target_pairs={{0,32},{32,0},{64,96},{96,64},{128,160},{160,128},{192,224},{224,1... | collective-permute-start | bytes 884744 | tf_op jit(solution)/shard_map/ppermute | solution.py:435
  164.5 0.0 all-to-all-done.2.pieces
  164.5 13.9 %all_to_all.22 = f32[32,8,256]{2,1,0:T(8,128)S(1)} all-to-all(f32[32,8,256]{2,1,0:T(8,128)S(1)} %spread_sum.3), channel_id=1, replica_groups=mesh['za'=4,'zb'=2,'zc'=2,'brick'=32] {'brick'}, dimensions={0} | all-to-all | bytes 524288 | tf_op jit(solution)/shard_map/all_to_all | solution.py:453
  178.5 9.0 %cholesky_and_inverse.1 = (f32[256,256]{1,0:T(8,128)}, bf16[256,256]{1,0:T(8,128)(2,1)S(1)}, bf16[256,256]{1,0:T(8,128)(2,1)S(1)}) custom-call(f32[256,256]{1,0:T(8,128)S(1)} %bitcast.12), custom_call_target="tpu_custom_call" | custom-call | tf_op jit(solution)/shard_map/cholesky_and_inverse/pallas_call | solution.py:361
  187.5 0.0 collective-permute-done.8.refs_1_
  187.5 0.0 collective-permute-done.10.refs_3_
  187.5 2.3 %make_basis.1 = f32[2048,256]{1,0:T(8,128)} custom-call(s16[4,144,256]{2,1,0:T(8,128)(2,1)S(1)} %bitcast.11, s16[4,144,256]{2,1,0:T(8,128)(2,1)S(1)} %collective-permute-done.8.refs_1_, s16[4,144,256]{2,1,0:T(8,128)(2,1)S(1)} %collective-permute-done.9.refs_2_, s16[4,144,256]{2,1,0:T(8,128)(2,1)S(1)} %collective-permute-done.10.refs_3_, ...), custom_call_target="tpu_custom_call" | custom-call | tf_op jit(solution)/shard_map/make_basis/pallas_call | solution.py:402
  (1 shorter events, 0.0 us)
Async XLA Ops:
  0.6 17.2 %collective-permute-start = (bf16[2048,256]{1,0:T(8,128)(2,1)}, bf16[2048,256]{1,0:T(8,128)(2,1)S(1)}, u32[]{:S(2)}, u32[]{:S(2)}) collective-permute-start(bf16[2048,256]{1,0:T(8,128)(2,1)} %probes.1), channel_id=1, source_target_pairs={{1,2},{3,4},{5,6},{7,8},{9,10},{11,12},{13,14},{15,16},{17,18},{19... | collective-permute-start | bytes 3145736 | tf_op jit(solution)/shard_map/ppermute | solution.py:418
  5.1 12.7 %collective-permute-start.1 = (bf16[2048,256]{1,0:T(8,128)(2,1)}, bf16[2048,256]{1,0:T(8,128)(2,1)S(1)}, u32[]{:S(2)}, u32[]{:S(2)}) collective-permute-start(bf16[2048,256]{1,0:T(8,128)(2,1)} %probes.1), channel_id=1, source_target_pairs={{0,1},{2,3},{4,5},{6,7},{8,9},{10,11},{12,13},{14,15},{16,17},{18,... | collective-permute-start | bytes 3145736 | tf_op jit(solution)/shard_map/ppermute | solution.py:418
  11.0 1.2 copy-start
  12.2 1.9 copy-start.2
  21.8 11.0 %collective-permute-start.2 = (bf16[8,256,128]{2,1,0:T(8,128)(2,1)S(1)}, bf16[8,256,128]{2,1,0:T(8,128)(2,1)S(1)}, u32[]{:S(2)}, u32[]{:S(2)}) collective-permute-start(bf16[8,256,128]{2,1,0:T(8,128)(2,1)S(1)} %get-tuple-element.21), channel_id=1, source_target_pairs={{1,2},{3,4},{5,6},{7,8},{9,10},{11,12},{13,14},{15,16},{17,18},{19... | collective-permute-start | bytes 1572872 | tf_op jit(solution)/shard_map/ppermute | solution.py:418
  25.5 7.4 %collective-permute-start.3 = (bf16[8,256,128]{2,1,0:T(8,128)(2,1)S(1)}, bf16[8,256,128]{2,1,0:T(8,128)(2,1)S(1)}, u32[]{:S(2)}, u32[]{:S(2)}) collective-permute-start(bf16[8,256,128]{2,1,0:T(8,128)(2,1)S(1)} %get-tuple-element.22), channel_id=1, source_target_pairs={{0,1},{2,3},{4,5},{6,7},{8,9},{10,11},{12,13},{14,15},{16,17},{18,... | collective-permute-start | bytes 1572872 | tf_op jit(solution)/shard_map/ppermute | solution.py:418
  27.4 10.5 %collective-permute-start.5 = (bf16[8,256,128]{2,1,0:T(8,128)(2,1)S(1)}, bf16[8,256,128]{2,1,0:T(8,128)(2,1)S(1)}, u32[]{:S(2)}, u32[]{:S(2)}) collective-permute-start(bf16[8,256,128]{2,1,0:T(8,128)(2,1)S(1)} %get-tuple-element.25), channel_id=1, source_target_pairs={{1,2},{3,4},{5,6},{7,8},{9,10},{11,12},{13,14},{15,16},{17,18},{19... | collective-permute-start | bytes 1572872 | tf_op jit(solution)/shard_map/ppermute | solution.py:418
  30.9 7.0 %collective-permute-start.6 = (bf16[8,256,128]{2,1,0:T(8,128)(2,1)S(1)}, bf16[8,256,128]{2,1,0:T(8,128)(2,1)S(1)}, u32[]{:S(2)}, u32[]{:S(2)}) collective-permute-start(bf16[8,256,128]{2,1,0:T(8,128)(2,1)S(1)} %get-tuple-element.26), channel_id=1, source_target_pairs={{0,1},{2,3},{4,5},{6,7},{8,9},{10,11},{12,13},{14,15},{16,17},{18,... | collective-permute-start | bytes 1572872 | tf_op jit(solution)/shard_map/ppermute | solution.py:418
  33.1 9.7 %collective-permute-start.4 = (bf16[4,256,128]{2,1,0:T(8,128)(2,1)S(1)}, bf16[4,256,128]{2,1,0:T(8,128)(2,1)S(1)}, u32[]{:S(2)}, u32[]{:S(2)}) collective-permute-start(bf16[4,256,128]{2,1,0:T(8,128)(2,1)S(1)} %get-tuple-element.24), channel_id=1, source_target_pairs={{0,32},{32,0},{64,96},{96,64},{128,160},{160,128},{192,224},{224,1... | collective-permute-start | bytes 786440 | tf_op jit(solution)/shard_map/ppermute | solution.py:435
  38.1 50.3 %copy-start.1 = (bf16[2048,256]{1,0:T(8,128)(2,1)S(1)}, bf16[2048,256]{1,0:T(8,128)(2,1)}, u32[]{:S(2)}) copy-start(bf16[2048,256]{1,0:T(8,128)(2,1)} %probes.1) | copy-start | bytes 3145732
  38.1 10.6 %collective-permute-start.7 = (bf16[4,256,128]{2,1,0:T(8,128)(2,1)S(1)}, bf16[4,256,128]{2,1,0:T(8,128)(2,1)S(1)}, u32[]{:S(2)}, u32[]{:S(2)}) collective-permute-start(bf16[4,256,128]{2,1,0:T(8,128)(2,1)S(1)} %get-tuple-element.28), channel_id=1, source_target_pairs={{0,32},{32,0},{64,96},{96,64},{128,160},{160,128},{192,224},{224,1... | collective-permute-start | bytes 786440 | tf_op jit(solution)/shard_map/ppermute | solution.py:435
  114.5 50.0 %all-to-all-start.2 = ((f32[16,8,256]{2,1,0:T(8,128)}), f32[16,8,256]{2,1,0:T(8,128)S(1)}, u32[]{:S(2)}, u32[]{:S(2)}) async-start(f32[16,8,256]{2,1,0:T(8,128)} %spread_sum.2), calls=%async_computation.2 | async-start | bytes 262144 | tf_op jit(solution)/shard_map/all_to_all | solution.py:450
  144.8 17.7 %collective-permute-start.9 = (s16[4,144,256]{2,1,0:T(8,128)(2,1)S(1)}, s16[4,144,256]{2,1,0:T(8,128)(2,1)S(1)}, u32[]{:S(2)}, u32[]{:S(2)}) collective-permute-start(s16[4,144,256]{2,1,0:T(8,128)(2,1)S(1)} %bitcast.9), channel_id=1, source_target_pairs={{0,64},{32,96},{64,0},{96,32},{128,192},{160,224},{192,128},{224,1... | collective-permute-start | bytes 884744 | tf_op jit(solution)/shard_map/ppermute | solution.py:435
  149.2 38.2 %collective-permute-start.8 = (s16[4,144,256]{2,1,0:T(8,128)(2,1)S(1)}, s16[4,144,256]{2,1,0:T(8,128)(2,1)S(1)}, u32[]{:S(2)}, u32[]{:S(2)}) collective-permute-start(s16[4,144,256]{2,1,0:T(8,128)(2,1)S(1)} %bitcast.10), channel_id=1, source_target_pairs={{0,32},{32,0},{64,96},{96,64},{128,160},{160,128},{192,224},{224,1... | collective-permute-start | bytes 884744 | tf_op jit(solution)/shard_map/ppermute | solution.py:435
  162.6 24.9 %collective-permute-start.10 = (s16[4,144,256]{2,1,0:T(8,128)(2,1)S(1)}, s16[4,144,256]{2,1,0:T(8,128)(2,1)S(1)}, u32[]{:S(2)}, u32[]{:S(2)}) collective-permute-start(s16[4,144,256]{2,1,0:T(8,128)(2,1)S(1)} %collective-permute-done.9.refs_2_), channel_id=1, source_target_pairs={{0,32},{32,0},{64,96},{96,64},{128,160},{160,128},{192,224},{224,1... | collective-permute-start | bytes 884744 | tf_op jit(solution)/shard_map/ppermute | solution.py:435
